TPU v7x, 256 devices: a whole 4x4x8 slice. The times are simulated.
256 devices in a mesh: rows: 32 (over y, z), feat: 8 (over x, core).
Axes of the slice: x: 4, y: 4, z: 8, core: 2. Of those that a mesh axis runs over, the one named last changes fastest.
Arguments:
- test_cells: bfloat16 [4096, 3072], P('rows', 'feat'), may hold values from -6 to 6
- train_cells: bfloat16 [16384, 3072], P('rows', 'feat'), may hold values from -6 to 6
- train_present: int32 [16, 16384], P('feat', 'rows'), may hold values from 0 to 1, as said below
- retrieved: int32 [32, 16], P('rows'), may hold values from 0 to 255, as said below
- w_query: bfloat16 [192, 192], replicated, may hold values from -0.4375 to 0.4375
- q_gain: float32 [192], replicated, may hold values from 0.75 to 1.25
- w_key: bfloat16 [192, 192], replicated, may hold values from -0.4375 to 0.4375
- k_gain: float32 [192], replicated, may hold values from 0.75 to 1.25
- w_value: bfloat16 [192, 192], replicated, may hold values from -0.4375 to 0.4375
- w_out: bfloat16 [192, 192], replicated, may hold values from -0.4375 to 0.4375
- gain_one: float32 [192], replicated, may hold values from 0.5 to 1.5
- w_up: bfloat16 [192, 768], replicated, may hold values from -0.4375 to 0.4375
- w_down: bfloat16 [768, 192], replicated, may hold values from -0.21875 to 0.21875
- gain_two: float32 [192], replicated, may hold values from 0.5 to 1.5
- cotangent: bfloat16 [4096, 3072], P('rows', 'feat'), may hold values from -6 to 6
Outputs:
- out_cells: bfloat16 [4096, 3072], P('rows', 'feat')
- grad_test: bfloat16 [4096, 3072], P('rows', 'feat')
- grad_train: bfloat16 [16384, 3072], P('rows', 'feat')
- grad_query: float32 [192, 192], replicated
- grad_key: float32 [192, 192], replicated
- grad_value: float32 [192, 192], replicated
- grad_out: float32 [192, 192], replicated
- grad_up: float32 [192, 768], replicated
- grad_down: float32 [768, 192], replicated
Inputs may be any that keep to these rules, and one draw needn't show every extreme that they name: `retrieved`: row b lists 16 distinct train blocks (block g is train rows g * 64 to g * 64 + 63). Call blocks o * 8 to o * 8 + 7 the blocks of row group o: row b takes from every row group either no block or exactly 1, and it always takes 1 block of row group b, among them block b * 8 + 7. `train_present`: 1 marks a present cell, 0 a missing one. For every feature, every train block holds at least one present cell.
All inputs are finite; a program needn't handle non-finite values.
Results may differ from a plain program's by a relative error of at most 0.019.
Values may be sent and summed in bfloat16 or wider, within the bound.
No kernel may reach another device: no remote copies, remote signals or barrier semaphores. Data moves between devices by JAX's collectives and lax.ppermute only.
A program may use at most 128 MiB of HBM per device.

v0:
```python
import math

import jax
import jax.numpy as jnp
from jax import lax
from jax.sharding import PartitionSpec as P

H = 6
BLK = 64


SCORE_TEMPER = 1.5


def rms_scale(pre, gain):
    return pre * lax.rsqrt(jnp.mean(pre * pre, axis=-1, keepdims=True) + 1e-06) * gain


def layer_scale(pre, gain):
    centred = pre - jnp.mean(pre, axis=-1, keepdims=True)
    return centred * lax.rsqrt(jnp.mean(centred * centred, axis=-1, keepdims=True) + 1e-05) * gain


def project_back(cells, weight, gain, pre, d_normed):
    _, back = jax.vjp(lambda inner: rms_scale(inner, gain), pre)
    (d_pre,) = back(d_normed)
    d_pre = d_pre.astype(jnp.bfloat16)
    grad_weight = jnp.dot(cells.T, d_pre, preferred_element_type=jnp.float32)
    d_cells = jnp.dot(d_pre, weight.T, preferred_element_type=jnp.float32)
    return (grad_weight, d_cells)


def head_side(query_cells, attended, w_out, gain_one, w_up, w_down, gain_two, cotangent):
    inner_one = query_cells.astype(jnp.float32) + jnp.dot(
        attended, w_out, preferred_element_type=jnp.float32
    )
    normed_one, back_one = jax.vjp(lambda inner: layer_scale(inner, gain_one), inner_one)
    normed_one = normed_one.astype(jnp.bfloat16)
    hidden_pre = jnp.dot(normed_one, w_up, preferred_element_type=jnp.float32)
    hidden, back_gelu = jax.vjp(jax.nn.gelu, hidden_pre)
    hidden = hidden.astype(jnp.bfloat16)
    inner_two = normed_one.astype(jnp.float32) + jnp.dot(
        hidden, w_down, preferred_element_type=jnp.float32
    )
    result, back_two = jax.vjp(lambda inner: layer_scale(inner, gain_two), inner_two)
    output = result.astype(jnp.bfloat16)
    (d_two,) = back_two(cotangent.astype(jnp.float32))
    d_two_b = d_two.astype(jnp.bfloat16)
    grad_down = jnp.dot(hidden.T, d_two_b, preferred_element_type=jnp.float32)
    (d_pre,) = back_gelu(jnp.dot(d_two_b, w_down.T, preferred_element_type=jnp.float32))
    d_pre_b = d_pre.astype(jnp.bfloat16)
    grad_up = jnp.dot(normed_one.T, d_pre_b, preferred_element_type=jnp.float32)
    d_normed = d_two + jnp.dot(d_pre_b, w_up.T, preferred_element_type=jnp.float32)
    (d_one,) = back_one(d_normed)
    d_one_b = d_one.astype(jnp.bfloat16)
    grad_out = jnp.dot(attended.T, d_one_b, preferred_element_type=jnp.float32)
    d_attended = jnp.dot(d_one_b, w_out.T, preferred_element_type=jnp.float32).astype(jnp.bfloat16)
    return (output, d_one, d_attended, grad_out, grad_up, grad_down)


def feature_probs(query, key, present, heads):
    rows = query.shape[0]
    count = key.shape[0]
    size = query.shape[1] // heads
    q_part = query.reshape(rows, heads, size)
    k_part = key.reshape(count, heads, size)
    scores = jnp.einsum("thd,khd->htk", q_part, k_part, preferred_element_type=jnp.float32) * (
        SCORE_TEMPER / math.sqrt(size)
    )
    weights = jnp.exp(scores) * present.astype(jnp.float32)
    return weights / jnp.sum(weights, axis=-1, keepdims=True)


def feature_forward(query, key, value, present, heads):
    rows = query.shape[0]
    count = key.shape[0]
    size = query.shape[1] // heads
    weights = feature_probs(query, key, present, heads).astype(jnp.bfloat16)
    v_part = value.reshape(count, heads, size)
    mixed = jnp.einsum("htk,khd->thd", weights, v_part, preferred_element_type=jnp.float32)
    return mixed.reshape(rows, heads * size).astype(jnp.bfloat16)


def feature_back(query, key, value, present, d_att, heads):
    rows = query.shape[0]
    count = key.shape[0]
    size = query.shape[1] // heads
    probs = feature_probs(query, key, present, heads)
    weights = probs.astype(jnp.bfloat16)
    q_part = query.reshape(rows, heads, size)
    k_part = key.reshape(count, heads, size)
    v_part = value.reshape(count, heads, size)
    g_part = d_att.reshape(rows, heads, size)
    grad_w = jnp.einsum("thd,khd->htk", g_part, v_part, preferred_element_type=jnp.float32)
    d_scores = probs * (grad_w - jnp.sum(probs * grad_w, axis=-1, keepdims=True))
    d_scores = (d_scores * (SCORE_TEMPER / math.sqrt(size))).astype(jnp.bfloat16)
    d_query = jnp.einsum(
        "htk,khd->thd", d_scores, k_part, preferred_element_type=jnp.float32
    ).reshape(rows, heads * size)
    d_key = (
        jnp.einsum("htk,thd->khd", d_scores, q_part, preferred_element_type=jnp.float32)
        .reshape(count, heads * size)
        .astype(jnp.bfloat16)
    )
    d_value = (
        jnp.einsum("htk,thd->khd", weights, g_part, preferred_element_type=jnp.float32)
        .reshape(count, heads * size)
        .astype(jnp.bfloat16)
    )
    return (d_query, d_key, d_value)


def on_device(
    test_cells,
    train_cells,
    train_present,
    retrieved,
    w_query,
    q_gain,
    w_key,
    k_gain,
    w_value,
    w_out,
    gain_one,
    w_up,
    w_down,
    gain_two,
    cotangent,
):
    owners = lax.axis_size("rows")
    width = w_query.shape[0]
    heads = H
    test_rows = test_cells.shape[0]
    feats = test_cells.shape[1] // width
    blocks_own = train_cells.shape[0] // BLK
    wanted = retrieved[0]
    count = wanted.shape[0]
    slots = max(1, 2 * count // owners)
    owner_of = wanted // blocks_own
    local_ids = wanted % blocks_own
    order = jnp.arange(count, dtype=jnp.int32)
    earlier = (owner_of[:, None] == owner_of[None, :]) & (order[None, :] < order[:, None])
    rank = jnp.sum(earlier.astype(jnp.int32), axis=1)
    position = owner_of * slots + rank
    places = jnp.arange(owners * slots, dtype=jnp.int32)
    hits = position[None, :] == places[:, None]
    requests = jnp.sum(jnp.where(hits, local_ids[None, :] + 1, 0), axis=1) - 1
    asked = lax.all_to_all(
        requests.reshape(owners, slots), "rows", split_axis=0, concat_axis=0, tiled=True
    )
    pick = jnp.clip(asked.reshape(-1), 0, blocks_own - 1)
    key_cells = train_cells.reshape(-1, width)
    key_pre = jnp.dot(key_cells, w_key, preferred_element_type=jnp.float32)
    own_present = jnp.transpose(train_present.reshape(feats, blocks_own, BLK), (1, 0, 2))
    own_keys = (
        rms_scale(key_pre, k_gain).astype(jnp.bfloat16).reshape(blocks_own, BLK, feats * width)
    )
    own_values = (
        jnp.dot(key_cells, w_value, preferred_element_type=jnp.float32)
        .astype(jnp.bfloat16)
        .reshape(blocks_own, BLK, feats * width)
    )
    got_keys, got_values, got_present = (
        lax.all_to_all(
            jnp.take(own_keys, pick, axis=0), "rows", split_axis=0, concat_axis=0, tiled=True
        ),
        lax.all_to_all(
            jnp.take(own_values, pick, axis=0), "rows", split_axis=0, concat_axis=0, tiled=True
        ),
        lax.all_to_all(
            jnp.take(own_present, pick, axis=0), "rows", split_axis=0, concat_axis=0, tiled=True
        ),
    )
    far_keys = jnp.take(got_keys, position, axis=0).reshape(-1, width)
    far_values = jnp.take(got_values, position, axis=0).reshape(-1, width)
    far_present = jnp.transpose(jnp.take(got_present, position, axis=0), (1, 0, 2)).reshape(
        feats, count * BLK
    )
    key_grid = far_keys.reshape(count * BLK, feats, width)
    value_grid = far_values.reshape(count * BLK, feats, width)
    query_cells = test_cells.reshape(-1, width)
    query_pre = jnp.dot(query_cells, w_query, preferred_element_type=jnp.float32)
    query_grid = rms_scale(query_pre, q_gain).astype(jnp.bfloat16).reshape(test_rows, feats, width)
    attended = jnp.stack(
        [
            feature_forward(
                query_grid[:, feature],
                key_grid[:, feature],
                value_grid[:, feature],
                far_present[feature],
                heads,
            )
            for feature in range(feats)
        ],
        axis=1,
    )
    attended = attended.reshape(-1, width)
    output, d_one, d_att, g_out, g_up, g_down = head_side(
        query_cells, attended, w_out, gain_one, w_up, w_down, gain_two, cotangent.reshape(-1, width)
    )
    d_att_grid = d_att.reshape(test_rows, feats, width)
    query_parts = []
    key_parts = []
    value_parts = []
    for feature in range(feats):
        d_query, d_key, d_value = feature_back(
            query_grid[:, feature],
            key_grid[:, feature],
            value_grid[:, feature],
            far_present[feature],
            d_att_grid[:, feature],
            heads,
        )
        query_parts.append(d_query)
        key_parts.append(d_key)
        value_parts.append(d_value)
    d_query_all = jnp.stack(query_parts, axis=1).reshape(-1, width)
    d_key_all = jnp.stack(key_parts, axis=1).reshape(count, BLK, feats * width)
    d_value_all = jnp.stack(value_parts, axis=1).reshape(count, BLK, feats * width)
    empty_slots = jnp.zeros((owners * slots, BLK, feats * width), jnp.bfloat16)
    send_keys = empty_slots.at[position].set(d_key_all)
    send_values = empty_slots.at[position].set(d_value_all)
    back_keys, back_values = (
        lax.all_to_all(send_keys, "rows", split_axis=0, concat_axis=0, tiled=True),
        lax.all_to_all(send_values, "rows", split_axis=0, concat_axis=0, tiled=True),
    )
    g_query, d_qcells = project_back(query_cells, w_query, q_gain, query_pre, d_query_all)
    grad_test = (d_one + d_qcells).astype(jnp.bfloat16).reshape(test_rows, feats * width)
    selector = (
        asked.reshape(-1)[:, None] == jnp.arange(blocks_own, dtype=jnp.int32)[None, :]
    ).astype(jnp.bfloat16)
    key_total = (
        jnp.einsum(
            "sb,sx->bx",
            selector,
            back_keys.reshape(owners * slots, -1),
            preferred_element_type=jnp.float32,
        )
        .astype(jnp.bfloat16)
        .reshape(-1, width)
    )
    value_total = (
        jnp.einsum(
            "sb,sx->bx",
            selector,
            back_values.reshape(owners * slots, -1),
            preferred_element_type=jnp.float32,
        )
        .astype(jnp.bfloat16)
        .reshape(-1, width)
    )
    g_key, d_kcells = project_back(key_cells, w_key, k_gain, key_pre, key_total.astype(jnp.float32))
    g_value = jnp.dot(key_cells.T, value_total, preferred_element_type=jnp.float32)
    d_vcells = jnp.dot(value_total, w_value.T, preferred_element_type=jnp.float32)
    grad_train = (d_kcells + d_vcells).astype(jnp.bfloat16).reshape(blocks_own * BLK, feats * width)
    sum_query, sum_key, sum_value, sum_out, sum_up, sum_down = lax.psum(
        (g_query, g_key, g_value, g_out, g_up, g_down), ("rows", "feat")
    )
    out_cells = output.reshape(test_rows, feats * width)
    return (
        out_cells,
        grad_test,
        grad_train,
        sum_query,
        sum_key,
        sum_value,
        sum_out,
        sum_up,
        sum_down,
    )


def solution(mesh):
    in_specs = (
        P("rows", "feat"),
        P("rows", "feat"),
        P("feat", "rows"),
        P("rows", None),
        P(),
        P(),
        P(),
        P(),
        P(),
        P(),
        P(),
        P(),
        P(),
        P(),
        P("rows", "feat"),
    )
    out_specs = (
        P("rows", "feat"),
        P("rows", "feat"),
        P("rows", "feat"),
        P(),
        P(),
        P(),
        P(),
        P(),
        P(),
    )
    return jax.shard_map(
        on_device, mesh=mesh, in_specs=in_specs, out_specs=out_specs, check_vma=False
    )
```

profile of v0, /device:TPU:32, one launch (start us, length us, event | category | flops | bytes accessed | tf_op | source)
XLA Modules:
  0.0 581.1 jit_solution(16820213837229973137)
XLA Ops:
  9.6 11.4 %all-to-all-start = ((s32[32,1,1]{2,1,0:T(1,128)}), s32[32,1,1]{2,1,0:T(1,128)S(1)}, u32[]{:S(2)}, u32[]{:S(2)}) async-start(s32[32,1,1]{2,1,0:T(1,128)} %copy.155), calls=%async_computation | async-start | bytes 32768 | tf_op jit(solution)/shard_map/all_to_all | solution.py:148
  27.4 2.1 all-to-all-done
  32.7 7.7 %all-to-all-start.3 = ((s32[32,1,128]{2,1,0:T(1,128)}), s32[32,1,128]{2,1,0:T(1,128)S(1)}, u32[]{:S(2)}, u32[]{:S(2)}) async-start(s32[32,1,128]{2,1,0:T(1,128)} %reshape.520), calls=%async_computation.3 | async-start | bytes 32768 | tf_op jit(solution)/shard_map/all_to_all | solution.py:170
  40.4 1.9 gather_fusion.4
  42.3 1.9 gather_fusion.2
  44.2 3.5 broadcast_select_fusion
  48.9 47.6 %all_to_all.31 = bf16[32,64,384]{2,1,0:T(8,128)(2,1)} all-to-all(bf16[32,64,384]{2,1,0:T(8,128)(2,1)S(1)} %get-tuple-element.98), channel_id=1, replica_groups=mesh['rows'=32,'feat'=8] {'rows'}, dimensions={0} | all-to-all | bytes 3145728 | tf_op jit(solution)/shard_map/all_to_all | solution.py:164
  96.5 5.3 all-to-all-start.1
  111.4 1.7 copy.169
  116.7 3.0 gather_fusion.5
  119.7 20.3 %all-to-all-done.1 = bf16[32,64,384]{2,1,0:T(8,128)(2,1)S(1)} async-done(((bf16[32,64,384]{2,1,0:T(8,128)(2,1)}), bf16[32,64,384]{2,1,0:T(8,128)(2,1)S(1)}, u32[]{:S(2)}, u32[]{:S(2)}) %all-to-all-start.1) | async-done | bytes 1572896 | tf_op jit(solution)/shard_map/all_to_all | solution.py:167
  141.5 2.5 broadcast_select_fusion.2
  144.0 3.1 reshape_reshape.7
  148.7 4.3 fusion.90
  153.0 2.3 copy.157
  155.3 2.5 copy.163
  157.8 2.5 fusion.89
  160.3 2.3 copy.161
  162.6 3.0 copy.165
  165.6 1.8 fusion.8
  176.8 2.9 convolution_convert_fusion.2
  180.6 2.0 copy.180
  182.6 2.0 copy.181
  184.6 3.7 pad_maximum_fusion.1
  190.2 2.8 scatter_fusion.1
  193.0 6.1 %all-to-all-start.5 = ((bf16[32,64,384]{2,1,0:T(8,128)(2,1)}), bf16[32,64,384]{2,1,0:T(8,128)(2,1)S(1)}, u32[]{:S(2)}, u32[]{:S(2)}) async-start(bf16[32,64,384]{2,1,0:T(8,128)(2,1)} %scatter_fusion.1), calls=%async_computation.5 | async-start | bytes 3145728 | tf_op jit(solution)/shard_map/all_to_all | solution.py:225
  199.1 3.3 fusion.96
  202.5 9.8 %fusion.33 = bf16[6,32,1024]{2,1,0:T(8,128)(2,1)} fusion(bf16[128,6,32]{0,2,1:T(8,128)(2,1)S(1)} %bitcast.157, f32[6,128,1024]{2,1,0:T(8,128)} %fusion.96, f32[6,128,1024]{2,1,0:T(8,128)} %copy-done.3, f32[6,128]{1,0:T(8,128)S(1)} %get-tuple-element.108, f32[1024]{0:T(1024)S(1)} %convert_element_type.208), kind=kOutput, calls=%fused_computation.38 | convolution fusion | flops 59180800 | bytes 6740992 | tf_op jit(solution)/shard_map/htk,thd->khd/dot_general | solution.py:101
  212.3 3.5 copy.177
  215.8 3.3 fusion.97
  219.1 9.6 %fusion.30 = bf16[6,32,1024]{2,1,0:T(8,128)(2,1)} fusion(bf16[128,6,32]{0,2,1:T(8,128)(2,1)S(1)} %bitcast.155, f32[6,128,1024]{2,1,0:T(8,128)} %fusion.97, f32[6,128,1024]{2,1,0:T(8,128)} %copy-done.2, f32[6,128]{1,0:T(8,128)S(1)} %get-tuple-element.106, f32[1024]{0:T(1024)S(1)} %convert_element_type.214), kind=kOutput, calls=%fused_computation.37 | convolution fusion | flops 59180800 | bytes 6740992 | tf_op jit(solution)/shard_map/htk,thd->khd/dot_general | solution.py:101
  228.7 3.5 copy.178
  232.2 4.5 pad_maximum_fusion
  236.7 3.5 reshape.482
  241.6 3.2 scatter_fusion
  244.8 9.8 %all-to-all-start.4 = ((bf16[32,64,384]{2,1,0:T(8,128)(2,1)}), bf16[32,64,384]{2,1,0:T(8,128)(2,1)}, u32[]{:S(2)}, u32[]{:S(2)}) async-start(bf16[32,64,384]{2,1,0:T(8,128)(2,1)} %scatter_fusion), calls=%async_computation.4 | async-start | bytes 3145728 | tf_op jit(solution)/shard_map/all_to_all | solution.py:224
  254.9 9.0 %fusion.17 = f32[6,32,128]{2,1,0:T(8,128)S(1)} fusion(bf16[1024,6,32]{0,2,1:T(8,128)(2,1)} %bitcast.144, f32[6,128,1024]{2,1,0:T(8,128)} %fusion.96, f32[6,128,1024]{2,1,0:T(8,128)} %copy-done.3, f32[6,128]{1,0:T(8,128)S(1)} %get-tuple-element.108, f32[1024]{0:T(1024)S(1)} %convert_element_type.208), kind=kOutput, calls=%fused_computation.26 | convolution fusion | flops 58984192 | bytes 6790144 | tf_op jit(solution)/shard_map/htk,khd->thd/dot_general | solution.py:97
  264.7 9.5 %fusion.23 = f32[6,32,128]{2,1,0:T(8,128)} fusion(bf16[1024,6,32]{0,2,1:T(8,128)(2,1)} %bitcast.142, f32[6,128,1024]{2,1,0:T(8,128)} %fusion.97, f32[6,128,1024]{2,1,0:T(8,128)} %copy-done.2, f32[6,128]{1,0:T(8,128)S(1)} %get-tuple-element.106, f32[1024]{0:T(1024)S(1)} %convert_element_type.214), kind=kOutput, calls=%fused_computation.28 | convolution fusion | flops 58984192 | bytes 6790144 | tf_op jit(solution)/shard_map/htk,khd->thd/dot_general | solution.py:97
  275.8 1.9 pad_maximum_fusion.2
  277.8 1.8 reshape.420
  279.6 1.7 copy.175
  284.3 1.8 fusion.52
  286.1 2.1 fusion.99
  288.2 2.5 fusion.51
  293.7 2.3 copy.186
  304.8 259.6 %all-reduce.3.cloned.1.call-done = (f32[192,192]{0,1:T(8,128)}, f32[192,192]{0,1:T(8,128)}, f32[192,192]{0,1:T(8,128)}, f32[192,192]{1,0:T(8,128)}, f32[192,768]{1,0:T(8,128)}, /*index=5*/f32[768,192]{0,1:T(8,128)}) async-done(((f32[192,192]{0,1:T(8,128)}, f32[192,192]{0,1:T(8,128)}, f32[192,192]{0,1:T(8,128)}, f32[192,192]{1,0:T(8,128)}, f32[192,768]{1,0:T(8,128)}, /*index=5*/f32[768,192]{0,1:T(8,128)}), ...) | async-done | bytes 1769488 | tf_op jit(solution)/shard_map/psum | solution.py:256
  564.4 1.8 copy.183
  571.3 1.9 copy.199
  (230 shorter events, 65.9 us)
Async XLA Ops:
  7.2 166.0 %copy-start = (bf16[768,192]{0,1:T(8,128)(2,1)S(1)}, bf16[768,192]{0,1:T(8,128)(2,1)}, u32[]{:S(2)}) copy-start(bf16[768,192]{0,1:T(8,128)(2,1)} %param.31) | copy-start | bytes 884740
  7.2 19.0 %copy-start.41 = (f32[192]{0:T(256)S(1)}, f32[192]{0:T(256)}, u32[]{:S(2)}) copy-start(f32[192]{0:T(256)} %param.26) | copy-start | bytes 2308
  8.8 12.2 %copy-start.54 = (s32[16]{0:T(128)}, s32[16]{0:T(128)S(1)}, u32[]{:S(2)}) copy-start(s32[16]{0:T(128)S(1)} %convert_reduce_fusion) | copy-start | bytes 196
  9.6 19.9 %all-to-all-start = ((s32[32,1,1]{2,1,0:T(1,128)}), s32[32,1,1]{2,1,0:T(1,128)S(1)}, u32[]{:S(2)}, u32[]{:S(2)}) async-start(s32[32,1,1]{2,1,0:T(1,128)} %copy.155), calls=%async_computation | async-start | bytes 32768 | tf_op jit(solution)/shard_map/all_to_all | solution.py:148
  32.7 16.2 %all-to-all-start.3 = ((s32[32,1,128]{2,1,0:T(1,128)}), s32[32,1,128]{2,1,0:T(1,128)S(1)}, u32[]{:S(2)}, u32[]{:S(2)}) async-start(s32[32,1,128]{2,1,0:T(1,128)} %reshape.520), calls=%async_computation.3 | async-start | bytes 32768 | tf_op jit(solution)/shard_map/all_to_all | solution.py:170
  48.9 52.8 %copy-start.35 = (bf16[128,384]{1,0:T(8,128)(2,1)S(1)}, bf16[128,384]{1,0:T(8,128)(2,1)}, u32[]{:S(2)}) copy-start(bf16[128,384]{1,0:T(8,128)(2,1)} %param.19) | copy-start | bytes 294916
  48.9 53.1 %copy-start.28 = (bf16[192,192]{1,0:T(8,128)(2,1)S(1)}, bf16[192,192]{1,0:T(8,128)(2,1)}, u32[]{:S(2)}) copy-start(bf16[192,192]{1,0:T(8,128)(2,1)} %param.23) | copy-start | bytes 221188
  96.5 43.4 %all-to-all-start.1 = ((bf16[32,64,384]{2,1,0:T(8,128)(2,1)}), bf16[32,64,384]{2,1,0:T(8,128)(2,1)S(1)}, u32[]{:S(2)}, u32[]{:S(2)}) async-start(bf16[32,64,384]{2,1,0:T(8,128)(2,1)} %get-tuple-element.99), calls=%async_computation.1 | async-start | bytes 3145728 | tf_op jit(solution)/shard_map/all_to_all | solution.py:167
  101.9 38.0 %copy-start.9 = (bf16[256,192]{1,0:T(8,128)(2,1)}, bf16[256,192]{1,0:T(8,128)(2,1)S(1)}, u32[]{:S(2)}) copy-start(bf16[256,192]{1,0:T(8,128)(2,1)S(1)} %reshape.410) | copy-start | bytes 294916
  113.8 26.2 %copy-start.51 = (pred[16]{0:T(512)(128)(4,1)}, pred[16]{0:T(512)(128)(4,1)S(1)}, u32[]{:S(2)}) copy-start(pred[16]{0:T(512)(128)(4,1)S(1)} %get-tuple-element.81) | copy-start | bytes 52
  155.3 14.8 %copy-start.15 = (bf16[1024,1,192]{0,2,1:T(8,128)(2,1)}, bf16[1024,1,192]{0,2,1:T(8,128)(2,1)S(1)}, u32[]{:S(2)}) copy-start(bf16[1024,1,192]{0,2,1:T(8,128)(2,1)S(1)} %copy.157) | copy-start | bytes 1179652
  157.8 9.6 %copy-start.14 = (bf16[1024,1,192]{0,2,1:T(8,128)(2,1)}, bf16[1024,1,192]{0,2,1:T(8,128)(2,1)S(1)}, u32[]{:S(2)}) copy-start(bf16[1024,1,192]{0,2,1:T(8,128)(2,1)S(1)} %copy.163) | copy-start | bytes 1179652
  162.6 6.6 %copy-start.13 = (bf16[1024,1,192]{0,2,1:T(8,128)(2,1)}, bf16[1024,1,192]{0,2,1:T(8,128)(2,1)S(1)}, u32[]{:S(2)}) copy-start(bf16[1024,1,192]{0,2,1:T(8,128)(2,1)S(1)} %copy.161) | copy-start | bytes 1179652
  165.6 2.6 copy-start.12
  167.4 1.8 copy-start.33
  170.1 2.3 copy-start.26
  170.1 2.6 copy-start.53
  170.1 2.7 copy-start.17
  171.7 1.9 copy-start.11
  171.8 1.9 copy-start.52
  172.4 2.9 copy-start.18
  172.8 1.7 copy-start.19
  173.1 2.1 copy-start.23
  176.0 3.7 copy-start.7
  176.8 2.9 copy-start.4
  184.6 5.7 copy-start.50
  193.0 9.4 %copy-start.34 = (bf16[128,1,192]{0,2,1:T(8,128)(2,1)S(1)}, bf16[128,1,192]{0,2,1:T(8,128)(2,1)}, u32[]{:S(2)}) copy-start(bf16[128,1,192]{0,2,1:T(8,128)(2,1)} %copy.159) | copy-start | bytes 147460
  193.0 51.8 %all-to-all-start.5 = ((bf16[32,64,384]{2,1,0:T(8,128)(2,1)}), bf16[32,64,384]{2,1,0:T(8,128)(2,1)S(1)}, u32[]{:S(2)}, u32[]{:S(2)}) async-start(bf16[32,64,384]{2,1,0:T(8,128)(2,1)} %scatter_fusion.1), calls=%async_computation.5 | async-start | bytes 3145728 | tf_op jit(solution)/shard_map/all_to_all | solution.py:225
  212.3 6.8 %copy-start.32 = (bf16[128,1,192]{0,2,1:T(8,128)(2,1)S(1)}, bf16[128,1,192]{0,2,1:T(8,128)(2,1)}, u32[]{:S(2)}) copy-start(bf16[128,1,192]{0,2,1:T(8,128)(2,1)} %copy.164) | copy-start | bytes 147460
  244.8 48.9 %all-to-all-start.4 = ((bf16[32,64,384]{2,1,0:T(8,128)(2,1)}), bf16[32,64,384]{2,1,0:T(8,128)(2,1)}, u32[]{:S(2)}, u32[]{:S(2)}) async-start(bf16[32,64,384]{2,1,0:T(8,128)(2,1)} %scatter_fusion), calls=%async_computation.4 | async-start | bytes 3145728 | tf_op jit(solution)/shard_map/all_to_all | solution.py:224
  254.6 309.8 %all-reduce.3.cloned.1.call-start = ((), (), s32[]{:S(2)}) async-start(), calls=%async_computation.6 | async-start | bytes 3932160 | tf_op jit(solution)/shard_map/psum | solution.py:256
  264.7 16.7 %copy-start.6 = (f32[256,192]{0,1:T(8,128)S(1)}, f32[256,192]{0,1:T(8,128)}, u32[]{:S(2)}) copy-start(f32[256,192]{0,1:T(8,128)} %copy-done.5) | copy-start | bytes 589828
  264.7 16.7 %copy-start.40 = (f32[192]{0:T(256)S(1)}, f32[192]{0:T(256)}, u32[]{:S(2)}) copy-start(f32[192]{0:T(256)} %param.24) | copy-start | bytes 2308
  264.7 17.7 %copy-start.46 = (f32[256]{0:T(256)S(1)}, f32[256]{0:T(256)}, u32[]{:S(2)}) copy-start(f32[256]{0:T(256)} %copy-done.45) | copy-start | bytes 3076
  264.7 17.8 %copy-start.44 = (f32[256]{0:T(256)S(1)}, f32[256]{0:T(256)}, u32[]{:S(2)}) copy-start(f32[256]{0:T(256)} %copy-done.43) | copy-start | bytes 3076
  264.7 18.8 %copy-start.10 = (bf16[256,192]{1,0:T(8,128)(2,1)S(1)}, bf16[256,192]{1,0:T(8,128)(2,1)}, u32[]{:S(2)}) copy-start(bf16[256,192]{1,0:T(8,128)(2,1)} %copy-done.9) | copy-start | bytes 294916
  274.1 10.2 %copy-start.8 = (f32[256,192]{0,1:T(8,128)S(1)}, f32[256,192]{0,1:T(8,128)}, u32[]{:S(2)}) copy-start(f32[256,192]{0,1:T(8,128)} %copy-done.7) | copy-start | bytes 589828
  274.1 12.0 %copy-start.20 = (bf16[256,192]{0,1:T(8,128)(2,1)S(1)}, bf16[256,192]{0,1:T(8,128)(2,1)}, u32[]{:S(2)}) copy-start(bf16[256,192]{0,1:T(8,128)(2,1)} %copy-done.19) | copy-start | bytes 294916
  286.1 5.5 copy-start.48
  296.0 3.5 copy-start.42
  296.5 3.2 copy-start.39
  296.5 3.2 copy-start.37
  299.7 2.1 copy-start.22
  299.7 2.1 copy-start.29
  300.0 3.0 copy-start.31
  300.0 3.3 copy-start.30
  303.3 270.7 %copy-start.1 = (bf16[768,192]{0,1:T(8,128)(2,1)S(1)}, bf16[768,192]{0,1:T(8,128)(2,1)}, u32[]{:S(2)}) copy-start(bf16[768,192]{0,1:T(8,128)(2,1)} %param.31) | copy-start | bytes 884740
  564.4 8.8 %copy-start.25 = (f32[768,192]{0,1:T(8,128)S(1)}, f32[768,192]{0,1:T(8,128)}, u32[]{:S(2)}) copy-start(f32[768,192]{0,1:T(8,128)} %get-tuple-element.124) | copy-start | bytes 1769476
  (13 other events, 13.4 us)
Sparse Core Ops, SparseCore 0:
  301.1 263.2 all-reduce.2
where the time goes:
time: 590 us; the launch traced here: 581 us
  waiting for transfers between devices  283 us (48%)
  local copies, waits for them, and re-layouts  100 us (17%)
  matrix products  68 us (12%)
  blocking collectives  47.6 us (8%)
  starting transfers between devices  40.5 us (7%)
  other arithmetic  26.1 us (4%)
  between operations  15.3 us (3%)
    psum x1, waiting for transfers between devices, on_device(): lax.psum((g_query, g_key, g_value, g_out, g_up, g_down), ('rows', 'feat'))  260 us
    all_to_all x1, blocking collectives, on_device(): lax.all_to_all(jnp.take(own_keys, pick, axis=0), 'rows', split_axis=0, co...  47.6 us
    all_to_all x1, waiting for transfers between devices, on_device(): lax.all_to_all(jnp.take(own_values, pick, axis=0), 'rows', split_axis=0,...  20.3 us
    dot_general x2, matrix products, feature_back(): jnp.einsum('htk,thd->khd', d_scores, q_part, preferred_element_type=jnp.f...  19.4 us
    dot_general x2, matrix products, feature_back(): jnp.einsum('htk,khd->thd', d_scores, k_part, preferred_element_type=jnp.f...  18.4 us
    unnamed x120, local copies, waits for them, and re-layouts  17.6 us
  transfers between devices with their start and end apart: 6, of which 4 were waited for; matrix products, arithmetic and copies ran while one was open for 20% of the time, Pallas kernels for 0%

commit v1 on v0

v1 whole, which is shorter than its diff:
```python
import functools
import math

import jax
import jax.numpy as jnp
from jax import lax
from jax.experimental import pallas as pl
from jax.experimental.pallas import tpu as pltpu
from jax.sharding import PartitionSpec as P

H = 6
BLK = 64
E = 192
W = 256
FFH = 768
SIZE = E // H
TEMPER = 1.5 / math.sqrt(SIZE)
LOG2E = math.log2(math.e)
GELU_C = math.sqrt(2.0 / math.pi)
ABSENT = 8.0
ABSENT_ABOVE = 7.0
MASKED = -30000.0
GRAD_ROWS = 4096

bf16 = jnp.bfloat16
f32 = jnp.float32


def dot_nn(a, b):
    return lax.dot_general(a, b, (((1,), (0,)), ((), ())), preferred_element_type=f32)


def dot_nt(a, b):
    return lax.dot_general(a, b, (((1,), (1,)), ((), ())), preferred_element_type=f32)


def dot_tn(a, b):
    return lax.dot_general(a, b, (((0,), (0,)), ((), ())), preferred_element_type=f32)


def pick_kernel(pick_ref, cells_ref, out_ref):
    def body(slot, carry):
        out_ref[slot] = cells_ref[pick_ref[slot]]
        return carry

    lax.fori_loop(0, out_ref.shape[0], body, 0)


def sum_kernel(asked_ref, back_ref, out_ref, acc_ref):
    acc_ref[...] = jnp.zeros_like(acc_ref)

    def body(slot, carry):
        asked = asked_ref[slot]

        @pl.when(asked >= 0)
        def _():
            acc_ref[asked] += back_ref[slot].astype(f32)

        return carry

    lax.fori_loop(0, back_ref.shape[0], body, 0)
    out_ref[...] = acc_ref[...].astype(bf16)


def mean_e(x):
    return jnp.sum(x, axis=-1, keepdims=True) * (1.0 / E)


def head_blocks(full):
    return jnp.concatenate(
        [full[SIZE * h : SIZE * (h + 1), 128 * h : 128 * (h + 1)] for h in range(H)]
        + [jnp.zeros((W - E, 128), f32)],
        axis=0,
    )


def spread_columns(tall, last):
    row = lax.broadcasted_iota(jnp.int32, tall.shape, 0)
    parts = []
    for h in range(H):
        inside = (row >= SIZE * h) & (row < SIZE * (h + 1))
        part = jnp.where(inside, tall, 0.0)
        if last:
            part = jnp.where(row == E, 1.0, part)
        parts.append(part)
    return jnp.concatenate(parts, axis=1).astype(bf16)


def spread_rows(wide):
    lane = lax.broadcasted_iota(jnp.int32, wide.shape, 1)
    parts = []
    for h in range(H):
        inside = (lane >= SIZE * h) & (lane < SIZE * (h + 1))
        parts.append(jnp.where(inside, wide, 0.0))
    return jnp.concatenate(parts, axis=0).astype(bf16)


def layer_norm(x, lane_in):
    centred = jnp.where(lane_in, x - mean_e(x), 0.0)
    scale = lax.rsqrt(mean_e(centred * centred) + 1e-05)
    return centred * scale, scale


def layer_norm_back(hat, scale, gain, dy):
    u = dy * gain
    return scale * (u - mean_e(u) - hat * mean_e(u * hat))


def rms_back(pre, scale, gain, dy):
    u = dy * gain
    return scale * (u - pre * (scale * scale) * mean_e(pre * u))


def main_kernel(
    chunk,
    owner_ref,
    rec_ref,
    test_ref,
    cot_ref,
    wq_ref,
    wk_ref,
    wv_ref,
    place_ref,
    wqt_ref,
    wkt_ref,
    wvt_ref,
    placet_ref,
    w_out_ref,
    w_up_ref,
    w_down_ref,
    gains_ref,
    out_ref,
    grad_test_ref,
    send_ref,
    grads_ref,
    cells_s,
    kp_s,
    k_s,
    v_s,
    e_s,
    p_s,
    d_s,
):
    count = owner_ref.shape[0]
    feats = 2
    rows = test_ref.shape[0]
    keys = count * BLK
    chunks = keys // chunk
    q_gain = gains_ref[0:1, :]
    k_gain = gains_ref[1:2, :]
    gain_one = gains_ref[2:3, :]
    gain_two = gains_ref[3:4, :]

    def gather(j, carry):
        cells_s[pl.ds(pl.multiple_of(j * BLK, BLK), BLK), :] = rec_ref[owner_ref[j]]
        return carry

    lax.fori_loop(0, count, gather, 0)

    test = test_ref[...]
    tc, qp, qr, qn, qt = [], [], [], [], []
    for f in range(feats):
        pre = dot_nn(test, wq_ref[f])
        scale = lax.rsqrt(mean_e(pre * pre) + 1e-06)
        norm = pre * scale * q_gain
        norm = norm.astype(bf16).astype(f32)
        tc.append(dot_nn(test, place_ref[f]))
        qp.append(pre)
        qr.append(scale)
        qn.append(norm)
        qt.append(spread_columns(norm.T, True))

    def scores(c, totals):
        start = pl.ds(pl.multiple_of(c * chunk, chunk), chunk)
        cells = cells_s[start, :]
        result = []
        for f in range(feats):
            pre = dot_nn(cells, wk_ref[f])
            lane = lax.broadcasted_iota(jnp.int32, pre.shape, 1)
            body = jnp.where(lane < E, pre, 0.0)
            scale = lax.rsqrt(mean_e(body * body) + 1e-06)
            norm = body * scale * k_gain
            bias = jnp.where((lane == E) & (pre > ABSENT_ABOVE), MASKED, 0.0)
            norm = (norm + bias).astype(bf16)
            kp_s[f, start, :] = body
            k_s[f, start, :] = norm
            v_s[f, start, :] = dot_nn(cells, wv_ref[f]).astype(bf16)
            e = jnp.exp2(dot_nn(norm, qt[f]) * (TEMPER * LOG2E))
            e_s[f, start, :] = e
            result.append(totals[f] + jnp.sum(e, axis=0, keepdims=True))
        return tuple(result)

    zero = jnp.zeros((1, H * rows), f32)
    totals = lax.fori_loop(0, chunks, scores, (zero,) * feats)
    inverse = [1.0 / total for total in totals]

    def attend(c, mixed):
        start = pl.ds(pl.multiple_of(c * chunk, chunk), chunk)
        result = []
        for f in range(feats):
            p = (e_s[f, start, :] * inverse[f]).astype(bf16)
            p_s[f, start, :] = p
            result.append(mixed[f] + dot_tn(v_s[f, start, :], p))
        return tuple(result)

    mixed = lax.fori_loop(0, chunks, attend, (jnp.zeros((W, H * rows), f32),) * feats)
    attended_t = [head_blocks(m) for m in mixed]

    attended = jnp.concatenate([a.T for a in attended_t], axis=0).astype(bf16)
    lane_in = lax.broadcasted_iota(jnp.int32, (feats * rows, W), 1) < E
    cells_f32 = jnp.concatenate(tc, axis=0)
    w_out = w_out_ref[...]
    w_up = w_up_ref[...]
    w_down = w_down_ref[...]
    inner_one = cells_f32 + dot_nn(attended, w_out)
    hat_one, scale_one = layer_norm(inner_one, lane_in)
    normed_one = (hat_one * gain_one).astype(bf16)
    pre = dot_nn(normed_one, w_up)
    tanh = jnp.tanh(GELU_C * (pre + 0.044715 * (pre * pre * pre)))
    hidden = (0.5 * pre * (1.0 + tanh)).astype(bf16)
    slope = 0.5 * (1.0 + tanh) + (0.5 * GELU_C) * pre * (1.0 - tanh * tanh) * (
        1.0 + (3 * 0.044715) * (pre * pre)
    )
    inner_two = normed_one.astype(f32) + dot_nn(hidden, w_down)
    hat_two, scale_two = layer_norm(inner_two, lane_in)
    out = (hat_two * gain_two).astype(bf16)
    out_ref[...] = (
        dot_nn(out[:rows], placet_ref[0]) + dot_nn(out[rows:], placet_ref[1])
    ).astype(bf16)
    cot_in = cot_ref[...]
    cot = jnp.concatenate([dot_nn(cot_in, place_ref[f]) for f in range(feats)], axis=0)
    d_two = layer_norm_back(hat_two, scale_two, gain_two, cot)
    d_two = jnp.where(lane_in, d_two, 0.0)
    d_two_b = d_two.astype(bf16)
    d_pre_b = (dot_nt(d_two_b, w_down) * slope).astype(bf16)
    d_normed = d_two + dot_nt(d_pre_b, w_up)
    d_one = layer_norm_back(hat_one, scale_one, gain_one, d_normed)
    d_one = jnp.where(lane_in, d_one, 0.0)
    d_one_b = d_one.astype(bf16)
    d_att = dot_nt(d_one_b, w_out).astype(bf16).astype(f32)
    put_grads(grads_ref, 6, dot_tn(attended, d_one_b)[:E])
    put_grads(grads_ref, 8, dot_tn(normed_one, d_pre_b)[:E])
    put_grads(grads_ref, 14, dot_tn(d_two_b, hidden)[:E])

    da_t, da_rows, q_rows, dots = [], [], [], []
    for f in range(feats):
        mine = d_att[f * rows : (f + 1) * rows]
        mine_t = mine.T
        da_t.append(spread_columns(mine_t, False))
        da_rows.append(spread_rows(mine))
        q_rows.append(spread_rows(qn[f]))
        product = mine_t * attended_t[f]
        dots.append(
            jnp.concatenate(
                [
                    jnp.sum(product[SIZE * h : SIZE * (h + 1)], axis=0, keepdims=True)
                    for h in range(H)
                ],
                axis=1,
            )
        )

    send_ref[...] = jnp.zeros_like(send_ref)

    def back(c, d_queries):
        start = pl.ds(pl.multiple_of(c * chunk, chunk), chunk)
        result = []
        d_cells = jnp.zeros((chunk, feats * E), f32)
        for f in range(feats):
            grad_w = dot_nn(v_s[f, start, :], da_t[f])
            probs = e_s[f, start, :] * inverse[f]
            d_scores = (probs * (grad_w - dots[f]) * TEMPER).astype(bf16)
            result.append(d_queries[f] + dot_tn(k_s[f, start, :], d_scores))
            d_key = dot_nn(d_scores, q_rows[f])
            d_value = dot_nn(p_s[f, start, :], da_rows[f]).astype(bf16)
            body = kp_s[f, start, :]
            scale = lax.rsqrt(mean_e(body * body) + 1e-06)
            d_kpre = rms_back(body, scale, k_gain, d_key).astype(bf16)
            d_s[start, 2 * f * W : (2 * f + 1) * W] = d_kpre
            d_s[start, (2 * f + 1) * W : (2 * f + 2) * W] = d_value
            d_cells = d_cells + dot_nn(d_kpre, wkt_ref[f]) + dot_nn(d_value, wvt_ref[f])
        d_cells = d_cells.astype(bf16)
        for b in range(chunk // BLK):
            send_ref[owner_ref[c * (chunk // BLK) + b]] = d_cells[b * BLK : (b + 1) * BLK]
        return tuple(result)

    d_queries = lax.fori_loop(0, chunks, back, (jnp.zeros((W, H * rows), f32),) * feats)

    d_test = jnp.zeros((rows, feats * E), f32)
    g_query = jnp.zeros((W, W), f32)
    placed = []
    for f in range(feats):
        d_query = head_blocks(d_queries[f]).T
        d_qpre = rms_back(qp[f], qr[f], q_gain, d_query).astype(bf16)
        g_query = g_query + dot_tn(tc[f].astype(bf16), d_qpre)
        d_one_f = d_one[f * rows : (f + 1) * rows]
        d_test = d_test + dot_nn(d_qpre, wqt_ref[f])
        placed.append(d_one_f[:, :E])
    grad_test_ref[...] = (d_test + jnp.concatenate(placed, axis=1)).astype(bf16)
    put_grads(grads_ref, 0, g_query[:E])
    kv = dot_tn(cells_s[...], d_s[...])
    put_grads(grads_ref, 2, kv[:E, : 2 * W] + kv[E:, 2 * W :])
    grads_ref[20 * E :, :] = jnp.zeros((GRAD_ROWS - 20 * E, 128), bf16)


def put_grads(grads_ref, first, value):
    for i in range(value.shape[1] // 128):
        rows = slice((first + i) * E, (first + i + 1) * E)
        grads_ref[rows, :] = value[:, 128 * i : 128 * (i + 1)].astype(bf16)


def take_grads(ref, first, pieces):
    return jnp.concatenate(
        [ref[(first + i) * E : (first + i + 1) * E, :].astype(f32) for i in range(pieces)], axis=1
    )


def add_kernel(in_ref, out_ref):
    out_ref[...] = jnp.sum(in_ref[...].astype(f32), axis=0).astype(bf16)


def add_copies_kernel(in_ref, out_ref):
    total = jnp.sum(in_ref[...].astype(f32), axis=0).astype(bf16)
    out_ref[...] = jnp.broadcast_to(total[None], out_ref.shape)


def unpack_kernel(in_ref, query_ref, key_ref, value_ref, w_out_ref, up_ref, down_ref):
    for i, ref in enumerate((query_ref, key_ref, value_ref, w_out_ref)):
        ref[...] = take_grads(in_ref, 2 * i, 2)[:, :E]
    up_ref[...] = take_grads(in_ref, 8, 6)
    down_ref[...] = take_grads(in_ref, 14, 6).T


def vmem_specs(n):
    return [pl.BlockSpec(memory_space=pltpu.VMEM)] * n


SMEM_SPEC = pl.BlockSpec(memory_space=pltpu.SMEM)
LIMIT = 48 * 1024 * 1024


def main_call(owner_of, rec, test_cells, cotangent, weights, chunk):
    count = owner_of.shape[0]
    keys = count * BLK
    rows, wide = test_cells.shape
    ht = H * rows
    return pl.pallas_call(
        functools.partial(main_kernel, chunk),
        out_shape=(
            jax.ShapeDtypeStruct((rows, wide), bf16),
            jax.ShapeDtypeStruct((rows, wide), bf16),
            jax.ShapeDtypeStruct(rec.shape, bf16),
            jax.ShapeDtypeStruct((GRAD_ROWS, 128), bf16),
        ),
        in_specs=[SMEM_SPEC] + vmem_specs(3 + len(weights)),
        out_specs=tuple(vmem_specs(4)),
        scratch_shapes=[
            pltpu.VMEM((keys, wide), bf16),
            pltpu.VMEM((2, keys, W), f32),
            pltpu.VMEM((2, keys, W), bf16),
            pltpu.VMEM((2, keys, W), bf16),
            pltpu.VMEM((2, keys, ht), f32),
            pltpu.VMEM((2, keys, ht), bf16),
            pltpu.VMEM((keys, 4 * W), bf16),
        ],
        compiler_params=pltpu.CompilerParams(vmem_limit_bytes=LIMIT),
    )(owner_of, rec, test_cells, cotangent, *weights)


def pad_to(x, rows, cols):
    return jnp.pad(x, ((0, rows - x.shape[0]), (0, cols - x.shape[1])))


def prepare(w_query, q_gain, w_key, k_gain, w_value, w_out, gain_one, w_up, w_down, gain_two):
    def at_feature(w):
        zero = jnp.zeros_like(w)
        return jnp.stack([jnp.concatenate([w, zero]), jnp.concatenate([zero, w])])

    def turned(w):
        t = pad_to(w.T, W, E)
        zero = jnp.zeros_like(t)
        return jnp.stack(
            [jnp.concatenate([t, zero], axis=1), jnp.concatenate([zero, t], axis=1)]
        )

    eye = jnp.eye(E, dtype=bf16)
    first = jnp.zeros((E, W), bf16).at[0, E].set(1.0)
    gains = jnp.stack([jnp.pad(g, (0, W - E)) for g in (q_gain, k_gain, gain_one, gain_two)])
    return (
        at_feature(pad_to(w_query, E, W)),
        at_feature(pad_to(w_key, E, W) + first),
        at_feature(pad_to(w_value, E, W)),
        at_feature(pad_to(eye, E, W)),
        turned(w_query),
        turned(w_key),
        turned(w_value),
        turned(eye),
        pad_to(w_out, W, W),
        pad_to(w_up, W, FFH),
        pad_to(w_down, FFH, W),
        gains,
    )


def on_device(
    test_cells,
    train_cells,
    train_present,
    retrieved,
    w_query,
    q_gain,
    w_key,
    k_gain,
    w_value,
    w_out,
    gain_one,
    w_up,
    w_down,
    gain_two,
    cotangent,
):
    owners = lax.axis_size("rows")
    feats = 2
    blocks_own = train_cells.shape[0] // BLK
    wide = train_cells.shape[1]
    wanted = retrieved[0]
    owner_of = wanted // blocks_own
    local_ids = wanted % blocks_own
    places = jnp.arange(owners, dtype=jnp.int32)
    hits = owner_of[None, :] == places[:, None]
    requests = jnp.sum(jnp.where(hits, local_ids[None, :] + 1, 0), axis=1) - 1
    asked = lax.all_to_all(
        requests.reshape(owners, 1), "rows", split_axis=0, concat_axis=0, tiled=True
    ).reshape(-1)
    pick = jnp.clip(asked, 0, blocks_own - 1)
    mask = jnp.repeat(train_present.T != 0, E, axis=1)
    marked = jnp.where(mask, train_cells, jnp.asarray(ABSENT, bf16)).reshape(blocks_own, BLK, wide)
    to_send = pl.pallas_call(
        pick_kernel,
        out_shape=jax.ShapeDtypeStruct((owners, BLK, wide), bf16),
        in_specs=[SMEM_SPEC] + vmem_specs(1),
        out_specs=vmem_specs(1)[0],
        compiler_params=pltpu.CompilerParams(vmem_limit_bytes=LIMIT),
    )(pick, marked)
    rec = lax.all_to_all(to_send, "rows", split_axis=0, concat_axis=0, tiled=True)
    weights = prepare(
        w_query, q_gain, w_key, k_gain, w_value, w_out, gain_one, w_up, w_down, gain_two
    )
    out_cells, grad_test, terms, grads = main_call(
        owner_of, rec, test_cells, cotangent, weights, 256
    )
    back = lax.all_to_all(terms, "rows", split_axis=0, concat_axis=0, tiled=True)
    grad_train = pl.pallas_call(
        sum_kernel,
        out_shape=jax.ShapeDtypeStruct((blocks_own, BLK, wide), bf16),
        in_specs=[SMEM_SPEC] + vmem_specs(1),
        out_specs=vmem_specs(1)[0],
        scratch_shapes=[pltpu.VMEM((blocks_own, BLK, wide), f32)],
        compiler_params=pltpu.CompilerParams(vmem_limit_bytes=LIMIT),
    )(asked, back).reshape(blocks_own * BLK, wide)
    return (out_cells, grad_test, grad_train) + sum_grads(grads)


def small_call(kernel, out_shape, *args):
    return pl.pallas_call(
        kernel,
        out_shape=out_shape,
        in_specs=vmem_specs(len(args)),
        out_specs=jax.tree.map(lambda _: vmem_specs(1)[0], out_shape),
    )(*args)


def sum_grads(grads):
    owners, feats = lax.axis_size("rows"), lax.axis_size("feat")
    share = GRAD_ROWS // feats
    piece = share // owners
    parts = lax.all_to_all(
        grads.reshape(feats, share, 128), "feat", split_axis=0, concat_axis=0, tiled=True
    )
    over_feat = small_call(add_kernel, jax.ShapeDtypeStruct((share, 128), bf16), parts)
    parts = lax.all_to_all(
        over_feat.reshape(owners, piece, 128), "rows", split_axis=0, concat_axis=0, tiled=True
    )
    copies = small_call(
        add_copies_kernel, jax.ShapeDtypeStruct((owners, piece, 128), bf16), parts
    )
    over_all = lax.all_to_all(copies, "rows", split_axis=0, concat_axis=0, tiled=True)
    total = lax.all_gather(over_all.reshape(share, 128), "feat", tiled=True)
    square = jax.ShapeDtypeStruct((E, E), f32)
    return small_call(
        unpack_kernel,
        (square,) * 4
        + (jax.ShapeDtypeStruct((E, FFH), f32), jax.ShapeDtypeStruct((FFH, E), f32)),
        total,
    )


def solution(mesh):
    in_specs = (
        P("rows", "feat"),
        P("rows", "feat"),
        P("feat", "rows"),
        P("rows", None),
        P(),
        P(),
        P(),
        P(),
        P(),
        P(),
        P(),
        P(),
        P(),
        P(),
        P("rows", "feat"),
    )
    out_specs = (
        P("rows", "feat"),
        P("rows", "feat"),
        P("rows", "feat"),
        P(),
        P(),
        P(),
        P(),
        P(),
        P(),
    )
    return jax.shard_map(
        on_device, mesh=mesh, in_specs=in_specs, out_specs=out_specs, check_vma=False
    )
```

time: 590 us -> 208 us (0.35); the launches traced: 581 us -> 207 us
  waiting for transfers between devices: 283 us -> 71.6 us
  local copies, waits for them, and re-layouts: 100 us -> 14.1 us
  matrix products: 68 us -> 0 us
  Pallas kernels: 0 us -> 29.2 us
  other arithmetic: 26.1 us -> 3.99 us
  starting transfers between devices: 40.5 us -> 21.9 us
    psum x1 -> x0, waiting for transfers between devices: 260 us -> none  [on_device(): lax.psum((g_query, g_key, g_value, g_out, g_up, g_down), ('rows', 'feat'))]
    dot_general x32 -> x0, matrix products: 68 us -> none  [the longest x2 19.4 us: feature_back(): jnp.einsum('htk,thd->khd', d_scores, q_part, preferred_element_type=jnp.f...]
    all_to_all x5 -> x3, waiting for transfers between devices: 23.6 us -> 70.9 us  [the longest x1 36 us: on_device(): lax.all_to_all(terms, 'rows', split_axis=0, concat_axis=0, tiled=True)]
    pallas_call x0 -> x6, Pallas kernels: none -> 29.2 us  [the longest x1 18.8 us: main_call(): pl.pallas_call(functools.partial(main_kernel, chunk), out_shape=(jax.Shap...]
    slice x12 -> x0, local copies, waits for them, and re-layouts: 21.5 us -> none  [the longest x3 9.09 us: on_device(): value_grid[:, feature]]
    convert_element_type x19 -> x0, local copies, waits for them, and re-layouts: 19.6 us -> none  [the longest x2 7.06 us: feature_back(): d_key = jnp.einsum('htk,thd->khd', d_scores, q_part, preferred_element_ty...]
    all_to_all x5 -> x3, starting transfers between devices: 40.2 us -> 21.8 us  [the longest x1 11.4 us: on_device(): lax.all_to_all(requests.reshape(owners, 1), 'rows', split_axis=0, concat_...]
    reshape x18 -> x0, local copies, waits for them, and re-layouts: 15 us -> none  [the longest x2 3.57 us: on_device(): d_query_all = jnp.stack(query_parts, axis=1).reshape(-1, width)]
  transfers between devices with their start and end apart: 6 -> 4, of which waited for: 4 -> 3; matrix products, arithmetic and copies ran while one was open for 20% -> 5% of each run, Pallas kernels for 0% -> 1%
where the time goes in v1:
time: 208 us; the launch traced here: 207 us
  waiting for transfers between devices  71.6 us (34%)
  blocking collectives  50.9 us (24%)
  Pallas kernels  29.2 us (14%)
  starting transfers between devices  21.9 us (11%)
  between operations  15.8 us (8%)
  local copies, waits for them, and re-layouts  14.1 us (7%)
  other arithmetic  3.99 us (2%)
    all_to_all x1, waiting for transfers between devices, on_device(): lax.all_to_all(terms, 'rows', split_axis=0, concat_axis=0, tiled=True)  36 us
    all_to_all x1, waiting for transfers between devices, on_device(): lax.all_to_all(to_send, 'rows', split_axis=0, concat_axis=0, tiled=True)  28.5 us
    all_to_all x1, blocking collectives, sum_grads(): lax.all_to_all(grads.reshape(feats, share, 128), 'feat', split_axis=0, co...  20.3 us
    pallas_call x1, Pallas kernels, main_call(): pl.pallas_call(functools.partial(main_kernel, chunk), out_shape=(jax.Shap...  18.8 us
    all_to_all x1, blocking collectives, sum_grads(): lax.all_to_all(over_feat.reshape(owners, piece, 128), 'rows', split_axis=...  15.7 us
    all_to_all x1, blocking collectives, sum_grads(): lax.all_to_all(copies, 'rows', split_axis=0, concat_axis=0, tiled=True)  14.9 us
    all_to_all x1, starting transfers between devices, on_device(): lax.all_to_all(requests.reshape(owners, 1), 'rows', split_axis=0, concat_...  11.4 us
    unnamed x38, local copies, waits for them, and re-layouts  7.84 us
  transfers between devices with their start and end apart: 4, of which 3 were waited for; matrix products, arithmetic and copies ran while one was open for 5% of the time, Pallas kernels for 1%

profile of v1, /device:TPU:32, one launch (start us, length us, event | category | flops | bytes accessed | tf_op | source)
XLA Modules:
  0.0 207.3 jit_solution(3176433659992115193)
XLA Ops:
  7.2 0.7 fusion.2
  7.8 0.1 select_reduce_fusion
  7.9 0.7 copy.53
  8.6 11.4 %all-to-all-start = ((s32[32,1,1]{2,1,0:T(1,128)}), s32[32,1,1]{2,1,0:T(1,128)S(1)}, u32[]{:S(2)}, u32[]{:S(2)}) async-start(s32[32,1,1]{2,1,0:T(1,128)} %copy.53), calls=%async_computation | async-start | bytes 32768 | tf_op jit(solution)/shard_map/all_to_all | solution.py:432
  20.0 0.7 compare_bitcast_fusion
  20.7 1.2 copy.54
  21.9 0.2 copy.55
  22.1 6.4 %all-to-all-done = s32[32,1,1]{2,1,0:T(1,128)S(1)} async-done(((s32[32,1,1]{2,1,0:T(1,128)}), s32[32,1,1]{2,1,0:T(1,128)S(1)}, u32[]{:S(2)}, u32[]{:S(2)}) %all-to-all-start) | async-done | bytes 160 | tf_op jit(solution)/shard_map/all_to_all | solution.py:432
  28.5 0.7 reduce.7.asked_ref
  29.2 2.1 %shard_map.214 = bf16[32,64,384]{2,1,0:T(8,128)(2,1)} custom-call(s32[32]{0:T(128)S(1)} %broadcast_clamp_fusion.pick_ref, bf16[8,64,384]{2,1,0:T(8,128)(2,1)S(1)} %bitcast.65), custom_call_target="tpu_custom_call" | custom-call | tf_op jit(solution)/shard_map/pallas_call | solution.py:438
  31.4 5.8 %all-to-all-start.1 = ((bf16[32,64,384]{2,1,0:T(8,128)(2,1)}), bf16[32,64,384]{2,1,0:T(8,128)(2,1)}, u32[]{:S(2)}, u32[]{:S(2)}) async-start(bf16[32,64,384]{2,1,0:T(8,128)(2,1)} %shard_map.214), calls=%async_computation.1 | async-start | bytes 3145728 | tf_op jit(solution)/shard_map/all_to_all | solution.py:445
  37.3 0.1 copy.56
  37.4 0.1 copy.58
  37.6 0.1 copy.57
  37.9 0.3 copy-done.9
  38.1 0.7 pad.90.w_out_ref
  38.8 0.2 copy.59
  39.0 0.1 pad.92.w_down_ref
  39.1 0.6 and_reduce_fusion
  40.4 0.6 fusion.3
  41.0 1.9 pad_dynamic-slice_fusion
  43.5 1.4 add.90
  45.1 0.1 pad_bitcast_fusion.5
  45.2 0.1 pad_bitcast_fusion.3
  45.3 0.1 pad_bitcast_fusion.7
  45.4 0.1 pad_bitcast_fusion.1
  45.7 0.1 pad_maximum_fusion.4
  45.8 0.1 pad_maximum_fusion.6
  45.9 0.1 pad_maximum_fusion
  46.0 0.8 pad_maximum_fusion.2
  46.8 28.5 %all-to-all-done.1.rec_ref = bf16[32,64,384]{2,1,0:T(8,128)(2,1)} async-done(((bf16[32,64,384]{2,1,0:T(8,128)(2,1)}), bf16[32,64,384]{2,1,0:T(8,128)(2,1)}, u32[]{:S(2)}, u32[]{:S(2)}) %all-to-all-start.1) | async-done | bytes 1572896 | tf_op jit(solution)/shard_map/all_to_all | solution.py:445
  75.3 1.0 copy-done
  76.3 0.9 copy-done.1
  77.2 0.9 copy-done.2
  78.1 0.9 copy-done.3
  79.0 18.8 %shard_map.215 = (bf16[128,384]{1,0:T(8,128)(2,1)}, bf16[128,384]{1,0:T(8,128)(2,1)}, bf16[32,64,384]{2,1,0:T(8,128)(2,1)}, bf16[4096,128]{1,0:T(8,128)(2,1)S(1)}) custom-call(s32[16]{0:T(128)S(1)} %and_select_fusion.2.owner_ref, bf16[32,64,384]{2,1,0:T(8,128)(2,1)} %all-to-all-done.1.rec_ref, bf16[128,384]{1,0:T(8,128)(2,1)S(1)} %copy-done.2, ...), custom_call_target="tpu_custom_call" | custom-call | tf_op jit(solution)/shard_map/pallas_call | solution.py:347
  97.8 20.3 %all_to_all.31.in_ref = bf16[8,512,128]{2,1,0:T(8,128)(2,1)} all-to-all(bf16[8,512,128]{2,1,0:T(8,128)(2,1)S(1)} %bitcast.66), channel_id=1, replica_groups=mesh['rows'=32,'feat'=8] {'feat'}, dimensions={0} | all-to-all | bytes 2097152 | tf_op jit(solution)/shard_map/all_to_all | solution.py:477
  118.1 2.0 shard_map.217
  120.1 15.7 %all_to_all.32.in_ref = bf16[32,16,128]{2,1,0:T(8,128)(2,1)} all-to-all(bf16[32,16,128]{2,1,0:T(8,128)(2,1)} %bitcast.67), channel_id=1, replica_groups=mesh['rows'=32,'feat'=8] {'rows'}, dimensions={0} | all-to-all | bytes 262144 | tf_op jit(solution)/shard_map/all_to_all | solution.py:481
  135.8 1.6 shard_map.218
  137.4 14.9 %all_to_all.33 = bf16[32,16,128]{2,1,0:T(8,128)(2,1)} all-to-all(bf16[32,16,128]{2,1,0:T(8,128)(2,1)} %shard_map.218), channel_id=1, replica_groups=mesh['rows'=32,'feat'=8] {'rows'}, dimensions={0} | all-to-all | bytes 262144 | tf_op jit(solution)/shard_map/all_to_all | solution.py:487
  152.3 4.6 %all-to-all-start.2 = ((bf16[32,64,384]{2,1,0:T(8,128)(2,1)}), bf16[32,64,384]{2,1,0:T(8,128)(2,1)S(1)}, u32[]{:S(2)}, u32[]{:S(2)}) async-start(bf16[32,64,384]{2,1,0:T(8,128)(2,1)} %get-tuple-element.33), calls=%async_computation.2 | async-start | bytes 3145728 | tf_op jit(solution)/shard_map/all_to_all | solution.py:452
  156.9 0.0 all-gather.2.cloned.1.call-start
  157.0 0.7 all-gather.2.cloned.1.call-update
  157.7 36.0 %all-to-all-done.2.back_ref = bf16[32,64,384]{2,1,0:T(8,128)(2,1)S(1)} async-done(((bf16[32,64,384]{2,1,0:T(8,128)(2,1)}), bf16[32,64,384]{2,1,0:T(8,128)(2,1)S(1)}, u32[]{:S(2)}, u32[]{:S(2)}) %all-to-all-start.2) | async-done | bytes 1572896 | tf_op jit(solution)/shard_map/all_to_all | solution.py:452
  193.7 1.9 shard_map.216
  195.6 2.7 %shard_map.219 = (f32[192,192]{1,0:T(8,128)}, f32[192,192]{1,0:T(8,128)}, f32[192,192]{1,0:T(8,128)}, f32[192,192]{1,0:T(8,128)}, f32[192,768]{1,0:T(8,128)}, /*index=5*/f32[768,192]{1,0:T(8,128)}) custom-call(bf16[4096,128]{1,0:T(8,128)(2,1)} %all-gather.2.cloned.1.call-done.in_ref), custom_call_target="tpu_custom_call" | custom-call | tf_op jit(solution)/shard_map/pallas_call | solution.py:465
  198.2 2.2 %copy.60 = f32[768,192]{0,1:T(8,128)} copy(f32[768,192]{1,0:T(8,128)} %get-tuple-element.85) | data formatting | bytes 1179648
  (53 shorter events, 0.5 us)
Async XLA Ops:
  8.6 19.9 %all-to-all-start = ((s32[32,1,1]{2,1,0:T(1,128)}), s32[32,1,1]{2,1,0:T(1,128)S(1)}, u32[]{:S(2)}, u32[]{:S(2)}) async-start(s32[32,1,1]{2,1,0:T(1,128)} %copy.53), calls=%async_computation | async-start | bytes 32768 | tf_op jit(solution)/shard_map/all_to_all | solution.py:432
  31.3 5.9 %copy-start.5 = (bf16[192,192]{1,0:T(8,128)(2,1)S(1)}, bf16[192,192]{1,0:T(8,128)(2,1)}, u32[]{:S(2)}) copy-start(bf16[192,192]{1,0:T(8,128)(2,1)} %param.21) | copy-start | bytes 221188
  31.3 6.1 %copy-start.6 = (bf16[192,192]{1,0:T(8,128)(2,1)S(1)}, bf16[192,192]{1,0:T(8,128)(2,1)}, u32[]{:S(2)}) copy-start(bf16[192,192]{1,0:T(8,128)(2,1)} %param.25) | copy-start | bytes 221188
  31.3 6.2 %copy-start.4 = (bf16[192,192]{1,0:T(8,128)(2,1)S(1)}, bf16[192,192]{1,0:T(8,128)(2,1)}, u32[]{:S(2)}) copy-start(bf16[192,192]{1,0:T(8,128)(2,1)} %param.23) | copy-start | bytes 221188
  31.3 6.4 %copy-start.10 = (f32[192]{0:T(256)S(1)}, f32[192]{0:T(256)}, u32[]{:S(2)}) copy-start(f32[192]{0:T(256)} %param.22) | copy-start | bytes 2308
  31.3 6.4 %copy-start.11 = (f32[192]{0:T(256)S(1)}, f32[192]{0:T(256)}, u32[]{:S(2)}) copy-start(f32[192]{0:T(256)} %param.24) | copy-start | bytes 2308
  31.4 6.4 %copy-start.12 = (f32[192]{0:T(256)S(1)}, f32[192]{0:T(256)}, u32[]{:S(2)}) copy-start(f32[192]{0:T(256)} %param.27) | copy-start | bytes 2308
  31.4 6.4 %copy-start.13 = (f32[192]{0:T(256)S(1)}, f32[192]{0:T(256)}, u32[]{:S(2)}) copy-start(f32[192]{0:T(256)} %param.30) | copy-start | bytes 2308
  31.4 43.9 %all-to-all-start.1 = ((bf16[32,64,384]{2,1,0:T(8,128)(2,1)}), bf16[32,64,384]{2,1,0:T(8,128)(2,1)}, u32[]{:S(2)}, u32[]{:S(2)}) async-start(bf16[32,64,384]{2,1,0:T(8,128)(2,1)} %shard_map.214), calls=%async_computation.1 | async-start | bytes 3145728 | tf_op jit(solution)/shard_map/all_to_all | solution.py:445
  37.2 0.9 copy-start.9
  37.2 1.6 copy-start.7
  37.3 1.6 copy-start.8
  37.7 1.4 copy-start.15
  45.9 0.9 copy-start.14
  75.3 1.0 copy-start
  76.3 0.9 copy-start.1
  77.2 0.9 copy-start.2
  78.1 0.9 copy-start.3
  152.3 41.4 %all-to-all-start.2 = ((bf16[32,64,384]{2,1,0:T(8,128)(2,1)}), bf16[32,64,384]{2,1,0:T(8,128)(2,1)S(1)}, u32[]{:S(2)}, u32[]{:S(2)}) async-start(bf16[32,64,384]{2,1,0:T(8,128)(2,1)} %get-tuple-element.33), calls=%async_computation.2 | async-start | bytes 3145728 | tf_op jit(solution)/shard_map/all_to_all | solution.py:452
  156.9 38.6 %all-gather.2.cloned.1.call-start = ((), (), s32[]{:S(2)}) async-start(), calls=%async_computation.6 | async-start | bytes 1179648 | tf_op jit(solution)/shard_map/all_gather | solution.py:488
Sparse Core Ops, SparseCore 0:
  159.6 25.1 all-gather.1

commit v2 on v1

v2 whole, which is shorter than its diff:
```python
import functools
import math

import jax
import jax.numpy as jnp
from jax import lax
from jax.experimental import pallas as pl
from jax.experimental.pallas import tpu as pltpu
from jax.sharding import PartitionSpec as P

H = 6
BLK = 64
E = 192
W = 256
FFH = 768
SIZE = E // H
TEMPER = 1.5 / math.sqrt(SIZE)
LOG2E = math.log2(math.e)
GELU_C = math.sqrt(2.0 / math.pi)
ABSENT = 8.0
ABSENT_ABOVE = 7.0
MASKED = -30000.0
GRAD_ROWS = 4096

bf16 = jnp.bfloat16
f32 = jnp.float32


def dot_nn(a, b):
    return lax.dot_general(a, b, (((1,), (0,)), ((), ())), preferred_element_type=f32)


def dot_nt(a, b):
    return lax.dot_general(a, b, (((1,), (1,)), ((), ())), preferred_element_type=f32)


def dot_tn(a, b):
    return lax.dot_general(a, b, (((0,), (0,)), ((), ())), preferred_element_type=f32)


def pick_kernel(asked_ref, cells_ref, out_ref, sem):
    def body(slot, carry):
        pltpu.make_async_copy(
            cells_ref.at[jnp.maximum(asked_ref[slot], 0)], out_ref.at[slot], sem
        ).start()
        return carry

    lax.fori_loop(0, out_ref.shape[0], body, 0)
    pltpu.make_async_copy(out_ref, out_ref, sem).wait()


def add_terms(asked_ref, back_ref, acc_ref):
    def body(slot, carry):
        asked = asked_ref[slot]

        @pl.when(asked >= 0)
        def _():
            acc_ref[asked] += back_ref[slot, : acc_ref.shape[1]].astype(f32)

        return carry

    lax.fori_loop(0, back_ref.shape[0], body, 0)


def sum_kernel(asked_ref, one_ref, two_ref, acc_ref):
    for part, ref in enumerate((one_ref, two_ref)):
        mine = acc_ref.at[part]
        mine[...] = jnp.zeros(mine.shape, f32)
        add_terms(asked_ref, ref, mine)


def last_kernel(asked_ref, sums_ref, three_ref, out_ref, acc_ref):
    acc_ref[...] = jnp.zeros_like(acc_ref)
    add_terms(asked_ref, three_ref, acc_ref)
    one, two, three = sums_ref[0], sums_ref[1], acc_ref[...]
    out_ref[:, :, 0:128] = jnp.concatenate([one, two[:, :16]], axis=1).astype(bf16)
    out_ref[:, :, 128:256] = jnp.concatenate([two[:, 16:], three[:, :32]], axis=1).astype(bf16)
    out_ref[:, :, 256:384] = three[:, 32:].astype(bf16)


def mean_e(x):
    return jnp.sum(x, axis=-1, keepdims=True) * (1.0 / E)


def head_blocks(full):
    return jnp.concatenate(
        [full[SIZE * h : SIZE * (h + 1), 128 * h : 128 * (h + 1)] for h in range(H)]
        + [jnp.zeros((W - E, 128), f32)],
        axis=0,
    )


def spread_columns(tall, last):
    row = lax.broadcasted_iota(jnp.int32, tall.shape, 0)
    parts = []
    for h in range(H):
        inside = (row >= SIZE * h) & (row < SIZE * (h + 1))
        part = jnp.where(inside, tall, 0.0)
        if last:
            part = jnp.where(row == E, 1.0, part)
        parts.append(part)
    return jnp.concatenate(parts, axis=1).astype(bf16)


def spread_rows(wide):
    lane = lax.broadcasted_iota(jnp.int32, wide.shape, 1)
    parts = []
    for h in range(H):
        inside = (lane >= SIZE * h) & (lane < SIZE * (h + 1))
        parts.append(jnp.where(inside, wide, 0.0))
    return jnp.concatenate(parts, axis=0).astype(bf16)


def layer_norm(x, lane_in):
    centred = jnp.where(lane_in, x - mean_e(x), 0.0)
    scale = lax.rsqrt(mean_e(centred * centred) + 1e-05)
    return centred * scale, scale


def layer_norm_back(hat, scale, gain, dy):
    u = dy * gain
    return scale * (u - mean_e(u) - hat * mean_e(u * hat))


def rms_back(pre, scale, gain, dy):
    u = dy * gain
    return scale * (u - pre * (scale * scale) * mean_e(pre * u))


def widen(x, cols):
    return jnp.concatenate([x, jnp.zeros((x.shape[0], cols - x.shape[1]), x.dtype)], axis=1)


def heighten(x, rows):
    return jnp.concatenate([x, jnp.zeros((rows - x.shape[0], x.shape[1]), x.dtype)], axis=0)


def prepare_kernel(
    test_ref,
    cot_ref,
    w_query_ref,
    w_key_ref,
    w_value_ref,
    w_out_ref,
    w_up_ref,
    w_down_t_ref,
    q_gain_ref,
    k_gain_ref,
    gain_one_ref,
    gain_two_ref,
    projections_ref,
    ffn_ref,
    gains_ref,
    cells_ref,
    q_pre_ref,
    q_tall_ref,
    q_rows_ref,
):
    rows = test_ref.shape[0]
    row = lax.broadcasted_iota(jnp.int32, (E, W), 0)
    lane = lax.broadcasted_iota(jnp.int32, (E, W), 1)
    place = jnp.where(row == lane, 1.0, 0.0).astype(bf16)
    first = jnp.where((row == 0) & (lane == E), 1.0, 0.0).astype(bf16)
    nothing = jnp.zeros((E, W), bf16)
    weights = (
        widen(w_query_ref[...], W),
        widen(w_key_ref[...], W) + first,
        widen(w_value_ref[...], W),
        place,
    )
    for i, weight in enumerate(weights):
        for f in range(2):
            projections_ref[i, f, f * E : (f + 1) * E, :] = weight
            projections_ref[i, f, (1 - f) * E : (2 - f) * E, :] = nothing
    ffn_ref[:, :FFH] = heighten(w_up_ref[...], W)
    ffn_ref[:, FFH : 2 * FFH] = heighten(w_down_t_ref[...], W)
    ffn_ref[:, 2 * FFH :] = heighten(widen(w_out_ref[...], W), W)
    for i, ref in enumerate((q_gain_ref, k_gain_ref, gain_one_ref, gain_two_ref)):
        gains_ref[i : i + 1, :] = widen(ref[...], W)
    test = test_ref[...]
    cot = cot_ref[...]
    q_gain = gains_ref[0:1, :]
    for f in range(2):
        here = slice(f * rows, (f + 1) * rows)
        cells_ref[0, here, :] = dot_nn(test, projections_ref[3, f])
        cells_ref[1, here, :] = dot_nn(cot, projections_ref[3, f])
        pre = dot_nn(test, projections_ref[0, f])
        norm = pre * lax.rsqrt(mean_e(pre * pre) + 1e-06) * q_gain
        norm = norm.astype(bf16).astype(f32)
        q_pre_ref[here, :] = pre
        q_tall_ref[f] = spread_columns(norm.T, True)
        q_rows_ref[f] = spread_rows(norm)


def main_kernel(
    chunk,
    owner_ref,
    rec_hbm,
    projections_hbm,
    ffn_hbm,
    gains_hbm,
    cells_hbm,
    q_pre_hbm,
    q_tall_hbm,
    q_rows_hbm,
    out_ref,
    grad_test_ref,
    one_ref,
    two_ref,
    three_ref,
    grads_ref,
    projections_ref,
    ffn_ref,
    gains_ref,
    cells_ref,
    q_pre_ref,
    q_tall_ref,
    q_rows_ref,
    cells_s,
    kp_s,
    k_s,
    v_s,
    e_s,
    p_s,
    d_s,
    rec_sem,
    sems,
):
    count = owner_ref.shape[0]
    feats = 2
    rows = out_ref.shape[0]
    keys = count * BLK
    chunks = keys // chunk

    def gather(j, carry):
        pltpu.make_async_copy(
            rec_hbm.at[owner_ref[j]],
            cells_s.at[pl.ds(pl.multiple_of(j * BLK, BLK), BLK), :],
            rec_sem,
        ).start()
        return carry

    lax.fori_loop(0, count, gather, 0)
    copies = [
        pltpu.make_async_copy(source, target, sems.at[i])
        for i, (source, target) in enumerate(
            (
                (projections_hbm, projections_ref),
                (gains_hbm, gains_ref),
                (q_tall_hbm, q_tall_ref),
                (ffn_hbm, ffn_ref),
                (cells_hbm, cells_ref),
                (q_pre_hbm, q_pre_ref),
                (q_rows_hbm, q_rows_ref),
            )
        )
    ]
    for copy in copies:
        copy.start()
    one_ref[...] = jnp.zeros_like(one_ref)
    two_ref[...] = jnp.zeros_like(two_ref)
    three_ref[...] = jnp.zeros_like(three_ref)
    pltpu.make_async_copy(cells_s, cells_s, rec_sem).wait()
    for copy in copies:
        copy.wait()

    q_gain = gains_ref[0:1, :]
    k_gain = gains_ref[1:2, :]
    gain_one = gains_ref[2:3, :]
    gain_two = gains_ref[3:4, :]

    def scores(c, totals):
        start = pl.ds(pl.multiple_of(c * chunk, chunk), chunk)
        cells = cells_s[start, :]
        result = []
        for f in range(feats):
            pre = dot_nn(cells, projections_ref[1, f])
            lane = lax.broadcasted_iota(jnp.int32, pre.shape, 1)
            body = jnp.where(lane < E, pre, 0.0)
            scale = lax.rsqrt(mean_e(body * body) + 1e-06)
            norm = body * scale * k_gain
            bias = jnp.where((lane == E) & (pre > ABSENT_ABOVE), MASKED, 0.0)
            norm = (norm + bias).astype(bf16)
            kp_s[f, start, :] = body
            k_s[f, start, :] = norm
            v_s[f, start, :] = dot_nn(cells, projections_ref[2, f]).astype(bf16)
            e = jnp.exp2(dot_nn(norm, q_tall_ref[f]) * (TEMPER * LOG2E))
            e_s[f, start, :] = e
            result.append(totals[f] + jnp.sum(e, axis=0, keepdims=True))
        return tuple(result)

    zero = jnp.zeros((1, H * rows), f32)
    totals = lax.fori_loop(0, chunks, scores, (zero,) * feats)
    inverse = [1.0 / total for total in totals]

    def attend(c, mixed):
        start = pl.ds(pl.multiple_of(c * chunk, chunk), chunk)
        result = []
        for f in range(feats):
            p = (e_s[f, start, :] * inverse[f]).astype(bf16)
            p_s[f, start, :] = p
            result.append(mixed[f] + dot_tn(v_s[f, start, :], p))
        return tuple(result)

    mixed = lax.fori_loop(0, chunks, attend, (jnp.zeros((W, H * rows), f32),) * feats)
    attended_t = [head_blocks(m) for m in mixed]

    attended = jnp.concatenate([a.T for a in attended_t], axis=0).astype(bf16)
    lane_in = lax.broadcasted_iota(jnp.int32, (feats * rows, W), 1) < E
    w_up = ffn_ref[:, :FFH]
    w_down_t = ffn_ref[:, FFH : 2 * FFH]
    w_out = ffn_ref[:, 2 * FFH :]
    inner_one = cells_ref[0] + dot_nn(attended, w_out)
    hat_one, scale_one = layer_norm(inner_one, lane_in)
    normed_one = (hat_one * gain_one).astype(bf16)
    pre = dot_nn(normed_one, w_up)
    tanh = jnp.tanh(GELU_C * (pre + 0.044715 * (pre * pre * pre)))
    hidden = (0.5 * pre * (1.0 + tanh)).astype(bf16)
    slope = 0.5 * (1.0 + tanh) + (0.5 * GELU_C) * pre * (1.0 - tanh * tanh) * (
        1.0 + (3 * 0.044715) * (pre * pre)
    )
    inner_two = normed_one.astype(f32) + dot_nt(hidden, w_down_t)
    hat_two, scale_two = layer_norm(inner_two, lane_in)
    out = (hat_two * gain_two).astype(bf16)
    out_ref[...] = (
        dot_nt(out[:rows], projections_ref[3, 0]) + dot_nt(out[rows:], projections_ref[3, 1])
    ).astype(bf16)
    d_two = layer_norm_back(hat_two, scale_two, gain_two, cells_ref[1])
    d_two = jnp.where(lane_in, d_two, 0.0)
    d_two_b = d_two.astype(bf16)
    d_pre_b = (dot_nn(d_two_b, w_down_t) * slope).astype(bf16)
    d_normed = d_two + dot_nt(d_pre_b, w_up)
    d_one = layer_norm_back(hat_one, scale_one, gain_one, d_normed)
    d_one = jnp.where(lane_in, d_one, 0.0)
    d_one_b = d_one.astype(bf16)
    d_att = dot_nt(d_one_b, w_out).astype(bf16).astype(f32)
    put_grads(grads_ref, 6, dot_tn(attended, d_one_b)[:E])
    put_grads(grads_ref, 8, dot_tn(normed_one, d_pre_b)[:E])
    put_grads(grads_ref, 14, dot_tn(d_two_b, hidden)[:E])

    da_t, da_rows, dots = [], [], []
    for f in range(feats):
        mine = d_att[f * rows : (f + 1) * rows]
        mine_t = mine.T
        da_t.append(spread_columns(mine_t, False))
        da_rows.append(spread_rows(mine))
        product = mine_t * attended_t[f]
        dots.append(
            jnp.concatenate(
                [
                    jnp.sum(product[SIZE * h : SIZE * (h + 1)], axis=0, keepdims=True)
                    for h in range(H)
                ],
                axis=1,
            )
        )

    def back(c, d_queries):
        start = pl.ds(pl.multiple_of(c * chunk, chunk), chunk)
        result = []
        d_cells = jnp.zeros((chunk, feats * E), f32)
        for f in range(feats):
            grad_w = dot_nn(v_s[f, start, :], da_t[f])
            probs = e_s[f, start, :] * inverse[f]
            d_scores = (probs * (grad_w - dots[f]) * TEMPER).astype(bf16)
            result.append(d_queries[f] + dot_tn(k_s[f, start, :], d_scores))
            d_key = dot_nn(d_scores, q_rows_ref[f])
            d_value = dot_nn(p_s[f, start, :], da_rows[f]).astype(bf16)
            body = kp_s[f, start, :]
            scale = lax.rsqrt(mean_e(body * body) + 1e-06)
            d_kpre = rms_back(body, scale, k_gain, d_key).astype(bf16)
            d_s[start, 2 * f * W : (2 * f + 1) * W] = d_kpre
            d_s[start, (2 * f + 1) * W : (2 * f + 2) * W] = d_value
            d_cells = d_cells + dot_nt(d_kpre, projections_ref[1, f])
            d_cells = d_cells + dot_nt(d_value, projections_ref[2, f])
        d_cells = d_cells.astype(bf16)
        for b in range(chunk // BLK):
            owner = owner_ref[c * (chunk // BLK) + b]
            block = d_cells[b * BLK : (b + 1) * BLK]
            one_ref[owner] = block[:48, :128]
            two_ref[owner, :16] = block[48:, :128]
            two_ref[owner, 16:] = block[:32, 128:256]
            three_ref[owner, :32] = block[32:, 128:256]
            three_ref[owner, 32:] = block[:, 256:]
        return tuple(result)

    d_queries = lax.fori_loop(0, chunks, back, (jnp.zeros((W, H * rows), f32),) * feats)

    d_test = jnp.zeros((rows, feats * E), f32)
    g_query = jnp.zeros((W, W), f32)
    placed = []
    for f in range(feats):
        here = slice(f * rows, (f + 1) * rows)
        d_query = head_blocks(d_queries[f]).T
        pre = q_pre_ref[here, :]
        scale = lax.rsqrt(mean_e(pre * pre) + 1e-06)
        d_qpre = rms_back(pre, scale, q_gain, d_query).astype(bf16)
        g_query = g_query + dot_tn(cells_ref[0, here, :].astype(bf16), d_qpre)
        d_test = d_test + dot_nt(d_qpre, projections_ref[0, f])
        placed.append(d_one[here, :E])
    grad_test_ref[...] = (d_test + jnp.concatenate(placed, axis=1)).astype(bf16)
    put_grads(grads_ref, 0, g_query[:E])
    kv = dot_tn(cells_s[...], d_s[...])
    put_grads(grads_ref, 2, kv[:E, : 2 * W] + kv[E:, 2 * W :])
    grads_ref[20 * E :, :] = jnp.zeros((GRAD_ROWS - 20 * E, 128), bf16)


def put_grads(grads_ref, first, value):
    for i in range(value.shape[1] // 128):
        rows = slice((first + i) * E, (first + i + 1) * E)
        grads_ref[rows, :] = value[:, 128 * i : 128 * (i + 1)].astype(bf16)


def take_grads(ref, first, pieces):
    return jnp.concatenate(
        [ref[(first + i) * E : (first + i + 1) * E, :].astype(f32) for i in range(pieces)], axis=1
    )


def ride_kernel(parts_ref, one_ref, out_ref):
    total = jnp.sum(parts_ref[...].astype(f32), axis=0).astype(bf16)
    out_ref[:, : one_ref.shape[1], :] = one_ref[...]
    out_ref[:, one_ref.shape[1] :, :] = total.reshape(
        out_ref.shape[0], out_ref.shape[1] - one_ref.shape[1], 128
    )


def ride_back_kernel(back_ref, two_ref, out_ref):
    cut = two_ref.shape[1]
    total = jnp.sum(back_ref[:, cut:, :].astype(f32), axis=0).astype(bf16)
    out_ref[:, :cut, :] = two_ref[...]
    out_ref[:, cut:, :] = jnp.broadcast_to(total[None], out_ref[:, cut:, :].shape)


def share_kernel(back_ref, three_in, share_ref, three_out, sem):
    pieces = share_ref.shape[1]
    copy = pltpu.make_async_copy(
        back_ref.at[:, pl.ds(back_ref.shape[1] - pieces, pieces), :], share_ref, sem
    )
    copy.start()
    copy.wait()


def unpack_kernel(in_ref, query_ref, key_ref, value_ref, w_out_ref, up_ref, down_t_ref):
    for i, ref in enumerate((query_ref, key_ref, value_ref, w_out_ref)):
        ref[...] = take_grads(in_ref, 2 * i, 2)[:, :E]
    up_ref[...] = take_grads(in_ref, 8, 6)
    down_t_ref[...] = take_grads(in_ref, 14, 6)


def vmem_specs(n):
    return [pl.BlockSpec(memory_space=pltpu.VMEM)] * n


SMEM_SPEC = pl.BlockSpec(memory_space=pltpu.SMEM)
LIMIT = 48 * 1024 * 1024


ANY_SPEC = pl.BlockSpec(memory_space=pl.ANY)
PARAMS = pltpu.CompilerParams(vmem_limit_bytes=LIMIT)


def shape(dims, dtype=bf16):
    return jax.ShapeDtypeStruct(dims, dtype)


def small_call(kernel, out_shape, *args):
    return pl.pallas_call(
        kernel,
        out_shape=out_shape,
        in_specs=vmem_specs(len(args)),
        out_specs=jax.tree.map(lambda _: vmem_specs(1)[0], out_shape),
        compiler_params=PARAMS,
    )(*args)


def prepare(test_cells, cotangent, weights):
    w_query, q_gain, w_key, k_gain, w_value, w_out, gain_one, w_up, w_down, gain_two = weights
    rows, wide = test_cells.shape
    ht = H * rows
    return small_call(
        prepare_kernel,
        (
            shape((4, 2, wide, W)),
            shape((W, 2 * FFH + W)),
            shape((4, W), f32),
            shape((2, 2 * rows, W), f32),
            shape((2 * rows, W), f32),
            shape((2, W, ht)),
            shape((2, ht, W)),
        ),
        test_cells,
        cotangent,
        w_query,
        w_key,
        w_value,
        w_out,
        w_up,
        w_down.T,
        *(gain.reshape(1, E) for gain in (q_gain, k_gain, gain_one, gain_two)),
    )


def main_call(owner_of, rec, prepared, rows, chunk):
    count = owner_of.shape[0]
    keys = count * BLK
    owners, _, wide = rec.shape
    ht = H * rows
    return pl.pallas_call(
        functools.partial(main_kernel, chunk),
        out_shape=(
            shape((rows, wide)),
            shape((rows, wide)),
            shape((owners, 48, 128)),
            shape((owners, 48, 128)),
            shape((owners, 96, 128)),
            shape((GRAD_ROWS, 128)),
        ),
        in_specs=[SMEM_SPEC] + [ANY_SPEC] * (1 + len(prepared)),
        out_specs=tuple(vmem_specs(6)),
        scratch_shapes=[pltpu.VMEM(x.shape, x.dtype) for x in prepared]
        + [
            pltpu.VMEM((keys, wide), bf16),
            pltpu.VMEM((2, keys, W), f32),
            pltpu.VMEM((2, keys, W), bf16),
            pltpu.VMEM((2, keys, W), bf16),
            pltpu.VMEM((2, keys, ht), f32),
            pltpu.VMEM((2, keys, ht), bf16),
            pltpu.VMEM((keys, 4 * W), bf16),
            pltpu.SemaphoreType.DMA,
            pltpu.SemaphoreType.DMA((len(prepared),)),
        ],
        compiler_params=PARAMS,
    )(owner_of, rec, *prepared)


def swap(x, axis):
    return lax.all_to_all(x, axis, split_axis=0, concat_axis=0, tiled=True)


def unpack_shapes():
    return (shape((E, E), f32),) * 4 + (shape((E, FFH), f32),) * 2


def on_device(
    test_cells,
    train_cells,
    train_present,
    retrieved,
    w_query,
    q_gain,
    w_key,
    k_gain,
    w_value,
    w_out,
    gain_one,
    w_up,
    w_down,
    gain_two,
    cotangent,
):
    owners, groups = lax.axis_size("rows"), lax.axis_size("feat")
    blocks_own = train_cells.shape[0] // BLK
    rows, wide = test_cells.shape
    count = retrieved.shape[1]
    owner_of = retrieved[0] // blocks_own
    table = swap(jnp.broadcast_to(retrieved, (owners, count)).reshape(owners, 1, count), "rows")
    table = table.reshape(owners, count)
    mine = table // blocks_own == lax.axis_index("rows")
    asked = jnp.sum(jnp.where(mine, table % blocks_own + 1, 0), axis=1) - 1
    mask = jnp.repeat(train_present.T != 0, E, axis=1)
    marked = jnp.where(mask, train_cells, jnp.asarray(ABSENT, bf16)).reshape(blocks_own, BLK, wide)
    to_send = pl.pallas_call(
        pick_kernel,
        out_shape=shape((owners, BLK, wide)),
        in_specs=[SMEM_SPEC] + vmem_specs(1),
        out_specs=ANY_SPEC,
        scratch_shapes=[pltpu.SemaphoreType.DMA],
        compiler_params=PARAMS,
    )(asked, marked)
    rec = swap(to_send, "rows")
    prepared = prepare(
        test_cells,
        cotangent,
        (w_query, q_gain, w_key, k_gain, w_value, w_out, gain_one, w_up, w_down, gain_two),
    )
    out_cells, grad_test, one, two, three, grads = main_call(owner_of, rec, prepared, rows, 256)

    share = GRAD_ROWS // groups
    piece = share // owners
    parts = swap(grads.reshape(groups, share, 128), "feat")
    riding = shape((owners, one.shape[1] + piece, 128))
    back_one = swap(small_call(ride_kernel, riding, parts, one), "rows")
    back_two = swap(small_call(ride_back_kernel, riding, back_one, two), "rows")
    over_all, three = pl.pallas_call(
        share_kernel,
        out_shape=(shape((owners, piece, 128)), shape(three.shape)),
        in_specs=[ANY_SPEC] * 2,
        out_specs=(ANY_SPEC,) * 2,
        scratch_shapes=[pltpu.SemaphoreType.DMA],
        input_output_aliases={1: 1},
        compiler_params=PARAMS,
    )(back_two, three)
    total = lax.all_gather(over_all.reshape(share, 128), "feat", tiled=True)
    back_three = swap(three, "rows")
    sums = pl.pallas_call(
        sum_kernel,
        out_shape=shape((2, blocks_own, one.shape[1], 128), f32),
        in_specs=[SMEM_SPEC] + vmem_specs(2),
        out_specs=vmem_specs(1)[0],
        compiler_params=PARAMS,
    )(asked, back_one, back_two)
    grad_train = pl.pallas_call(
        last_kernel,
        out_shape=shape((blocks_own, BLK, wide)),
        in_specs=[SMEM_SPEC] + vmem_specs(2),
        out_specs=vmem_specs(1)[0],
        scratch_shapes=[pltpu.VMEM((blocks_own, three.shape[1], 128), f32)],
        compiler_params=PARAMS,
    )(asked, sums, back_three).reshape(blocks_own * BLK, wide)
    *others, g_down_t = small_call(unpack_kernel, unpack_shapes(), total)
    return (out_cells, grad_test, grad_train, *others, g_down_t.T)


def solution(mesh):
    in_specs = (
        P("rows", "feat"),
        P("rows", "feat"),
        P("feat", "rows"),
        P("rows", None),
        P(),
        P(),
        P(),
        P(),
        P(),
        P(),
        P(),
        P(),
        P(),
        P(),
        P("rows", "feat"),
    )
    out_specs = (
        P("rows", "feat"),
        P("rows", "feat"),
        P("rows", "feat"),
        P(),
        P(),
        P(),
        P(),
        P(),
        P(),
    )
    return jax.shard_map(
        on_device, mesh=mesh, in_specs=in_specs, out_specs=out_specs, check_vma=False
    )
```

time: 208 us -> 199 us (0.957)
  blocking collectives: 50.9 us -> 64.9 us
  waiting for transfers between devices: 71.6 us -> 58.2 us
  other arithmetic: 3.99 us -> 0.88 us
  local copies, waits for them, and re-layouts: 14.1 us -> 11.2 us
  Pallas kernels: 29.2 us -> 26.8 us
    all_to_all x3, blocking collectives: 50.9 us -> 64.9 us  [swap(): return lax.all_to_all(x, axis, split_axis=0, concat_axis=0, tiled=True)]
    all_to_all x3, waiting for transfers between devices: 70.9 us -> 58.2 us  [swap(): return lax.all_to_all(x, axis, split_axis=0, concat_axis=0, tiled=True)]
    pallas_call x3 -> x4, Pallas kernels: 6.29 us -> 2.23 us  [small_call(): pl.pallas_call(kernel, out_shape=out_shape, in_specs=vmem_specs(len(args)...]
    pad x14 -> x0, local copies, waits for them, and re-layouts: 2.78 us -> none  [the longest x10 2.76 us: pad_to(): return jnp.pad(x, ((0, rows - x.shape[0]), (0, cols - x.shape[1])))]
    unnamed x38 -> x35, local copies, waits for them, and re-layouts: 7.84 us -> 9.76 us
    pallas_call x3 -> x5, Pallas kernels: 22.9 us -> 24.6 us  [the longest x1 18.9 us: main_call(): pl.pallas_call(functools.partial(main_kernel, chunk), out_shape=(shape((r...]
  transfers between devices with their start and end apart: 4 -> 4, of which waited for: 3 -> 3; matrix products, arithmetic and copies ran while one was open for 5% -> 1% of each run, Pallas kernels for 1% -> 2%
where the time goes in v2:
time: 199 us; the launch traced here: 198 us
  blocking collectives  64.9 us (33%)
  waiting for transfers between devices  58.2 us (29%)
  Pallas kernels  26.8 us (13%)
  starting transfers between devices  22.1 us (11%)
  between operations  14.3 us (7%)
  local copies, waits for them, and re-layouts  11.2 us (6%)
    all_to_all x3, blocking collectives, swap(): return lax.all_to_all(x, axis, split_axis=0, concat_axis=0, tiled=True)  64.9 us
    all_to_all x3, waiting for transfers between devices, swap(): return lax.all_to_all(x, axis, split_axis=0, concat_axis=0, tiled=True)  58.2 us
    all_to_all x3, starting transfers between devices, swap(): return lax.all_to_all(x, axis, split_axis=0, concat_axis=0, tiled=True)  22.1 us
    pallas_call x1, Pallas kernels, main_call(): pl.pallas_call(functools.partial(main_kernel, chunk), out_shape=(shape((r...  18.9 us
    unnamed x35, local copies, waits for them, and re-layouts  9.76 us
  transfers between devices with their start and end apart: 4, of which 3 were waited for; matrix products, arithmetic and copies ran while one was open for 1% of the time, Pallas kernels for 2%

profile of v2, /device:TPU:32, one launch (start us, length us, event | category | flops | bytes accessed | tf_op | source)
XLA Modules:
  0.0 198.4 jit_solution(16636011162932523915)
XLA Ops:
  7.2 1.3 reshape.51
  8.4 11.4 %all-to-all-start = ((s32[32,1,16]{2,1,0:T(1,128)}), s32[32,1,16]{2,1,0:T(1,128)S(1)}, u32[]{:S(2)}, u32[]{:S(2)}) async-start(s32[32,1,16]{2,1,0:T(1,128)} %reshape.51), calls=%async_computation | async-start | bytes 32768 | tf_op jit(solution)/shard_map/all_to_all | solution.py:538
  19.8 0.7 compare_bitcast_fusion
  20.5 1.2 copy.31
  21.7 0.2 copy.32
  21.9 6.4 %all-to-all-done = s32[32,1,16]{2,1,0:T(1,128)S(1)} async-done(((s32[32,1,16]{2,1,0:T(1,128)}), s32[32,1,16]{2,1,0:T(1,128)S(1)}, u32[]{:S(2)}, u32[]{:S(2)}) %all-to-all-start) | async-done | bytes 2080 | tf_op jit(solution)/shard_map/all_to_all | solution.py:538
  28.4 0.1 fusion.3
  28.5 1.7 shard_map.214
  30.2 0.0 copy-start.2
  30.2 0.0 copy-start.6
  30.3 0.0 copy-start.7
  30.3 0.0 copy-start.12
  30.3 0.0 copy-start.13
  30.3 0.0 copy-start.14
  30.3 0.0 copy-start.15
  30.3 0.0 copy-start.16
  30.3 5.8 %all-to-all-start.1 = ((bf16[32,64,384]{2,1,0:T(8,128)(2,1)}), bf16[32,64,384]{2,1,0:T(8,128)(2,1)}, u32[]{:S(2)}, u32[]{:S(2)}) async-start(bf16[32,64,384]{2,1,0:T(8,128)(2,1)} %shard_map.214), calls=%async_computation.1 | async-start | bytes 3145728 | tf_op jit(solution)/shard_map/all_to_all | solution.py:538
  36.2 0.0 all-gather.2.cloned.1.call-start
  36.2 0.0 copy-done.2
  36.2 0.0 copy-done.6
  36.2 0.0 copy-done.7
  36.2 0.0 copy-done.12
  36.3 0.0 copy-start.3
  36.3 1.0 copy-done.3
  37.3 0.9 copy-done.8
  38.1 0.9 copy-done.9
  39.0 0.9 copy-done.10
  39.9 0.9 copy-done.11
  40.8 0.7 shard_map.215
  41.5 0.0 copy-start
  41.5 1.1 copy-done
  42.7 0.7 copy-done.4
  43.4 30.9 %all-to-all-done.1.rec_hbm = bf16[32,64,384]{2,1,0:T(8,128)(2,1)} async-done(((bf16[32,64,384]{2,1,0:T(8,128)(2,1)}), bf16[32,64,384]{2,1,0:T(8,128)(2,1)}, u32[]{:S(2)}, u32[]{:S(2)}) %all-to-all-start.1) | async-done | bytes 1572896 | tf_op jit(solution)/shard_map/all_to_all | solution.py:538
  74.2 0.9 copy-done.5
  75.2 18.9 %shard_map.216 = (bf16[128,384]{1,0:T(8,128)(2,1)}, bf16[128,384]{1,0:T(8,128)(2,1)}, bf16[32,48,128]{2,1,0:T(8,128)(2,1)S(1)}, bf16[32,48,128]{2,1,0:T(8,128)(2...) custom-call(s32[16]{0:T(128)S(1)} %and_select_fusion.owner_ref, ...), custom_call_target="tpu_custom_call" | custom-call | tf_op jit(solution)/shard_map/pallas_call | solution.py:509
  94.1 20.2 %all_to_all.30.parts_ref = bf16[8,512,128]{2,1,0:T(8,128)(2,1)S(1)} all-to-all(bf16[8,512,128]{2,1,0:T(8,128)(2,1)S(1)} %bitcast.18), channel_id=1, replica_groups=mesh['rows'=32,'feat'=8] {'feat'}, dimensions={0} | all-to-all | bytes 2097152 | tf_op jit(solution)/shard_map/all_to_all | solution.py:538
  114.3 0.2 shard_map.217
  114.4 23.0 %all_to_all.31.back_ref.one_ref = bf16[32,64,128]{2,1,0:T(8,128)(2,1)S(1)} all-to-all(bf16[32,64,128]{2,1,0:T(8,128)(2,1)S(1)} %shard_map.217), channel_id=1, replica_groups=mesh['rows'=32,'feat'=8] {'rows'}, dimensions={0} | all-to-all | bytes 1048576 | tf_op jit(solution)/shard_map/all_to_all | solution.py:538
  137.4 0.1 shard_map.218
  137.5 21.8 %all_to_all.32.two_ref.back_ref = bf16[32,64,128]{2,1,0:T(8,128)(2,1)S(1)} all-to-all(bf16[32,64,128]{2,1,0:T(8,128)(2,1)S(1)} %shard_map.218), channel_id=1, replica_groups=mesh['rows'=32,'feat'=8] {'rows'}, dimensions={0} | all-to-all | bytes 1048576 | tf_op jit(solution)/shard_map/all_to_all | solution.py:538
  159.2 0.7 shard_map.220
  159.9 0.0 all-gather.2.cloned.1.call-update
  159.9 4.9 %all-to-all-start.5 = ((bf16[32,96,128]{2,1,0:T(8,128)(2,1)}), bf16[32,96,128]{2,1,0:T(8,128)(2,1)S(1)}, u32[]{:S(2)}, u32[]{:S(2)}) async-start(bf16[32,96,128]{2,1,0:T(8,128)(2,1)} %get-tuple-element.43), calls=%async_computation.5 | async-start | bytes 1572864 | tf_op jit(solution)/shard_map/all_to_all | solution.py:538
  164.8 1.5 shard_map.219.sums_ref
  166.3 20.9 %all-to-all-done.5.three_ref = bf16[32,96,128]{2,1,0:T(8,128)(2,1)S(1)} async-done(((bf16[32,96,128]{2,1,0:T(8,128)(2,1)}), bf16[32,96,128]{2,1,0:T(8,128)(2,1)S(1)}, u32[]{:S(2)}, u32[]{:S(2)}) %all-to-all-start.5) | async-done | bytes 786464 | tf_op jit(solution)/shard_map/all_to_all | solution.py:538
  187.2 1.8 shard_map.221
  189.0 1.2 copy-done.1
  190.2 1.3 shard_map.222
  (15 shorter events, 0.1 us)
Async XLA Ops:
  8.4 19.9 %all-to-all-start = ((s32[32,1,16]{2,1,0:T(1,128)}), s32[32,1,16]{2,1,0:T(1,128)S(1)}, u32[]{:S(2)}, u32[]{:S(2)}) async-start(s32[32,1,16]{2,1,0:T(1,128)} %reshape.51), calls=%async_computation | async-start | bytes 32768 | tf_op jit(solution)/shard_map/all_to_all | solution.py:538
  30.2 6.0 %copy-start.2 = (bf16[192,768]{1,0:T(8,128)(2,1)S(1)}, bf16[192,768]{1,0:T(8,128)(2,1)}, u32[]{:S(2)}) copy-start(bf16[192,768]{1,0:T(8,128)(2,1)} %w_up_ref.1) | copy-start | bytes 884740
  30.2 6.0 %copy-start.6 = (bf16[128,384]{1,0:T(8,128)(2,1)S(1)}, bf16[128,384]{1,0:T(8,128)(2,1)}, u32[]{:S(2)}) copy-start(bf16[128,384]{1,0:T(8,128)(2,1)} %test_ref.1) | copy-start | bytes 294916
  30.3 6.0 %copy-start.7 = (bf16[128,384]{1,0:T(8,128)(2,1)S(1)}, bf16[128,384]{1,0:T(8,128)(2,1)}, u32[]{:S(2)}) copy-start(bf16[128,384]{1,0:T(8,128)(2,1)} %cot_ref.1) | copy-start | bytes 294916
  30.3 6.0 %copy-start.12 = (f32[192]{0:T(256)S(1)}, f32[192]{0:T(256)}, u32[]{:S(2)}) copy-start(f32[192]{0:T(256)} %param.20) | copy-start | bytes 2308
  30.3 6.0 %copy-start.13 = (f32[192]{0:T(256)S(1)}, f32[192]{0:T(256)}, u32[]{:S(2)}) copy-start(f32[192]{0:T(256)} %param.22) | copy-start | bytes 2308
  30.3 6.0 %copy-start.14 = (f32[192]{0:T(256)S(1)}, f32[192]{0:T(256)}, u32[]{:S(2)}) copy-start(f32[192]{0:T(256)} %param.25) | copy-start | bytes 2308
  30.3 6.0 %copy-start.15 = (f32[192]{0:T(256)S(1)}, f32[192]{0:T(256)}, u32[]{:S(2)}) copy-start(f32[192]{0:T(256)} %param.28) | copy-start | bytes 2308
  30.3 13.1 %copy-start.16 = (s32[1,16]{1,0:T(1,128)S(1)}, s32[1,16]{1,0:T(1,128)}, u32[]{:S(2)}) copy-start(s32[1,16]{1,0:T(1,128)} %param.18) | copy-start | bytes 196
  30.3 43.9 %all-to-all-start.1 = ((bf16[32,64,384]{2,1,0:T(8,128)(2,1)}), bf16[32,64,384]{2,1,0:T(8,128)(2,1)}, u32[]{:S(2)}, u32[]{:S(2)}) async-start(bf16[32,64,384]{2,1,0:T(8,128)(2,1)} %shard_map.214), calls=%async_computation.1 | async-start | bytes 3145728 | tf_op jit(solution)/shard_map/all_to_all | solution.py:538
  36.2 152.8 %all-gather.2.cloned.1.call-start = ((), (), s32[]{:S(2)}) async-start(), calls=%async_computation.6 | async-start | bytes 1179648 | tf_op jit(solution)/shard_map/all_gather | solution.py:604
  36.3 1.0 copy-start.3
  37.3 0.9 copy-start.8
  38.1 0.9 copy-start.9
  39.0 0.9 copy-start.10
  39.9 0.9 copy-start.11
  41.5 1.2 copy-start
  42.7 0.7 copy-start.4
  74.2 1.0 copy-start.5
  159.9 27.2 %all-to-all-start.5 = ((bf16[32,96,128]{2,1,0:T(8,128)(2,1)}), bf16[32,96,128]{2,1,0:T(8,128)(2,1)S(1)}, u32[]{:S(2)}, u32[]{:S(2)}) async-start(bf16[32,96,128]{2,1,0:T(8,128)(2,1)} %get-tuple-element.43), calls=%async_computation.5 | async-start | bytes 1572864 | tf_op jit(solution)/shard_map/all_to_all | solution.py:538
  189.0 1.2 copy-start.1
Sparse Core Ops, SparseCore 0:
  160.1 20.1 all-gather.1

commit v3 on v2

--- a/solution.py
+++ b/solution.py
@@ -62,20 +62,19 @@
     lax.fori_loop(0, back_ref.shape[0], body, 0)
 
 
-def sum_kernel(asked_ref, one_ref, two_ref, acc_ref):
-    for part, ref in enumerate((one_ref, two_ref)):
-        mine = acc_ref.at[part]
-        mine[...] = jnp.zeros(mine.shape, f32)
-        add_terms(asked_ref, ref, mine)
-
-
-def last_kernel(asked_ref, sums_ref, three_ref, out_ref, acc_ref):
+def sum_kernel(asked_ref, zero_ref, one_ref, zero_acc, one_acc):
+    for ref, acc in ((zero_ref, zero_acc), (one_ref, one_acc)):
+        acc[...] = jnp.zeros(acc.shape, f32)
+        add_terms(asked_ref, ref, acc)
+
+
+def last_kernel(asked_ref, zero_ref, one_ref, back_ref, out_ref, acc_ref):
     acc_ref[...] = jnp.zeros_like(acc_ref)
-    add_terms(asked_ref, three_ref, acc_ref)
-    one, two, three = sums_ref[0], sums_ref[1], acc_ref[...]
-    out_ref[:, :, 0:128] = jnp.concatenate([one, two[:, :16]], axis=1).astype(bf16)
-    out_ref[:, :, 128:256] = jnp.concatenate([two[:, 16:], three[:, :32]], axis=1).astype(bf16)
-    out_ref[:, :, 256:384] = three[:, 32:].astype(bf16)
+    add_terms(asked_ref, back_ref, acc_ref)
+    zero, one, two = zero_ref[...], one_ref[...], acc_ref[...]
+    out_ref[:, :, 0:128] = zero[:, :BLK].astype(bf16)
+    out_ref[:, :, 128:256] = jnp.concatenate([zero[:, BLK:], one[:, :32]], axis=1).astype(bf16)
+    out_ref[:, :, 256:384] = jnp.concatenate([one[:, 32:], two], axis=1).astype(bf16)
 
 
 def mean_e(x):
@@ -125,6 +124,16 @@
 def rms_back(pre, scale, gain, dy):
     u = dy * gain
     return scale * (u - pre * (scale * scale) * mean_e(pre * u))
+
+
+def feature_lanes(f):
+    return slice(128 * f, 128 * f + W)
+
+
+def side_by_side(first, second):
+    return jnp.concatenate(
+        [first[:, :128], first[:, 128:] + second[:, :128], second[:, 128:]], axis=1
+    )
 
 
 def widen(x, cols):
@@ -161,7 +170,7 @@
     lane = lax.broadcasted_iota(jnp.int32, (E, W), 1)
     place = jnp.where(row == lane, 1.0, 0.0).astype(bf16)
     first = jnp.where((row == 0) & (lane == E), 1.0, 0.0).astype(bf16)
-    nothing = jnp.zeros((E, W), bf16)
+    nothing = jnp.zeros((W - E, W), bf16)
     weights = (
         widen(w_query_ref[...], W),
         widen(w_key_ref[...], W) + first,
@@ -170,8 +179,9 @@
     )
     for i, weight in enumerate(weights):
         for f in range(2):
-            projections_ref[i, f, f * E : (f + 1) * E, :] = weight
-            projections_ref[i, f, (1 - f) * E : (2 - f) * E, :] = nothing
+            skip = f * (W - E)
+            projections_ref[i, f, skip : skip + E, :] = weight
+            projections_ref[i, f, (1 - f) * E : (1 - f) * E + W - E, :] = nothing
     ffn_ref[:, :FFH] = heighten(w_up_ref[...], W)
     ffn_ref[:, FFH : 2 * FFH] = heighten(w_down_t_ref[...], W)
     ffn_ref[:, 2 * FFH :] = heighten(widen(w_out_ref[...], W), W)
@@ -182,9 +192,10 @@
     q_gain = gains_ref[0:1, :]
     for f in range(2):
         here = slice(f * rows, (f + 1) * rows)
-        cells_ref[0, here, :] = dot_nn(test, projections_ref[3, f])
-        cells_ref[1, here, :] = dot_nn(cot, projections_ref[3, f])
-        pre = dot_nn(test, projections_ref[0, f])
+        lanes = feature_lanes(f)
+        cells_ref[0, here, :] = dot_nn(test[:, lanes], projections_ref[3, f])
+        cells_ref[1, here, :] = dot_nn(cot[:, lanes], projections_ref[3, f])
+        pre = dot_nn(test[:, lanes], projections_ref[0, f])
         norm = pre * lax.rsqrt(mean_e(pre * pre) + 1e-06) * q_gain
         norm = norm.astype(bf16).astype(f32)
         q_pre_ref[here, :] = pre
@@ -195,6 +206,7 @@
 def main_kernel(
     chunk,
     owner_ref,
+    core_ref,
     rec_hbm,
     projections_hbm,
     ffn_hbm,
@@ -205,10 +217,11 @@
     q_rows_hbm,
     out_ref,
     grad_test_ref,
+    zero_ref,
     one_ref,
     two_ref,
-    three_ref,
-    grads_ref,
+    keep_hbm,
+    give_hbm,
     projections_ref,
     ffn_ref,
     gains_ref,
@@ -223,6 +236,7 @@
     e_s,
     p_s,
     d_s,
+    grads_ref,
     rec_sem,
     sems,
 ):
@@ -257,9 +271,9 @@
     ]
     for copy in copies:
         copy.start()
+    zero_ref[...] = jnp.zeros_like(zero_ref)
     one_ref[...] = jnp.zeros_like(one_ref)
     two_ref[...] = jnp.zeros_like(two_ref)
-    three_ref[...] = jnp.zeros_like(three_ref)
     pltpu.make_async_copy(cells_s, cells_s, rec_sem).wait()
     for copy in copies:
         copy.wait()
@@ -271,10 +285,9 @@
 
     def scores(c, totals):
         start = pl.ds(pl.multiple_of(c * chunk, chunk), chunk)
-        cells = cells_s[start, :]
         result = []
         for f in range(feats):
-            pre = dot_nn(cells, projections_ref[1, f])
+            pre = dot_nn(cells_s[start, feature_lanes(f)], projections_ref[1, f])
             lane = lax.broadcasted_iota(jnp.int32, pre.shape, 1)
             body = jnp.where(lane < E, pre, 0.0)
             scale = lax.rsqrt(mean_e(body * body) + 1e-06)
@@ -283,7 +296,7 @@
             norm = (norm + bias).astype(bf16)
             kp_s[f, start, :] = body
             k_s[f, start, :] = norm
-            v_s[f, start, :] = dot_nn(cells, projections_ref[2, f]).astype(bf16)
+            v_s[f, start, :] = dot_nn(cells_s[start, feature_lanes(f)], projections_ref[2, f]).astype(bf16)
             e = jnp.exp2(dot_nn(norm, q_tall_ref[f]) * (TEMPER * LOG2E))
             e_s[f, start, :] = e
             result.append(totals[f] + jnp.sum(e, axis=0, keepdims=True))
@@ -292,6 +305,7 @@
     zero = jnp.zeros((1, H * rows), f32)
     totals = lax.fori_loop(0, chunks, scores, (zero,) * feats)
     inverse = [1.0 / total for total in totals]
+    inverse_tempered = [TEMPER / total for total in totals]
 
     def attend(c, mixed):
         start = pl.ds(pl.multiple_of(c * chunk, chunk), chunk)
@@ -299,10 +313,10 @@
         for f in range(feats):
             p = (e_s[f, start, :] * inverse[f]).astype(bf16)
             p_s[f, start, :] = p
-            result.append(mixed[f] + dot_tn(v_s[f, start, :], p))
+            result.append(mixed[f] + dot_tn(v_s[f, start, :E], p))
         return tuple(result)
 
-    mixed = lax.fori_loop(0, chunks, attend, (jnp.zeros((W, H * rows), f32),) * feats)
+    mixed = lax.fori_loop(0, chunks, attend, (jnp.zeros((E, H * rows), f32),) * feats)
     attended_t = [head_blocks(m) for m in mixed]
 
     attended = jnp.concatenate([a.T for a in attended_t], axis=0).astype(bf16)
@@ -322,8 +336,8 @@
     inner_two = normed_one.astype(f32) + dot_nt(hidden, w_down_t)
     hat_two, scale_two = layer_norm(inner_two, lane_in)
     out = (hat_two * gain_two).astype(bf16)
-    out_ref[...] = (
-        dot_nt(out[:rows], projections_ref[3, 0]) + dot_nt(out[rows:], projections_ref[3, 1])
+    out_ref[...] = side_by_side(
+        dot_nt(out[:rows], projections_ref[3, 0]), dot_nt(out[rows:], projections_ref[3, 1])
     ).astype(bf16)
     d_two = layer_norm_back(hat_two, scale_two, gain_two, cells_ref[1])
     d_two = jnp.where(lane_in, d_two, 0.0)
@@ -358,12 +372,12 @@
     def back(c, d_queries):
         start = pl.ds(pl.multiple_of(c * chunk, chunk), chunk)
         result = []
-        d_cells = jnp.zeros((chunk, feats * E), f32)
+        d_cells = []
         for f in range(feats):
             grad_w = dot_nn(v_s[f, start, :], da_t[f])
-            probs = e_s[f, start, :] * inverse[f]
-            d_scores = (probs * (grad_w - dots[f]) * TEMPER).astype(bf16)
-            result.append(d_queries[f] + dot_tn(k_s[f, start, :], d_scores))
+            probs = e_s[f, start, :] * inverse_tempered[f]
+            d_scores = (probs * (grad_w - dots[f])).astype(bf16)
+            result.append(d_queries[f] + dot_tn(k_s[f, start, :E], d_scores))
             d_key = dot_nn(d_scores, q_rows_ref[f])
             d_value = dot_nn(p_s[f, start, :], da_rows[f]).astype(bf16)
             body = kp_s[f, start, :]
@@ -371,22 +385,23 @@
             d_kpre = rms_back(body, scale, k_gain, d_key).astype(bf16)
             d_s[start, 2 * f * W : (2 * f + 1) * W] = d_kpre
             d_s[start, (2 * f + 1) * W : (2 * f + 2) * W] = d_value
-            d_cells = d_cells + dot_nt(d_kpre, projections_ref[1, f])
-            d_cells = d_cells + dot_nt(d_value, projections_ref[2, f])
-        d_cells = d_cells.astype(bf16)
+            d_cells.append(
+                dot_nt(d_kpre, projections_ref[1, f]) + dot_nt(d_value, projections_ref[2, f])
+            )
+        d_cells = side_by_side(*d_cells).astype(bf16)
         for b in range(chunk // BLK):
             owner = owner_ref[c * (chunk // BLK) + b]
             block = d_cells[b * BLK : (b + 1) * BLK]
-            one_ref[owner] = block[:48, :128]
-            two_ref[owner, :16] = block[48:, :128]
-            two_ref[owner, 16:] = block[:32, 128:256]
-            three_ref[owner, :32] = block[32:, 128:256]
-            three_ref[owner, 32:] = block[:, 256:]
+            zero_ref[owner, :BLK] = block[:, :128]
+            zero_ref[owner, BLK:] = block[:32, 128:256]
+            one_ref[owner, :32] = block[32:, 128:256]
+            one_ref[owner, 32:] = block[:16, 256:]
+            two_ref[owner] = block[16:, 256:]
         return tuple(result)
 
-    d_queries = lax.fori_loop(0, chunks, back, (jnp.zeros((W, H * rows), f32),) * feats)
-
-    d_test = jnp.zeros((rows, feats * E), f32)
+    d_queries = lax.fori_loop(0, chunks, back, (jnp.zeros((E, H * rows), f32),) * feats)
+
+    d_test = []
     g_query = jnp.zeros((W, W), f32)
     placed = []
     for f in range(feats):
@@ -396,13 +411,29 @@
         scale = lax.rsqrt(mean_e(pre * pre) + 1e-06)
         d_qpre = rms_back(pre, scale, q_gain, d_query).astype(bf16)
         g_query = g_query + dot_tn(cells_ref[0, here, :].astype(bf16), d_qpre)
-        d_test = d_test + dot_nt(d_qpre, projections_ref[0, f])
+        d_test.append(dot_nt(d_qpre, projections_ref[0, f]))
         placed.append(d_one[here, :E])
-    grad_test_ref[...] = (d_test + jnp.concatenate(placed, axis=1)).astype(bf16)
+    grad_test_ref[...] = (side_by_side(*d_test) + jnp.concatenate(placed, axis=1)).astype(bf16)
     put_grads(grads_ref, 0, g_query[:E])
-    kv = dot_tn(cells_s[...], d_s[...])
-    put_grads(grads_ref, 2, kv[:E, : 2 * W] + kv[E:, 2 * W :])
+    kv = jnp.zeros((E, 2 * W), f32)
+    for f in range(feats):
+        both = dot_tn(cells_s[:, feature_lanes(f)], d_s[:, 2 * f * W : 2 * (f + 1) * W])
+        kv = kv + both[f * (W - E) : f * (W - E) + E]
+    put_grads(grads_ref, 2, kv)
     grads_ref[20 * E :, :] = jnp.zeros((GRAD_ROWS - 20 * E, 128), bf16)
+    core = core_ref[0]
+    halves = [
+        pltpu.make_async_copy(
+            grads_ref.at[pl.ds(pl.multiple_of(half * (GRAD_ROWS // 2), 128), GRAD_ROWS // 2), :],
+            target,
+            sems.at[i],
+        )
+        for i, (half, target) in enumerate(((core, keep_hbm), (1 - core, give_hbm)))
+    ]
+    for copy in halves:
+        copy.start()
+    for copy in halves:
+        copy.wait()
 
 
 def put_grads(grads_ref, first, value):
@@ -417,12 +448,19 @@
     )
 
 
-def ride_kernel(parts_ref, one_ref, out_ref):
-    total = jnp.sum(parts_ref[...].astype(f32), axis=0).astype(bf16)
-    out_ref[:, : one_ref.shape[1], :] = one_ref[...]
-    out_ref[:, one_ref.shape[1] :, :] = total.reshape(
-        out_ref.shape[0], out_ref.shape[1] - one_ref.shape[1], 128
-    )
+def halve_kernel(bit_ref, keep_ref, got_ref, next_keep_ref, next_give_ref):
+    half = next_keep_ref.shape[0]
+    bit = bit_ref[0]
+    for part, ref in ((bit, next_keep_ref), (1 - bit, next_give_ref)):
+        rows = pl.ds(pl.multiple_of(part * half, 128), half)
+        ref[...] = (keep_ref[rows, :].astype(f32) + got_ref[rows, :].astype(f32)).astype(bf16)
+
+
+def ride_kernel(keep_ref, got_ref, one_ref, out_ref):
+    cut = one_ref.shape[1]
+    total = (keep_ref[...].astype(f32) + got_ref[...].astype(f32)).astype(bf16)
+    out_ref[:, :cut, :] = one_ref[...]
+    out_ref[:, cut:, :] = total.reshape(out_ref.shape[0], out_ref.shape[1] - cut, 128)
 
 
 def ride_back_kernel(back_ref, two_ref, out_ref):
@@ -432,20 +470,26 @@
     out_ref[:, cut:, :] = jnp.broadcast_to(total[None], out_ref[:, cut:, :].shape)
 
 
-def share_kernel(back_ref, three_in, share_ref, three_out, sem):
-    pieces = share_ref.shape[1]
-    copy = pltpu.make_async_copy(
-        back_ref.at[:, pl.ds(back_ref.shape[1] - pieces, pieces), :], share_ref, sem
-    )
-    copy.start()
-    copy.wait()
-
-
-def unpack_kernel(in_ref, query_ref, key_ref, value_ref, w_out_ref, up_ref, down_t_ref):
+def share_kernel(back_ref, out_ref):
+    pieces = out_ref.shape[1] // back_ref.shape[0]
+    share = back_ref[:, back_ref.shape[1] - pieces :, :].reshape(out_ref.shape[1], 128)
+    out_ref[...] = jnp.broadcast_to(share[None], out_ref.shape)
+
+
+def unpack_kernel(
+    core_ref, mine_ref, got_ref, query_ref, key_ref, value_ref, w_out_ref, up_ref, down_t_ref, all_ref
+):
+    chips, share, _ = mine_ref.shape
+    core = core_ref[0]
+    for half, ref in ((core, mine_ref), (1 - core, got_ref)):
+        for chip in range(chips):
+            place = (chip % 2) * 2 + chip // 2
+            start = pl.multiple_of(half * (chips * share) + place * share, 128)
+            all_ref[pl.ds(start, share), :] = ref[chip]
     for i, ref in enumerate((query_ref, key_ref, value_ref, w_out_ref)):
-        ref[...] = take_grads(in_ref, 2 * i, 2)[:, :E]
-    up_ref[...] = take_grads(in_ref, 8, 6)
-    down_t_ref[...] = take_grads(in_ref, 14, 6)
+        ref[...] = take_grads(all_ref, 2 * i, 2)[:, :E]
+    up_ref[...] = take_grads(all_ref, 8, 6)
+    down_t_ref[...] = take_grads(all_ref, 14, 6)
 
 
 def vmem_specs(n):
@@ -464,14 +508,15 @@
     return jax.ShapeDtypeStruct(dims, dtype)
 
 
-def small_call(kernel, out_shape, *args):
+def small_call(kernel, out_shape, *args, scalars=(), scratch=()):
     return pl.pallas_call(
         kernel,
         out_shape=out_shape,
-        in_specs=vmem_specs(len(args)),
+        in_specs=[SMEM_SPEC] * len(scalars) + vmem_specs(len(args)),
         out_specs=jax.tree.map(lambda _: vmem_specs(1)[0], out_shape),
+        scratch_shapes=scratch,
         compiler_params=PARAMS,
-    )(*args)
+    )(*scalars, *args)
 
 
 def prepare(test_cells, cotangent, weights):
@@ -481,7 +526,7 @@
     return small_call(
         prepare_kernel,
         (
-            shape((4, 2, wide, W)),
+            shape((4, 2, W, W)),
             shape((W, 2 * FFH + W)),
             shape((4, W), f32),
             shape((2, 2 * rows, W), f32),
@@ -501,7 +546,7 @@
     )
 
 
-def main_call(owner_of, rec, prepared, rows, chunk):
+def main_call(owner_of, core, rec, prepared, rows, chunk):
     count = owner_of.shape[0]
     keys = count * BLK
     owners, _, wide = rec.shape
@@ -511,13 +556,14 @@
         out_shape=(
             shape((rows, wide)),
             shape((rows, wide)),
+            shape((owners, 96, 128)),
             shape((owners, 48, 128)),
             shape((owners, 48, 128)),
-            shape((owners, 96, 128)),
-            shape((GRAD_ROWS, 128)),
+            shape((GRAD_ROWS // 2, 128)),
+            shape((GRAD_ROWS // 2, 128)),
         ),
-        in_specs=[SMEM_SPEC] + [ANY_SPEC] * (1 + len(prepared)),
-        out_specs=tuple(vmem_specs(6)),
+        in_specs=[SMEM_SPEC] * 2 + [ANY_SPEC] * (1 + len(prepared)),
+        out_specs=tuple(vmem_specs(5)) + (ANY_SPEC,) * 2,
         scratch_shapes=[pltpu.VMEM(x.shape, x.dtype) for x in prepared]
         + [
             pltpu.VMEM((keys, wide), bf16),
@@ -527,19 +573,16 @@
             pltpu.VMEM((2, keys, ht), f32),
             pltpu.VMEM((2, keys, ht), bf16),
             pltpu.VMEM((keys, 4 * W), bf16),
+            pltpu.VMEM((GRAD_ROWS, 128), bf16),
             pltpu.SemaphoreType.DMA,
             pltpu.SemaphoreType.DMA((len(prepared),)),
         ],
         compiler_params=PARAMS,
-    )(owner_of, rec, *prepared)
+    )(owner_of, core, rec, *prepared)
 
 
 def swap(x, axis):
     return lax.all_to_all(x, axis, split_axis=0, concat_axis=0, tiled=True)
-
-
-def unpack_shapes():
-    return (shape((E, E), f32),) * 4 + (shape((E, FFH), f32),) * 2
 
 
 def on_device(
@@ -584,42 +627,68 @@
         cotangent,
         (w_query, q_gain, w_key, k_gain, w_value, w_out, gain_one, w_up, w_down, gain_two),
     )
-    out_cells, grad_test, one, two, three, grads = main_call(owner_of, rec, prepared, rows, 256)
-
-    share = GRAD_ROWS // groups
-    piece = share // owners
-    parts = swap(grads.reshape(groups, share, 128), "feat")
+    feat = lax.axis_index("feat")
+    core, low, high = ((feat // bit % 2).reshape(1) for bit in (1, 2, 4))
+    out_cells, grad_test, zero, one, two, keep, give = main_call(
+        owner_of, core, rec, prepared, rows, 1024
+    )
+
+    back_zero = swap(zero, "rows")
+    got = flip(give, 1)
+    half = keep.shape[0] // 2
+    keep, give = small_call(halve_kernel, (shape((half, 128)),) * 2, keep, got, scalars=(low,))
+    got = flip(give, 2)
+    half = half // 2
+    keep, give = small_call(halve_kernel, (shape((half, 128)),) * 2, keep, got, scalars=(high,))
+    got = flip(give, 4)
+    piece = half // owners
     riding = shape((owners, one.shape[1] + piece, 128))
-    back_one = swap(small_call(ride_kernel, riding, parts, one), "rows")
+    back_one = swap(small_call(ride_kernel, riding, keep, got, one), "rows")
     back_two = swap(small_call(ride_back_kernel, riding, back_one, two), "rows")
-    over_all, three = pl.pallas_call(
-        share_kernel,
-        out_shape=(shape((owners, piece, 128)), shape(three.shape)),
-        in_specs=[ANY_SPEC] * 2,
-        out_specs=(ANY_SPEC,) * 2,
-        scratch_shapes=[pltpu.SemaphoreType.DMA],
-        input_output_aliases={1: 1},
-        compiler_params=PARAMS,
-    )(back_two, three)
-    total = lax.all_gather(over_all.reshape(share, 128), "feat", tiled=True)
-    back_three = swap(three, "rows")
-    sums = pl.pallas_call(
+    chips = groups // 2
+    copies = small_call(share_kernel, shape((chips, half, 128)), back_two)
+    mine = lax.all_to_all(
+        copies,
+        "feat",
+        split_axis=0,
+        concat_axis=0,
+        tiled=True,
+        axis_index_groups=[[2 * chip + c for chip in range(chips)] for c in range(2)],
+    )
+    others = flip(mine, 1)
+    sums = small_call(
         sum_kernel,
-        out_shape=shape((2, blocks_own, one.shape[1], 128), f32),
-        in_specs=[SMEM_SPEC] + vmem_specs(2),
-        out_specs=vmem_specs(1)[0],
-        compiler_params=PARAMS,
-    )(asked, back_one, back_two)
-    grad_train = pl.pallas_call(
+        tuple(shape((blocks_own, x.shape[1], 128), f32) for x in (zero, one)),
+        back_zero,
+        back_one,
+        scalars=(asked,),
+    )
+    grad_train = small_call(
         last_kernel,
-        out_shape=shape((blocks_own, BLK, wide)),
-        in_specs=[SMEM_SPEC] + vmem_specs(2),
-        out_specs=vmem_specs(1)[0],
-        scratch_shapes=[pltpu.VMEM((blocks_own, three.shape[1], 128), f32)],
-        compiler_params=PARAMS,
-    )(asked, sums, back_three).reshape(blocks_own * BLK, wide)
-    *others, g_down_t = small_call(unpack_kernel, unpack_shapes(), total)
-    return (out_cells, grad_test, grad_train, *others, g_down_t.T)
+        shape((blocks_own, BLK, wide)),
+        *sums,
+        back_two,
+        scalars=(asked,),
+        scratch=[pltpu.VMEM((blocks_own, two.shape[1], 128), f32)],
+    ).reshape(blocks_own * BLK, wide)
+    *weights, g_down_t = unpack(core, mine, others)
+    return (out_cells, grad_test, grad_train, *weights, g_down_t.T)
+
+
+def flip(x, bit):
+    count = lax.axis_size("feat")
+    return lax.ppermute(x, "feat", [(i, i ^ bit) for i in range(count)])
+
+
+def unpack(core, mine, others):
+    return small_call(
+        unpack_kernel,
+        (shape((E, E), f32),) * 4 + (shape((E, FFH), f32),) * 2,
+        mine,
+        others,
+        scalars=(core,),
+        scratch=[pltpu.VMEM((GRAD_ROWS, 128), bf16)],
+    )
 
 
 def solution(mesh):

time: 199 us -> 184 us (0.925)
  between operations: 14.3 us -> 0.92 us
  blocking collectives: 64.9 us -> 53.8 us
  waiting for transfers between devices: 58.2 us -> 68.3 us
  Pallas kernels: 26.8 us -> 21.1 us
  starting transfers between devices: 22.1 us -> 26.8 us
    all_to_all x3 -> x2, blocking collectives: 64.9 us -> 41.6 us  [swap(): return lax.all_to_all(x, axis, split_axis=0, concat_axis=0, tiled=True)]
    ppermute x0 -> x4, waiting for transfers between devices: none -> 12.4 us  [flip(): return lax.ppermute(x, 'feat', [(i, i ^ bit) for i in range(count)])]
    all_to_all x0 -> x1, blocking collectives: none -> 12.2 us  [on_device(): lax.all_to_all(copies, 'feat', split_axis=0, concat_axis=0, tiled=True, a...]
    pallas_call x1, Pallas kernels: 18.9 us -> 13.7 us  [main_call(): pl.pallas_call(functools.partial(main_kernel, chunk), out_shape=(shape((r...]
    ppermute x0 -> x4, starting transfers between devices: none -> 4.79 us  [flip(): return lax.ppermute(x, 'feat', [(i, i ^ bit) for i in range(count)])]
    all_to_all x3, waiting for transfers between devices: 58.2 us -> 55.9 us  [swap(): return lax.all_to_all(x, axis, split_axis=0, concat_axis=0, tiled=True)]
    pallas_call x7 -> x9, Pallas kernels: 6.17 us -> 5.66 us  [small_call(): pl.pallas_call(kernel, out_shape=out_shape, in_specs=[SMEM_SPEC] * len(sc...]
    unnamed x35 -> x41, local copies, waits for them, and re-layouts: 9.76 us -> 9.85 us
  transfers between devices with their start and end apart: 4 -> 7, of which waited for: 3 -> 6; matrix products, arithmetic and copies ran while one was open for 1% -> 1% of each run, Pallas kernels for 2% -> 2%
where the time goes in v3:
time: 184 us; the launch traced here: 183 us
  waiting for transfers between devices  68.3 us (37%)
  blocking collectives  53.8 us (29%)
  starting transfers between devices  26.8 us (15%)
  Pallas kernels  21.1 us (11%)
  local copies, waits for them, and re-layouts  11.3 us (6%)
    all_to_all x3, waiting for transfers between devices, swap(): return lax.all_to_all(x, axis, split_axis=0, concat_axis=0, tiled=True)  55.9 us
    all_to_all x2, blocking collectives, swap(): return lax.all_to_all(x, axis, split_axis=0, concat_axis=0, tiled=True)  41.6 us
    all_to_all x3, starting transfers between devices, swap(): return lax.all_to_all(x, axis, split_axis=0, concat_axis=0, tiled=True)  22 us
    pallas_call x1, Pallas kernels, main_call(): pl.pallas_call(functools.partial(main_kernel, chunk), out_shape=(shape((r...  13.7 us
    ppermute x4, waiting for transfers between devices, flip(): return lax.ppermute(x, 'feat', [(i, i ^ bit) for i in range(count)])  12.4 us
    all_to_all x1, blocking collectives, on_device(): lax.all_to_all(copies, 'feat', split_axis=0, concat_axis=0, tiled=True, a...  12.2 us
    unnamed x41, local copies, waits for them, and re-layouts  9.85 us
    pallas_call x9, Pallas kernels, small_call(): pl.pallas_call(kernel, out_shape=out_shape, in_specs=[SMEM_SPEC] * len(sc...  5.66 us
  transfers between devices with their start and end apart: 7, of which 6 were waited for; matrix products, arithmetic and copies ran while one was open for 1% of the time, Pallas kernels for 2%

profile of v3, /device:TPU:32, one launch (start us, length us, event | category | flops | bytes accessed | tf_op | source)
XLA Modules:
  0.0 183.1 jit_solution(15908870511385235551)
XLA Ops:
  0.6 1.3 reshape.55
  1.9 11.4 %all-to-all-start = ((s32[32,1,16]{2,1,0:T(1,128)}), s32[32,1,16]{2,1,0:T(1,128)S(1)}, u32[]{:S(2)}, u32[]{:S(2)}) async-start(s32[32,1,16]{2,1,0:T(1,128)} %reshape.55), calls=%async_computation | async-start | bytes 32768 | tf_op jit(solution)/shard_map/all_to_all | solution.py:585
  13.3 0.7 compare_bitcast_fusion
  14.0 1.2 copy.30
  15.2 0.2 copy.31
  15.4 6.4 %all-to-all-done = s32[32,1,16]{2,1,0:T(1,128)S(1)} async-done(((s32[32,1,16]{2,1,0:T(1,128)}), s32[32,1,16]{2,1,0:T(1,128)S(1)}, u32[]{:S(2)}, u32[]{:S(2)}) %all-to-all-start) | async-done | bytes 2080 | tf_op jit(solution)/shard_map/all_to_all | solution.py:585
  21.8 0.1 fusion.3
  22.0 1.7 shard_map.214
  23.7 0.0 copy-start.5
  23.7 0.0 copy-start.9
  23.7 0.0 copy-start.10
  23.7 0.0 copy-start.15
  23.7 0.0 copy-start.16
  23.7 0.0 copy-start.19
  23.8 5.8 %all-to-all-start.1 = ((bf16[32,64,384]{2,1,0:T(8,128)(2,1)}), bf16[32,64,384]{2,1,0:T(8,128)(2,1)}, u32[]{:S(2)}, u32[]{:S(2)}) async-start(bf16[32,64,384]{2,1,0:T(8,128)(2,1)} %shard_map.214), calls=%async_computation.1 | async-start | bytes 3145728 | tf_op jit(solution)/shard_map/all_to_all | solution.py:585
  29.7 0.0 copy-start.6
  29.7 1.0 copy-done.6
  30.7 0.9 copy-done.11
  31.5 0.9 copy-done.12
  32.4 0.9 copy-done.13
  33.3 0.9 copy-done.14
  34.2 0.6 shard_map.215
  34.8 1.0 copy-done
  35.8 0.7 copy-done.7
  36.5 31.2 %all-to-all-done.1.rec_hbm = bf16[32,64,384]{2,1,0:T(8,128)(2,1)} async-done(((bf16[32,64,384]{2,1,0:T(8,128)(2,1)}), bf16[32,64,384]{2,1,0:T(8,128)(2,1)}, u32[]{:S(2)}, u32[]{:S(2)}) %all-to-all-start.1) | async-done | bytes 1572896 | tf_op jit(solution)/shard_map/all_to_all | solution.py:585
  67.7 0.9 copy-done.8
  68.6 13.7 %shard_map.216 = (bf16[128,384]{1,0:T(8,128)(2,1)}, bf16[128,384]{1,0:T(8,128)(2,1)}, bf16[32,96,128]{2,1,0:T(8,128)(2,1)}, bf16[32,48,128]{2,1,0:T(8,128)(2,1)S...) custom-call(s32[16]{0:T(128)S(1)} %and_select_fusion.owner_ref, ...), custom_call_target="tpu_custom_call" | custom-call | tf_op jit(solution)/shard_map/pallas_call | solution.py:554
  82.4 0.7 copy-done.1
  83.1 0.7 copy-done.3
  83.9 2.1 %collective-permute-done.got_ref = bf16[2048,128]{1,0:T(8,128)(2,1)S(1)} collective-permute-done((bf16[2048,128]{1,0:T(8,128)(2,1)}, bf16[2048,128]{1,0:T(8,128)(2,1)S(1)}, u32[]{:S(2)}, u32[]{:S(2)}) %collective-permute-start) | collective-permute-done | bytes 524320 | tf_op jit(solution)/shard_map/ppermute | solution.py:680
  86.0 0.1 shard_map.217
  86.1 1.6 collective-permute-start.1
  87.7 6.9 %collective-permute-done.1.got_ref = bf16[1024,128]{1,0:T(8,128)(2,1)S(1)} collective-permute-done((bf16[1024,128]{1,0:T(8,128)(2,1)S(1)}, bf16[1024,128]{1,0:T(8,128)(2,1)S(1)}, u32[]{:S(2)}, u32[]{:S(2)}) %collective-permute-start.1) | collective-permute-done | bytes 262176 | tf_op jit(solution)/shard_map/ppermute | solution.py:680
  94.6 0.1 shard_map.218
  94.6 3.1 %collective-permute-start.2 = (bf16[512,128]{1,0:T(8,128)(2,1)S(1)}, bf16[512,128]{1,0:T(8,128)(2,1)S(1)}, u32[]{:S(2)}, u32[]{:S(2)}) collective-permute-start(bf16[512,128]{1,0:T(8,128)(2,1)S(1)} %get-tuple-element.50), channel_id=1, source_target_pairs={{0,4},{1,5},{2,6},{3,7},{4,0},{5,1},{6,2},{7,3},{8,12},{9,13},{10,... | collective-permute-start | bytes 393224 | tf_op jit(solution)/shard_map/ppermute | solution.py:680
  97.7 3.4 %collective-permute-done.2.got_ref = bf16[512,128]{1,0:T(8,128)(2,1)S(1)} collective-permute-done((bf16[512,128]{1,0:T(8,128)(2,1)S(1)}, bf16[512,128]{1,0:T(8,128)(2,1)S(1)}, u32[]{:S(2)}, u32[]{:S(2)}) %collective-permute-start.2) | collective-permute-done | bytes 131104 | tf_op jit(solution)/shard_map/ppermute | solution.py:680
  101.2 0.1 shard_map.219
  101.3 21.7 %all_to_all.30.one_ref.back_ref = bf16[32,64,128]{2,1,0:T(8,128)(2,1)S(1)} all-to-all(bf16[32,64,128]{2,1,0:T(8,128)(2,1)S(1)} %shard_map.219), channel_id=1, replica_groups=mesh['rows'=32,'feat'=8] {'rows'}, dimensions={0} | all-to-all | bytes 1048576 | tf_op jit(solution)/shard_map/all_to_all | solution.py:585
  122.9 0.1 shard_map.221
  123.0 19.9 %all_to_all.31.back_ref = bf16[32,64,128]{2,1,0:T(8,128)(2,1)S(1)} all-to-all(bf16[32,64,128]{2,1,0:T(8,128)(2,1)S(1)} %shard_map.221), channel_id=1, replica_groups=mesh['rows'=32,'feat'=8] {'rows'}, dimensions={0} | all-to-all | bytes 1048576 | tf_op jit(solution)/shard_map/all_to_all | solution.py:585
  142.9 0.1 shard_map.223
  143.0 12.2 %all_to_all.32.mine_ref = bf16[4,512,128]{2,1,0:T(8,128)(2,1)S(1)} all-to-all(bf16[4,512,128]{2,1,0:T(8,128)(2,1)S(1)} %shard_map.223), channel_id=1, replica_groups={{0,2,4,6},{1,3,5,7},{8,10,12,14},{9,11,13,15},{16,18,20,22},{17,19,21,2..., dimensions={0} | all-to-all | bytes 1048576 | tf_op jit(solution)/shard_map/all_to_all | solution.py:650
  155.2 4.8 %all-to-all-start.2 = ((bf16[32,96,128]{2,1,0:T(8,128)(2,1)}), bf16[32,96,128]{2,1,0:T(8,128)(2,1)S(1)}, u32[]{:S(2)}, u32[]{:S(2)}) async-start(bf16[32,96,128]{2,1,0:T(8,128)(2,1)} %get-tuple-element.44), calls=%async_computation.2 | async-start | bytes 1572864 | tf_op jit(solution)/shard_map/all_to_all | solution.py:585
  160.0 0.1 collective-permute-start.3
  160.1 18.3 %all-to-all-done.2.zero_ref = bf16[32,96,128]{2,1,0:T(8,128)(2,1)S(1)} async-done(((bf16[32,96,128]{2,1,0:T(8,128)(2,1)}), bf16[32,96,128]{2,1,0:T(8,128)(2,1)S(1)}, u32[]{:S(2)}, u32[]{:S(2)}) %all-to-all-start.2) | async-done | bytes 786464 | tf_op jit(solution)/shard_map/all_to_all | solution.py:585
  178.4 1.5 shard_map.220
  179.9 1.8 shard_map.222
  181.8 1.4 shard_map.224
  (28 shorter events, 0.1 us)
Async XLA Ops:
  1.9 19.9 %all-to-all-start = ((s32[32,1,16]{2,1,0:T(1,128)}), s32[32,1,16]{2,1,0:T(1,128)S(1)}, u32[]{:S(2)}, u32[]{:S(2)}) async-start(s32[32,1,16]{2,1,0:T(1,128)} %reshape.55), calls=%async_computation | async-start | bytes 32768 | tf_op jit(solution)/shard_map/all_to_all | solution.py:585
  23.7 6.0 %copy-start.5 = (bf16[192,768]{1,0:T(8,128)(2,1)S(1)}, bf16[192,768]{1,0:T(8,128)(2,1)}, u32[]{:S(2)}) copy-start(bf16[192,768]{1,0:T(8,128)(2,1)} %w_up_ref.1) | copy-start | bytes 884740
  23.7 6.0 %copy-start.9 = (bf16[128,384]{1,0:T(8,128)(2,1)S(1)}, bf16[128,384]{1,0:T(8,128)(2,1)}, u32[]{:S(2)}) copy-start(bf16[128,384]{1,0:T(8,128)(2,1)} %test_ref.1) | copy-start | bytes 294916
  23.7 6.0 %copy-start.10 = (bf16[128,384]{1,0:T(8,128)(2,1)S(1)}, bf16[128,384]{1,0:T(8,128)(2,1)}, u32[]{:S(2)}) copy-start(bf16[128,384]{1,0:T(8,128)(2,1)} %cot_ref.1) | copy-start | bytes 294916
  23.7 6.0 %copy-start.15 = (f32[192]{0:T(256)S(1)}, f32[192]{0:T(256)}, u32[]{:S(2)}) copy-start(f32[192]{0:T(256)} %param.20) | copy-start | bytes 2308
  23.7 6.0 %copy-start.16 = (f32[192]{0:T(256)S(1)}, f32[192]{0:T(256)}, u32[]{:S(2)}) copy-start(f32[192]{0:T(256)} %param.22) | copy-start | bytes 2308
  23.7 6.0 %copy-start.17 = (f32[192]{0:T(256)S(1)}, f32[192]{0:T(256)}, u32[]{:S(2)}) copy-start(f32[192]{0:T(256)} %param.25) | copy-start | bytes 2308
  23.7 5.9 %copy-start.18 = (f32[192]{0:T(256)S(1)}, f32[192]{0:T(256)}, u32[]{:S(2)}) copy-start(f32[192]{0:T(256)} %param.28) | copy-start | bytes 2308
  23.7 12.7 %copy-start.19 = (s32[1,16]{1,0:T(1,128)S(1)}, s32[1,16]{1,0:T(1,128)}, u32[]{:S(2)}) copy-start(s32[1,16]{1,0:T(1,128)} %param.18) | copy-start | bytes 196
  23.8 43.9 %all-to-all-start.1 = ((bf16[32,64,384]{2,1,0:T(8,128)(2,1)}), bf16[32,64,384]{2,1,0:T(8,128)(2,1)}, u32[]{:S(2)}, u32[]{:S(2)}) async-start(bf16[32,64,384]{2,1,0:T(8,128)(2,1)} %shard_map.214), calls=%async_computation.1 | async-start | bytes 3145728 | tf_op jit(solution)/shard_map/all_to_all | solution.py:585
  29.7 1.0 copy-start.6
  30.7 0.9 copy-start.11
  31.5 0.9 copy-start.12
  32.4 0.9 copy-start.13
  33.3 0.9 copy-start.14
  34.8 1.0 copy-start
  35.8 0.7 copy-start.7
  67.7 1.0 copy-start.8
  82.4 0.7 copy-start.1
  83.1 0.7 copy-start.3
  83.9 17.3 %copy-start.4 = (bf16[32,48,128]{2,1,0:T(8,128)(2,1)S(1)}, bf16[32,48,128]{2,1,0:T(8,128)(2,1)}, u32[]{:S(2)}) copy-start(bf16[32,48,128]{2,1,0:T(8,128)(2,1)} %copy-done.3) | copy-start | bytes 1179652
  83.9 2.1 %collective-permute-start = (bf16[2048,128]{1,0:T(8,128)(2,1)}, bf16[2048,128]{1,0:T(8,128)(2,1)S(1)}, u32[]{:S(2)}, u32[]{:S(2)}) collective-permute-start(bf16[2048,128]{1,0:T(8,128)(2,1)} %get-tuple-element.46), channel_id=1, source_target_pairs={{0,1},{1,0},{2,3},{3,2},{4,5},{5,4},{6,7},{7,6},{8,9},{9,8},{10,11... | collective-permute-start | bytes 1572872 | tf_op jit(solution)/shard_map/ppermute | solution.py:680
  86.1 36.8 %copy-start.2 = (bf16[32,48,128]{2,1,0:T(8,128)(2,1)S(1)}, bf16[32,48,128]{2,1,0:T(8,128)(2,1)}, u32[]{:S(2)}) copy-start(bf16[32,48,128]{2,1,0:T(8,128)(2,1)} %copy-done.1) | copy-start | bytes 1179652
  86.1 8.4 %collective-permute-start.1 = (bf16[1024,128]{1,0:T(8,128)(2,1)S(1)}, bf16[1024,128]{1,0:T(8,128)(2,1)S(1)}, u32[]{:S(2)}, u32[]{:S(2)}) collective-permute-start(bf16[1024,128]{1,0:T(8,128)(2,1)S(1)} %get-tuple-element.48), channel_id=1, source_target_pairs={{0,2},{1,3},{2,0},{3,1},{4,6},{5,7},{6,4},{7,5},{8,10},{9,11},{10,... | collective-permute-start | bytes 786440 | tf_op jit(solution)/shard_map/ppermute | solution.py:680
  94.6 6.6 %collective-permute-start.2 = (bf16[512,128]{1,0:T(8,128)(2,1)S(1)}, bf16[512,128]{1,0:T(8,128)(2,1)S(1)}, u32[]{:S(2)}, u32[]{:S(2)}) collective-permute-start(bf16[512,128]{1,0:T(8,128)(2,1)S(1)} %get-tuple-element.50), channel_id=1, source_target_pairs={{0,4},{1,5},{2,6},{3,7},{4,0},{5,1},{6,2},{7,3},{8,12},{9,13},{10,... | collective-permute-start | bytes 393224 | tf_op jit(solution)/shard_map/ppermute | solution.py:680
  155.2 23.2 %all-to-all-start.2 = ((bf16[32,96,128]{2,1,0:T(8,128)(2,1)}), bf16[32,96,128]{2,1,0:T(8,128)(2,1)S(1)}, u32[]{:S(2)}, u32[]{:S(2)}) async-start(bf16[32,96,128]{2,1,0:T(8,128)(2,1)} %get-tuple-element.44), calls=%async_computation.2 | async-start | bytes 1572864 | tf_op jit(solution)/shard_map/all_to_all | solution.py:585
  160.0 21.7 %collective-permute-start.3 = (bf16[4,512,128]{2,1,0:T(8,128)(2,1)S(1)}, bf16[4,512,128]{2,1,0:T(8,128)(2,1)S(1)}, u32[]{:S(2)}, u32[]{:S(2)}) collective-permute-start(bf16[4,512,128]{2,1,0:T(8,128)(2,1)S(1)} %all_to_all.32.mine_ref), channel_id=1, source_target_pairs={{0,1},{1,0},{2,3},{3,2},{4,5},{5,4},{6,7},{7,6},{8,9},{9,8},{10,11... | collective-permute-start | bytes 1572872 | tf_op jit(solution)/shard_map/ppermute | solution.py:680

commit v4 on v3

--- a/solution.py
+++ b/solution.py
@@ -161,9 +161,7 @@
     ffn_ref,
     gains_ref,
     cells_ref,
-    q_pre_ref,
     q_tall_ref,
-    q_rows_ref,
 ):
     rows = test_ref.shape[0]
     row = lax.broadcasted_iota(jnp.int32, (E, W), 0)
@@ -198,13 +196,11 @@
         pre = dot_nn(test[:, lanes], projections_ref[0, f])
         norm = pre * lax.rsqrt(mean_e(pre * pre) + 1e-06) * q_gain
         norm = norm.astype(bf16).astype(f32)
-        q_pre_ref[here, :] = pre
         q_tall_ref[f] = spread_columns(norm.T, True)
-        q_rows_ref[f] = spread_rows(norm)
 
 
 def main_kernel(
-    chunk,
+    tile,
     owner_ref,
     core_ref,
     rec_hbm,
@@ -212,31 +208,31 @@
     ffn_hbm,
     gains_hbm,
     cells_hbm,
-    q_pre_hbm,
     q_tall_hbm,
-    q_rows_hbm,
     out_ref,
     grad_test_ref,
-    zero_ref,
-    one_ref,
-    two_ref,
+    zero_hbm,
+    one_hbm,
+    two_hbm,
     keep_hbm,
     give_hbm,
     projections_ref,
     ffn_ref,
     gains_ref,
     cells_ref,
-    q_pre_ref,
     q_tall_ref,
-    q_rows_ref,
     cells_s,
     kp_s,
     k_s,
     v_s,
     e_s,
     p_s,
+    ds_s,
     d_s,
     grads_ref,
+    zero_ref,
+    one_ref,
+    two_ref,
     rec_sem,
     sems,
 ):
@@ -244,7 +240,6 @@
     feats = 2
     rows = out_ref.shape[0]
     keys = count * BLK
-    chunks = keys // chunk
 
     def gather(j, carry):
         pltpu.make_async_copy(
@@ -262,10 +257,8 @@
                 (projections_hbm, projections_ref),
                 (gains_hbm, gains_ref),
                 (q_tall_hbm, q_tall_ref),
+                (cells_hbm, cells_ref),
                 (ffn_hbm, ffn_ref),
-                (cells_hbm, cells_ref),
-                (q_pre_hbm, q_pre_ref),
-                (q_rows_hbm, q_rows_ref),
             )
         )
     ]
@@ -275,7 +268,7 @@
     one_ref[...] = jnp.zeros_like(one_ref)
     two_ref[...] = jnp.zeros_like(two_ref)
     pltpu.make_async_copy(cells_s, cells_s, rec_sem).wait()
-    for copy in copies:
+    for copy in copies[:3]:
         copy.wait()
 
     q_gain = gains_ref[0:1, :]
@@ -283,42 +276,36 @@
     gain_one = gains_ref[2:3, :]
     gain_two = gains_ref[3:4, :]
 
-    def scores(c, totals):
-        start = pl.ds(pl.multiple_of(c * chunk, chunk), chunk)
-        result = []
-        for f in range(feats):
-            pre = dot_nn(cells_s[start, feature_lanes(f)], projections_ref[1, f])
+    tiles = [slice(t * tile, (t + 1) * tile) for t in range(keys // tile)]
+    totals = []
+    for f in range(feats):
+        total = jnp.zeros((8, H * rows), f32)
+        for here in tiles:
+            cells = cells_s[here, feature_lanes(f)]
+            pre = dot_nn(cells, projections_ref[1, f])
             lane = lax.broadcasted_iota(jnp.int32, pre.shape, 1)
             body = jnp.where(lane < E, pre, 0.0)
             scale = lax.rsqrt(mean_e(body * body) + 1e-06)
-            norm = body * scale * k_gain
             bias = jnp.where((lane == E) & (pre > ABSENT_ABOVE), MASKED, 0.0)
-            norm = (norm + bias).astype(bf16)
-            kp_s[f, start, :] = body
-            k_s[f, start, :] = norm
-            v_s[f, start, :] = dot_nn(cells_s[start, feature_lanes(f)], projections_ref[2, f]).astype(bf16)
+            norm = (body * scale * k_gain + bias).astype(bf16)
+            kp_s[f, here, :] = body
+            k_s[f, here, :] = norm
+            v_s[f, here, :] = dot_nn(cells, projections_ref[2, f]).astype(bf16)
             e = jnp.exp2(dot_nn(norm, q_tall_ref[f]) * (TEMPER * LOG2E))
-            e_s[f, start, :] = e
-            result.append(totals[f] + jnp.sum(e, axis=0, keepdims=True))
-        return tuple(result)
-
-    zero = jnp.zeros((1, H * rows), f32)
-    totals = lax.fori_loop(0, chunks, scores, (zero,) * feats)
+            e_s[f, here, :] = e
+            total = total + jnp.sum(e.reshape(tile // 8, 8, H * rows), axis=0)
+        totals.append(jnp.sum(total, axis=0, keepdims=True))
     inverse = [1.0 / total for total in totals]
     inverse_tempered = [TEMPER / total for total in totals]
-
-    def attend(c, mixed):
-        start = pl.ds(pl.multiple_of(c * chunk, chunk), chunk)
-        result = []
-        for f in range(feats):
-            p = (e_s[f, start, :] * inverse[f]).astype(bf16)
-            p_s[f, start, :] = p
-            result.append(mixed[f] + dot_tn(v_s[f, start, :E], p))
-        return tuple(result)
-
-    mixed = lax.fori_loop(0, chunks, attend, (jnp.zeros((E, H * rows), f32),) * feats)
+    mixed = []
+    for f in range(feats):
+        for here in tiles:
+            p_s[f, here, :] = (e_s[f, here, :] * inverse[f]).astype(bf16)
+        mixed.append(dot_tn(v_s[f, :, :E], p_s[f]))
     attended_t = [head_blocks(m) for m in mixed]
 
+    for copy in copies[3:]:
+        copy.wait()
     attended = jnp.concatenate([a.T for a in attended_t], axis=0).astype(bf16)
     lane_in = lax.broadcasted_iota(jnp.int32, (feats * rows, W), 1) < E
     w_up = ffn_ref[:, :FFH]
@@ -353,7 +340,15 @@
     put_grads(grads_ref, 14, dot_tn(d_two_b, hidden)[:E])
 
     da_t, da_rows, dots = [], [], []
+    q_cells, q_pre, q_scale, q_rows = [], [], [], []
     for f in range(feats):
+        cells = cells_ref[0, f * rows : (f + 1) * rows, :].astype(bf16)
+        pre = dot_nn(cells, projections_ref[0, 0])
+        scale = lax.rsqrt(mean_e(pre * pre) + 1e-06)
+        q_cells.append(cells)
+        q_pre.append(pre)
+        q_scale.append(scale)
+        q_rows.append(spread_rows((pre * scale * q_gain).astype(bf16).astype(f32)))
         mine = d_att[f * rows : (f + 1) * rows]
         mine_t = mine.T
         da_t.append(spread_columns(mine_t, False))
@@ -369,37 +364,44 @@
             )
         )
 
-    def back(c, d_queries):
-        start = pl.ds(pl.multiple_of(c * chunk, chunk), chunk)
-        result = []
+    d_queries = []
+    for f in range(feats):
+        for here in tiles:
+            grad_w = dot_nn(v_s[f, here, :], da_t[f])
+            probs = e_s[f, here, :] * inverse_tempered[f]
+            ds_s[f, here, :] = (probs * (grad_w - dots[f])).astype(bf16)
+        d_queries.append(dot_tn(k_s[f, :, :E], ds_s[f]))
+    for t, here in enumerate(tiles):
         d_cells = []
         for f in range(feats):
-            grad_w = dot_nn(v_s[f, start, :], da_t[f])
-            probs = e_s[f, start, :] * inverse_tempered[f]
-            d_scores = (probs * (grad_w - dots[f])).astype(bf16)
-            result.append(d_queries[f] + dot_tn(k_s[f, start, :E], d_scores))
-            d_key = dot_nn(d_scores, q_rows_ref[f])
-            d_value = dot_nn(p_s[f, start, :], da_rows[f]).astype(bf16)
-            body = kp_s[f, start, :]
+            d_key = dot_nn(ds_s[f, here, :], q_rows[f])
+            d_value = dot_nn(p_s[f, here, :], da_rows[f]).astype(bf16)
+            body = kp_s[f, here, :]
             scale = lax.rsqrt(mean_e(body * body) + 1e-06)
             d_kpre = rms_back(body, scale, k_gain, d_key).astype(bf16)
-            d_s[start, 2 * f * W : (2 * f + 1) * W] = d_kpre
-            d_s[start, (2 * f + 1) * W : (2 * f + 2) * W] = d_value
+            d_s[here, 2 * f * W : (2 * f + 1) * W] = d_kpre
+            d_s[here, (2 * f + 1) * W : (2 * f + 2) * W] = d_value
             d_cells.append(
                 dot_nt(d_kpre, projections_ref[1, f]) + dot_nt(d_value, projections_ref[2, f])
             )
         d_cells = side_by_side(*d_cells).astype(bf16)
-        for b in range(chunk // BLK):
-            owner = owner_ref[c * (chunk // BLK) + b]
+        for b in range(tile // BLK):
+            owner = owner_ref[t * (tile // BLK) + b]
             block = d_cells[b * BLK : (b + 1) * BLK]
             zero_ref[owner, :BLK] = block[:, :128]
             zero_ref[owner, BLK:] = block[:32, 128:256]
             one_ref[owner, :32] = block[32:, 128:256]
             one_ref[owner, 32:] = block[:16, 256:]
             two_ref[owner] = block[16:, 256:]
-        return tuple(result)
-
-    d_queries = lax.fori_loop(0, chunks, back, (jnp.zeros((E, H * rows), f32),) * feats)
+
+    sends = [
+        pltpu.make_async_copy(source, target, sems.at[i])
+        for i, (source, target) in enumerate(
+            ((zero_ref, zero_hbm), (one_ref, one_hbm), (two_ref, two_hbm))
+        )
+    ]
+    for copy in sends:
+        copy.start()
 
     d_test = []
     g_query = jnp.zeros((W, W), f32)
@@ -407,10 +409,8 @@
     for f in range(feats):
         here = slice(f * rows, (f + 1) * rows)
         d_query = head_blocks(d_queries[f]).T
-        pre = q_pre_ref[here, :]
-        scale = lax.rsqrt(mean_e(pre * pre) + 1e-06)
-        d_qpre = rms_back(pre, scale, q_gain, d_query).astype(bf16)
-        g_query = g_query + dot_tn(cells_ref[0, here, :].astype(bf16), d_qpre)
+        d_qpre = rms_back(q_pre[f], q_scale[f], q_gain, d_query).astype(bf16)
+        g_query = g_query + dot_tn(q_cells[f], d_qpre)
         d_test.append(dot_nt(d_qpre, projections_ref[0, f]))
         placed.append(d_one[here, :E])
     grad_test_ref[...] = (side_by_side(*d_test) + jnp.concatenate(placed, axis=1)).astype(bf16)
@@ -422,17 +422,14 @@
     put_grads(grads_ref, 2, kv)
     grads_ref[20 * E :, :] = jnp.zeros((GRAD_ROWS - 20 * E, 128), bf16)
     core = core_ref[0]
-    halves = [
-        pltpu.make_async_copy(
-            grads_ref.at[pl.ds(pl.multiple_of(half * (GRAD_ROWS // 2), 128), GRAD_ROWS // 2), :],
-            target,
-            sems.at[i],
+    for i, (half, target) in enumerate(((core, keep_hbm), (1 - core, give_hbm))):
+        start = pl.multiple_of(half * (GRAD_ROWS // 2), 128)
+        copy = pltpu.make_async_copy(
+            grads_ref.at[pl.ds(start, GRAD_ROWS // 2), :], target, sems.at[len(sends)]
         )
-        for i, (half, target) in enumerate(((core, keep_hbm), (1 - core, give_hbm)))
-    ]
-    for copy in halves:
         copy.start()
-    for copy in halves:
+        sends.append(copy)
+    for copy in sends:
         copy.wait()
 
 
@@ -456,7 +453,7 @@
         ref[...] = (keep_ref[rows, :].astype(f32) + got_ref[rows, :].astype(f32)).astype(bf16)
 
 
-def ride_kernel(keep_ref, got_ref, one_ref, out_ref):
+def ride_kernel(keep_ref, got_ref, one_ref, earlier_ref, out_ref):
     cut = one_ref.shape[1]
     total = (keep_ref[...].astype(f32) + got_ref[...].astype(f32)).astype(bf16)
     out_ref[:, :cut, :] = one_ref[...]
@@ -470,7 +467,7 @@
     out_ref[:, cut:, :] = jnp.broadcast_to(total[None], out_ref[:, cut:, :].shape)
 
 
-def share_kernel(back_ref, out_ref):
+def share_kernel(back_ref, zero_ref, one_ref, out_ref):
     pieces = out_ref.shape[1] // back_ref.shape[0]
     share = back_ref[:, back_ref.shape[1] - pieces :, :].reshape(out_ref.shape[1], 128)
     out_ref[...] = jnp.broadcast_to(share[None], out_ref.shape)
@@ -497,18 +494,21 @@
 
 
 SMEM_SPEC = pl.BlockSpec(memory_space=pltpu.SMEM)
-LIMIT = 48 * 1024 * 1024
-
-
+MIB = 1024 * 1024
+
+
+BUSY = pl.CostEstimate(flops=10**9, bytes_accessed=4 * MIB, transcendentals=0)
 ANY_SPEC = pl.BlockSpec(memory_space=pl.ANY)
-PARAMS = pltpu.CompilerParams(vmem_limit_bytes=LIMIT)
+HBM_SPEC = pl.BlockSpec(memory_space=pltpu.HBM)
+PARAMS = pltpu.CompilerParams(vmem_limit_bytes=12 * MIB)
+MAIN_PARAMS = pltpu.CompilerParams(vmem_limit_bytes=62 * MIB)
 
 
 def shape(dims, dtype=bf16):
     return jax.ShapeDtypeStruct(dims, dtype)
 
 
-def small_call(kernel, out_shape, *args, scalars=(), scratch=()):
+def small_call(kernel, out_shape, *args, scalars=(), scratch=(), cost=None):
     return pl.pallas_call(
         kernel,
         out_shape=out_shape,
@@ -516,6 +516,7 @@
         out_specs=jax.tree.map(lambda _: vmem_specs(1)[0], out_shape),
         scratch_shapes=scratch,
         compiler_params=PARAMS,
+        cost_estimate=cost,
     )(*scalars, *args)
 
 
@@ -523,47 +524,37 @@
     w_query, q_gain, w_key, k_gain, w_value, w_out, gain_one, w_up, w_down, gain_two = weights
     rows, wide = test_cells.shape
     ht = H * rows
-    return small_call(
-        prepare_kernel,
-        (
-            shape((4, 2, W, W)),
-            shape((W, 2 * FFH + W)),
-            shape((4, W), f32),
-            shape((2, 2 * rows, W), f32),
-            shape((2 * rows, W), f32),
-            shape((2, W, ht)),
-            shape((2, ht, W)),
-        ),
-        test_cells,
-        cotangent,
-        w_query,
-        w_key,
-        w_value,
-        w_out,
-        w_up,
-        w_down.T,
-        *(gain.reshape(1, E) for gain in (q_gain, k_gain, gain_one, gain_two)),
-    )
-
-
-def main_call(owner_of, core, rec, prepared, rows, chunk):
+    shapes = (
+        shape((4, 2, W, W)),
+        shape((W, 2 * FFH + W)),
+        shape((4, W), f32),
+        shape((2, 2 * rows, W), f32),
+        shape((2, W, ht)),
+    )
+    args = (test_cells, cotangent, w_query, w_key, w_value, w_out, w_up, w_down.T) + tuple(
+        gain.reshape(1, E) for gain in (q_gain, k_gain, gain_one, gain_two)
+    )
+    return small_call(prepare_kernel, shapes, *args)
+
+
+def main_call(owner_of, core, rec, prepared, rows, tile):
     count = owner_of.shape[0]
     keys = count * BLK
     owners, _, wide = rec.shape
     ht = H * rows
     return pl.pallas_call(
-        functools.partial(main_kernel, chunk),
+        functools.partial(main_kernel, tile),
         out_shape=(
             shape((rows, wide)),
             shape((rows, wide)),
-            shape((owners, 96, 128)),
-            shape((owners, 48, 128)),
-            shape((owners, 48, 128)),
-            shape((GRAD_ROWS // 2, 128)),
-            shape((GRAD_ROWS // 2, 128)),
+            pltpu.HBM((owners, 96, 128), bf16),
+            pltpu.HBM((owners, 48, 128), bf16),
+            pltpu.HBM((owners, 48, 128), bf16),
+            pltpu.HBM((GRAD_ROWS // 2, 128), bf16),
+            pltpu.HBM((GRAD_ROWS // 2, 128), bf16),
         ),
-        in_specs=[SMEM_SPEC] * 2 + [ANY_SPEC] * (1 + len(prepared)),
-        out_specs=tuple(vmem_specs(5)) + (ANY_SPEC,) * 2,
+        in_specs=[SMEM_SPEC] * 2 + [HBM_SPEC] * (1 + len(prepared)),
+        out_specs=tuple(vmem_specs(2)) + (HBM_SPEC,) * 5,
         scratch_shapes=[pltpu.VMEM(x.shape, x.dtype) for x in prepared]
         + [
             pltpu.VMEM((keys, wide), bf16),
@@ -572,12 +563,16 @@
             pltpu.VMEM((2, keys, W), bf16),
             pltpu.VMEM((2, keys, ht), f32),
             pltpu.VMEM((2, keys, ht), bf16),
+            pltpu.VMEM((2, keys, ht), bf16),
             pltpu.VMEM((keys, 4 * W), bf16),
             pltpu.VMEM((GRAD_ROWS, 128), bf16),
+            pltpu.VMEM((owners, 96, 128), bf16),
+            pltpu.VMEM((owners, 48, 128), bf16),
+            pltpu.VMEM((owners, 48, 128), bf16),
             pltpu.SemaphoreType.DMA,
             pltpu.SemaphoreType.DMA((len(prepared),)),
         ],
-        compiler_params=PARAMS,
+        compiler_params=MAIN_PARAMS,
     )(owner_of, core, rec, *prepared)
 
 
@@ -607,7 +602,7 @@
     rows, wide = test_cells.shape
     count = retrieved.shape[1]
     owner_of = retrieved[0] // blocks_own
-    table = swap(jnp.broadcast_to(retrieved, (owners, count)).reshape(owners, 1, count), "rows")
+    table = swap(jnp.broadcast_to(retrieved[None], (owners, 1, count)), "rows")
     table = table.reshape(owners, count)
     mine = table // blocks_own == lax.axis_index("rows")
     asked = jnp.sum(jnp.where(mine, table % blocks_own + 1, 0), axis=1) - 1
@@ -643,10 +638,31 @@
     got = flip(give, 4)
     piece = half // owners
     riding = shape((owners, one.shape[1] + piece, 128))
-    back_one = swap(small_call(ride_kernel, riding, keep, got, one), "rows")
+    ride = pl.pallas_call(
+        ride_kernel,
+        out_shape=riding,
+        in_specs=vmem_specs(3) + [ANY_SPEC],
+        out_specs=vmem_specs(1)[0],
+        compiler_params=PARAMS,
+    )(keep, got, one, back_zero)
+    back_one = swap(ride, "rows")
     back_two = swap(small_call(ride_back_kernel, riding, back_one, two), "rows")
     chips = groups // 2
-    copies = small_call(share_kernel, shape((chips, half, 128)), back_two)
+    sums = small_call(
+        sum_kernel,
+        tuple(shape((blocks_own, x.shape[1], 128), f32) for x in (zero, one)),
+        back_zero,
+        back_one,
+        scalars=(asked,),
+        cost=BUSY,
+    )
+    copies = pl.pallas_call(
+        share_kernel,
+        out_shape=shape((chips, half, 128)),
+        in_specs=vmem_specs(1) + [ANY_SPEC] * 2,
+        out_specs=vmem_specs(1)[0],
+        compiler_params=PARAMS,
+    )(back_two, *sums)
     mine = lax.all_to_all(
         copies,
         "feat",
@@ -656,13 +672,6 @@
         axis_index_groups=[[2 * chip + c for chip in range(chips)] for c in range(2)],
     )
     others = flip(mine, 1)
-    sums = small_call(
-        sum_kernel,
-        tuple(shape((blocks_own, x.shape[1], 128), f32) for x in (zero, one)),
-        back_zero,
-        back_one,
-        scalars=(asked,),
-    )
     grad_train = small_call(
         last_kernel,
         shape((blocks_own, BLK, wide)),
@@ -670,6 +679,7 @@
         back_two,
         scalars=(asked,),
         scratch=[pltpu.VMEM((blocks_own, two.shape[1], 128), f32)],
+        cost=BUSY,
     ).reshape(blocks_own * BLK, wide)
     *weights, g_down_t = unpack(core, mine, others)
     return (out_cells, grad_test, grad_train, *weights, g_down_t.T)

time: 184 us -> 171 us (0.929)
  blocking collectives: 53.8 us -> 33.6 us
  starting transfers between devices: 26.8 us -> 33 us
  local copies, waits for them, and re-layouts: 11.3 us -> 6.95 us
  waiting for transfers between devices: 68.3 us -> 71.2 us
    all_to_all x2 -> x1, blocking collectives: 41.6 us -> 21.4 us  [swap(): return lax.all_to_all(x, axis, split_axis=0, concat_axis=0, tiled=True)]
    all_to_all x3 -> x4, starting transfers between devices: 22 us -> 28.1 us  [swap(): return lax.all_to_all(x, axis, split_axis=0, concat_axis=0, tiled=True)]
    unnamed x41 -> x45, local copies, waits for them, and re-layouts: 9.85 us -> 5.47 us
    all_to_all x3 -> x4, waiting for transfers between devices: 55.9 us -> 58.9 us  [swap(): return lax.all_to_all(x, axis, split_axis=0, concat_axis=0, tiled=True)]
    pallas_call x9 -> x7, Pallas kernels: 5.66 us -> 6.33 us  [small_call(): pl.pallas_call(kernel, out_shape=out_shape, in_specs=[SMEM_SPEC] * len(sc...]
    pallas_call x1 -> x3, Pallas kernels: 13.7 us -> 13.9 us  [the longest x1 13.8 us: main_call(): pl.pallas_call(functools.partial(main_kernel, tile), out_shape=(shape((ro...]
  transfers between devices with their start and end apart: 7 -> 8, of which waited for: 6 -> 8; matrix products, arithmetic and copies ran while one was open for 1% -> 2% of each run, Pallas kernels for 2% -> 2%
where the time goes in v4:
time: 171 us; the launch traced here: 169 us
  waiting for transfers between devices  71.2 us (42%)
  blocking collectives  33.6 us (20%)
  starting transfers between devices  33 us (19%)
  Pallas kernels  22 us (13%)
  local copies, waits for them, and re-layouts  6.95 us (4%)
    all_to_all x4, waiting for transfers between devices, swap(): return lax.all_to_all(x, axis, split_axis=0, concat_axis=0, tiled=True)  58.9 us
    all_to_all x4, starting transfers between devices, swap(): return lax.all_to_all(x, axis, split_axis=0, concat_axis=0, tiled=True)  28.1 us
    all_to_all x1, blocking collectives, swap(): return lax.all_to_all(x, axis, split_axis=0, concat_axis=0, tiled=True)  21.4 us
    pallas_call x1, Pallas kernels, main_call(): pl.pallas_call(functools.partial(main_kernel, tile), out_shape=(shape((ro...  13.8 us
    ppermute x4, waiting for transfers between devices, flip(): return lax.ppermute(x, 'feat', [(i, i ^ bit) for i in range(count)])  12.3 us
    all_to_all x1, blocking collectives, on_device(): lax.all_to_all(copies, 'feat', split_axis=0, concat_axis=0, tiled=True, a...  12.2 us
    pallas_call x7, Pallas kernels, small_call(): pl.pallas_call(kernel, out_shape=out_shape, in_specs=[SMEM_SPEC] * len(sc...  6.33 us
    unnamed x45, local copies, waits for them, and re-layouts  5.47 us
  transfers between devices with their start and end apart: 8, of which 8 were waited for; matrix products, arithmetic and copies ran while one was open for 2% of the time, Pallas kernels for 2%

profile of v4, /device:TPU:32, one launch (start us, length us, event | category | flops | bytes accessed | tf_op | source)
XLA Modules:
  0.0 169.2 jit_solution(6255617695444066414)
XLA Ops:
  0.6 1.3 broadcast_in_dim.15
  1.9 11.4 %all-to-all-start = ((s32[32,1,16]{2,1,0:T(1,128)}), s32[32,1,16]{2,1,0:T(1,128)S(1)}, u32[]{:S(2)}, u32[]{:S(2)}) async-start(s32[32,1,16]{2,1,0:T(1,128)} %broadcast_in_dim.15), calls=%async_computation | async-start | bytes 32768 | tf_op jit(solution)/shard_map/all_to_all | solution.py:580
  13.3 0.7 compare_bitcast_fusion
  14.0 1.2 copy.30
  15.2 0.2 copy.31
  15.4 6.4 %all-to-all-done = s32[32,1,16]{2,1,0:T(1,128)S(1)} async-done(((s32[32,1,16]{2,1,0:T(1,128)}), s32[32,1,16]{2,1,0:T(1,128)S(1)}, u32[]{:S(2)}, u32[]{:S(2)}) %all-to-all-start) | async-done | bytes 2080 | tf_op jit(solution)/shard_map/all_to_all | solution.py:580
  21.8 0.1 fusion.3
  22.0 1.7 %shard_map.214 = bf16[32,64,384]{2,1,0:T(8,128)(2,1)} custom-call(s32[32]{0:T(128)S(1)} %broadcast_add_fusion.asked_ref, bf16[8,64,384]{2,1,0:T(8,128)(2,1)S(1)} %bitcast.18), custom_call_target="tpu_custom_call" | custom-call | tf_op jit(solution)/shard_map/pallas_call | solution.py:611
  23.7 0.0 copy-start.7
  23.7 0.0 copy-start.8
  23.7 0.0 copy-start.10
  23.7 0.0 copy-start.11
  23.8 0.0 copy-start.14
  23.8 0.0 copy-start.16
  23.8 0.0 copy-start.18
  23.8 0.0 copy-start.19
  23.9 5.8 %all-to-all-start.1 = ((bf16[32,64,384]{2,1,0:T(8,128)(2,1)}), bf16[32,64,384]{2,1,0:T(8,128)(2,1)}, u32[]{:S(2)}, u32[]{:S(2)}) async-start(bf16[32,64,384]{2,1,0:T(8,128)(2,1)} %shard_map.214), calls=%async_computation.1 | async-start | bytes 3145728 | tf_op jit(solution)/shard_map/all_to_all | solution.py:580
  29.8 0.5 shard_map.215
  30.4 1.0 copy-done
  31.4 0.9 copy-done.1
  32.3 0.9 copy-done.2
  33.2 0.8 copy-done.3
  34.0 0.6 copy-done.15
  34.6 0.5 and_select_fusion.owner_ref
  35.1 32.7 %all-to-all-done.1.rec_hbm = bf16[32,64,384]{2,1,0:T(8,128)(2,1)} async-done(((bf16[32,64,384]{2,1,0:T(8,128)(2,1)}), bf16[32,64,384]{2,1,0:T(8,128)(2,1)}, u32[]{:S(2)}, u32[]{:S(2)}) %all-to-all-start.1) | async-done | bytes 1572896 | tf_op jit(solution)/shard_map/all_to_all | solution.py:580
  67.8 13.8 %shard_map.216 = (bf16[128,384]{1,0:T(8,128)(2,1)}, bf16[128,384]{1,0:T(8,128)(2,1)}, bf16[32,96,128]{2,1,0:T(8,128)(2,1)}, bf16[32,48,128]{2,1,0:T(8,128)(2,1)}...) custom-call(s32[16]{0:T(128)} %and_select_fusion.owner_ref, ...), custom_call_target="tpu_custom_call" | custom-call | tf_op jit(solution)/shard_map/pallas_call | solution.py:545
  81.6 0.0 copy-start.6
  81.6 6.0 %all-to-all-start.2 = ((bf16[32,96,128]{2,1,0:T(8,128)(2,1)}), bf16[32,96,128]{2,1,0:T(8,128)(2,1)S(1)}, u32[]{:S(2)}, u32[]{:S(2)}) async-start(bf16[32,96,128]{2,1,0:T(8,128)(2,1)} %get-tuple-element.40), calls=%async_computation.2 | async-start | bytes 1572864 | tf_op jit(solution)/shard_map/all_to_all | solution.py:580
  87.7 0.3 collective-permute-start
  88.0 1.9 %collective-permute-done.got_ref = bf16[2048,128]{1,0:T(8,128)(2,1)S(1)} collective-permute-done((bf16[2048,128]{1,0:T(8,128)(2,1)S(1)}, bf16[2048,128]{1,0:T(8,128)(2,1)S(1)}, u32[]{:S(2)}, u32[]{:S(2)}) %collective-permute-start) | collective-permute-done | bytes 524320 | tf_op jit(solution)/shard_map/ppermute | solution.py:690
  89.9 0.1 shard_map.217
  90.0 1.6 collective-permute-start.1
  91.5 6.9 %collective-permute-done.1.got_ref = bf16[1024,128]{1,0:T(8,128)(2,1)S(1)} collective-permute-done((bf16[1024,128]{1,0:T(8,128)(2,1)S(1)}, bf16[1024,128]{1,0:T(8,128)(2,1)S(1)}, u32[]{:S(2)}, u32[]{:S(2)}) %collective-permute-start.1) | collective-permute-done | bytes 262176 | tf_op jit(solution)/shard_map/ppermute | solution.py:690
  98.4 0.1 shard_map.218
  98.5 3.1 %collective-permute-start.2 = (bf16[512,128]{1,0:T(8,128)(2,1)S(1)}, bf16[512,128]{1,0:T(8,128)(2,1)S(1)}, u32[]{:S(2)}, u32[]{:S(2)}) collective-permute-start(bf16[512,128]{1,0:T(8,128)(2,1)S(1)} %get-tuple-element.46), channel_id=1, source_target_pairs={{0,4},{1,5},{2,6},{3,7},{4,0},{5,1},{6,2},{7,3},{8,12},{9,13},{10,... | collective-permute-start | bytes 393224 | tf_op jit(solution)/shard_map/ppermute | solution.py:690
  101.6 3.5 %collective-permute-done.2.got_ref = bf16[512,128]{1,0:T(8,128)(2,1)S(1)} collective-permute-done((bf16[512,128]{1,0:T(8,128)(2,1)S(1)}, bf16[512,128]{1,0:T(8,128)(2,1)S(1)}, u32[]{:S(2)}, u32[]{:S(2)}) %collective-permute-start.2) | collective-permute-done | bytes 131104 | tf_op jit(solution)/shard_map/ppermute | solution.py:690
  105.0 4.9 %all-to-all-done.2.earlier_ref.zero_ref = bf16[32,96,128]{2,1,0:T(8,128)(2,1)S(1)} async-done(((bf16[32,96,128]{2,1,0:T(8,128)(2,1)}), bf16[32,96,128]{2,1,0:T(8,128)(2,1)S(1)}, u32[]{:S(2)}, u32[]{:S(2)}) %all-to-all-start.2) | async-done | bytes 786464 | tf_op jit(solution)/shard_map/all_to_all | solution.py:580
  110.0 0.1 shard_map.219
  110.1 21.4 %all_to_all.30.one_ref.back_ref = bf16[32,64,128]{2,1,0:T(8,128)(2,1)S(1)} all-to-all(bf16[32,64,128]{2,1,0:T(8,128)(2,1)S(1)} %shard_map.219), channel_id=1, replica_groups=mesh['rows'=32,'feat'=8] {'rows'}, dimensions={0} | all-to-all | bytes 1048576 | tf_op jit(solution)/shard_map/all_to_all | solution.py:580
  131.5 0.9 shard_map.221
  132.3 4.8 %all-to-all-start.4 = ((bf16[32,64,128]{2,1,0:T(8,128)(2,1)}), bf16[32,64,128]{2,1,0:T(8,128)(2,1)S(1)}, u32[]{:S(2)}, u32[]{:S(2)}) async-start(bf16[32,64,128]{2,1,0:T(8,128)(2,1)} %shard_map.221), calls=%async_computation.4 | async-start | bytes 1048576 | tf_op jit(solution)/shard_map/all_to_all | solution.py:580
  137.2 1.6 shard_map.220
  138.8 14.9 %all-to-all-done.4.back_ref = bf16[32,64,128]{2,1,0:T(8,128)(2,1)S(1)} async-done(((bf16[32,64,128]{2,1,0:T(8,128)(2,1)}), bf16[32,64,128]{2,1,0:T(8,128)(2,1)S(1)}, u32[]{:S(2)}, u32[]{:S(2)}) %all-to-all-start.4) | async-done | bytes 524320 | tf_op jit(solution)/shard_map/all_to_all | solution.py:580
  153.7 0.1 shard_map.223
  153.8 12.2 %all_to_all.31.mine_ref = bf16[4,512,128]{2,1,0:T(8,128)(2,1)S(1)} all-to-all(bf16[4,512,128]{2,1,0:T(8,128)(2,1)S(1)} %shard_map.223), channel_id=1, replica_groups={{0,2,4,6},{1,3,5,7},{8,10,12,14},{9,11,13,15},{16,18,20,22},{17,19,21,2..., dimensions={0} | all-to-all | bytes 1048576 | tf_op jit(solution)/shard_map/all_to_all | solution.py:666
  165.9 1.8 %shard_map.222 = bf16[8,64,384]{2,1,0:T(8,128)(2,1)} custom-call(s32[32]{0:T(128)S(1)} %broadcast_add_fusion.asked_ref, f32[8,96,128]{2,1,0:T(8,128)S(1)} %get-tuple-element.48.zero_ref, f32[8,48,128]{2,1,0:T(8,128)S(1)} %get-tuple-element.49.one_ref, bf16[32,64,128]{2,1,0:T(8,128)(2,1)S(1)} %all-to-all-done.4.back_ref), custom_call_target="tpu_custom_call" | custom-call | flops 1000000000 | bytes 4194304 | tf_op jit(solution)/shard_map/pallas_call | solution.py:512
  167.8 0.1 collective-permute-done.3.got_ref
  167.8 1.4 shard_map.224
  (33 shorter events, 0.1 us)
Async XLA Ops:
  1.9 19.9 %all-to-all-start = ((s32[32,1,16]{2,1,0:T(1,128)}), s32[32,1,16]{2,1,0:T(1,128)S(1)}, u32[]{:S(2)}, u32[]{:S(2)}) async-start(s32[32,1,16]{2,1,0:T(1,128)} %broadcast_in_dim.15), calls=%async_computation | async-start | bytes 32768 | tf_op jit(solution)/shard_map/all_to_all | solution.py:580
  23.7 6.0 %copy-start.7 = (bf16[192,768]{1,0:T(8,128)(2,1)S(1)}, bf16[192,768]{1,0:T(8,128)(2,1)}, u32[]{:S(2)}) copy-start(bf16[192,768]{1,0:T(8,128)(2,1)} %w_up_ref.1) | copy-start | bytes 884740
  23.7 6.0 %copy-start.8 = (bf16[768,192]{0,1:T(8,128)(2,1)S(1)}, bf16[768,192]{0,1:T(8,128)(2,1)}, u32[]{:S(2)}) copy-start(bf16[768,192]{0,1:T(8,128)(2,1)} %param.27) | copy-start | bytes 884740
  23.7 6.0 %copy-start.9 = (bf16[128,384]{1,0:T(8,128)(2,1)S(1)}, bf16[128,384]{1,0:T(8,128)(2,1)}, u32[]{:S(2)}) copy-start(bf16[128,384]{1,0:T(8,128)(2,1)} %test_ref.1) | copy-start | bytes 294916
  23.7 6.0 %copy-start.10 = (bf16[128,384]{1,0:T(8,128)(2,1)S(1)}, bf16[128,384]{1,0:T(8,128)(2,1)}, u32[]{:S(2)}) copy-start(bf16[128,384]{1,0:T(8,128)(2,1)} %cot_ref.1) | copy-start | bytes 294916
  23.7 6.0 %copy-start.11 = (bf16[192,192]{1,0:T(8,128)(2,1)S(1)}, bf16[192,192]{1,0:T(8,128)(2,1)}, u32[]{:S(2)}) copy-start(bf16[192,192]{1,0:T(8,128)(2,1)} %w_query_ref.1) | copy-start | bytes 221188
  23.8 6.0 %copy-start.12 = (bf16[192,192]{1,0:T(8,128)(2,1)S(1)}, bf16[192,192]{1,0:T(8,128)(2,1)}, u32[]{:S(2)}) copy-start(bf16[192,192]{1,0:T(8,128)(2,1)} %w_key_ref.1) | copy-start | bytes 221188
  23.8 6.0 %copy-start.13 = (bf16[192,192]{1,0:T(8,128)(2,1)S(1)}, bf16[192,192]{1,0:T(8,128)(2,1)}, u32[]{:S(2)}) copy-start(bf16[192,192]{1,0:T(8,128)(2,1)} %w_value_ref.1) | copy-start | bytes 221188
  23.8 6.0 %copy-start.14 = (bf16[192,192]{1,0:T(8,128)(2,1)S(1)}, bf16[192,192]{1,0:T(8,128)(2,1)}, u32[]{:S(2)}) copy-start(bf16[192,192]{1,0:T(8,128)(2,1)} %w_out_ref.1) | copy-start | bytes 221188
  23.8 6.0 %copy-start.16 = (f32[192]{0:T(256)S(1)}, f32[192]{0:T(256)}, u32[]{:S(2)}) copy-start(f32[192]{0:T(256)} %param.20) | copy-start | bytes 2308
  23.8 6.0 %copy-start.17 = (f32[192]{0:T(256)S(1)}, f32[192]{0:T(256)}, u32[]{:S(2)}) copy-start(f32[192]{0:T(256)} %param.22) | copy-start | bytes 2308
  23.8 6.0 %copy-start.18 = (f32[192]{0:T(256)S(1)}, f32[192]{0:T(256)}, u32[]{:S(2)}) copy-start(f32[192]{0:T(256)} %param.25) | copy-start | bytes 2308
  23.8 6.0 %copy-start.19 = (f32[192]{0:T(256)S(1)}, f32[192]{0:T(256)}, u32[]{:S(2)}) copy-start(f32[192]{0:T(256)} %param.28) | copy-start | bytes 2308
  23.8 10.7 %copy-start.20 = (s32[1,16]{1,0:T(1,128)S(1)}, s32[1,16]{1,0:T(1,128)}, u32[]{:S(2)}) copy-start(s32[1,16]{1,0:T(1,128)} %param.18) | copy-start | bytes 196
  23.9 43.9 %all-to-all-start.1 = ((bf16[32,64,384]{2,1,0:T(8,128)(2,1)}), bf16[32,64,384]{2,1,0:T(8,128)(2,1)}, u32[]{:S(2)}, u32[]{:S(2)}) async-start(bf16[32,64,384]{2,1,0:T(8,128)(2,1)} %shard_map.214), calls=%async_computation.1 | async-start | bytes 3145728 | tf_op jit(solution)/shard_map/all_to_all | solution.py:580
  30.4 1.0 copy-start
  31.4 0.9 copy-start.1
  32.3 0.9 copy-start.2
  33.2 0.8 copy-start.3
  34.0 0.6 copy-start.15
  81.6 6.1 %copy-start.21 = (bf16[2048,128]{1,0:T(8,128)(2,1)S(1)}, bf16[2048,128]{1,0:T(8,128)(2,1)}, u32[]{:S(2)}) copy-start(bf16[2048,128]{1,0:T(8,128)(2,1)} %get-tuple-element.42) | copy-start | bytes 1572868
  81.6 8.3 %copy-start.4 = (bf16[2048,128]{1,0:T(8,128)(2,1)S(1)}, bf16[2048,128]{1,0:T(8,128)(2,1)}, u32[]{:S(2)}) copy-start(bf16[2048,128]{1,0:T(8,128)(2,1)} %get-tuple-element.41.keep_ref) | copy-start | bytes 1572868
  81.6 28.4 %copy-start.6 = (bf16[32,48,128]{2,1,0:T(8,128)(2,1)S(1)}, bf16[32,48,128]{2,1,0:T(8,128)(2,1)}, u32[]{:S(2)}) copy-start(bf16[32,48,128]{2,1,0:T(8,128)(2,1)} %get-tuple-element.47.one_ref) | copy-start | bytes 1179652
  81.6 28.4 %all-to-all-start.2 = ((bf16[32,96,128]{2,1,0:T(8,128)(2,1)}), bf16[32,96,128]{2,1,0:T(8,128)(2,1)S(1)}, u32[]{:S(2)}, u32[]{:S(2)}) async-start(bf16[32,96,128]{2,1,0:T(8,128)(2,1)} %get-tuple-element.40), calls=%async_computation.2 | async-start | bytes 1572864 | tf_op jit(solution)/shard_map/all_to_all | solution.py:580
  87.7 2.2 %collective-permute-start = (bf16[2048,128]{1,0:T(8,128)(2,1)S(1)}, bf16[2048,128]{1,0:T(8,128)(2,1)S(1)}, u32[]{:S(2)}, u32[]{:S(2)}) collective-permute-start(bf16[2048,128]{1,0:T(8,128)(2,1)S(1)} %copy-done.21), channel_id=1, source_target_pairs={{0,1},{1,0},{2,3},{3,2},{4,5},{5,4},{6,7},{7,6},{8,9},{9,8},{10,11... | collective-permute-start | bytes 1572872 | tf_op jit(solution)/shard_map/ppermute | solution.py:690
  90.0 8.4 %collective-permute-start.1 = (bf16[1024,128]{1,0:T(8,128)(2,1)S(1)}, bf16[1024,128]{1,0:T(8,128)(2,1)S(1)}, u32[]{:S(2)}, u32[]{:S(2)}) collective-permute-start(bf16[1024,128]{1,0:T(8,128)(2,1)S(1)} %get-tuple-element.44), channel_id=1, source_target_pairs={{0,2},{1,3},{2,0},{3,1},{4,6},{5,7},{6,4},{7,5},{8,10},{9,11},{10,... | collective-permute-start | bytes 786440 | tf_op jit(solution)/shard_map/ppermute | solution.py:690
  98.5 33.0 %copy-start.5 = (bf16[32,48,128]{2,1,0:T(8,128)(2,1)S(1)}, bf16[32,48,128]{2,1,0:T(8,128)(2,1)}, u32[]{:S(2)}) copy-start(bf16[32,48,128]{2,1,0:T(8,128)(2,1)} %get-tuple-element.50.two_ref) | copy-start | bytes 1179652
  98.5 6.6 %collective-permute-start.2 = (bf16[512,128]{1,0:T(8,128)(2,1)S(1)}, bf16[512,128]{1,0:T(8,128)(2,1)S(1)}, u32[]{:S(2)}, u32[]{:S(2)}) collective-permute-start(bf16[512,128]{1,0:T(8,128)(2,1)S(1)} %get-tuple-element.46), channel_id=1, source_target_pairs={{0,4},{1,5},{2,6},{3,7},{4,0},{5,1},{6,2},{7,3},{8,12},{9,13},{10,... | collective-permute-start | bytes 393224 | tf_op jit(solution)/shard_map/ppermute | solution.py:690
  132.3 21.4 %all-to-all-start.4 = ((bf16[32,64,128]{2,1,0:T(8,128)(2,1)}), bf16[32,64,128]{2,1,0:T(8,128)(2,1)S(1)}, u32[]{:S(2)}, u32[]{:S(2)}) async-start(bf16[32,64,128]{2,1,0:T(8,128)(2,1)} %shard_map.221), calls=%async_computation.4 | async-start | bytes 1048576 | tf_op jit(solution)/shard_map/all_to_all | solution.py:580
  165.9 1.9 %collective-permute-start.3 = (bf16[4,512,128]{2,1,0:T(8,128)(2,1)S(1)}, bf16[4,512,128]{2,1,0:T(8,128)(2,1)S(1)}, u32[]{:S(2)}, u32[]{:S(2)}) collective-permute-start(bf16[4,512,128]{2,1,0:T(8,128)(2,1)S(1)} %all_to_all.31.mine_ref), channel_id=1, source_target_pairs={{0,1},{1,0},{2,3},{3,2},{4,5},{5,4},{6,7},{7,6},{8,9},{9,8},{10,11... | collective-permute-start | bytes 1572872 | tf_op jit(solution)/shard_map/ppermute | solution.py:690

commit v5 on v4

--- a/solution.py
+++ b/solution.py
@@ -21,6 +21,7 @@
 ABSENT_ABOVE = 7.0
 MASKED = -30000.0
 GRAD_ROWS = 4096
+Z = 8
 
 bf16 = jnp.bfloat16
 f32 = jnp.float32
@@ -38,11 +39,64 @@
     return lax.dot_general(a, b, (((0,), (0,)), ((), ())), preferred_element_type=f32)
 
 
-def pick_kernel(asked_ref, cells_ref, out_ref, sem):
-    def body(slot, carry):
-        pltpu.make_async_copy(
-            cells_ref.at[jnp.maximum(asked_ref[slot], 0)], out_ref.at[slot], sem
-        ).start()
+def mark_kernel(
+    train_hbm,
+    present_hbm,
+    retrieved_hbm,
+    marked_ref,
+    requests_ref,
+    train_ref,
+    present_ref,
+    retrieved_ref,
+    sems,
+):
+    copies = [
+        pltpu.make_async_copy(source, target, sems.at[i])
+        for i, (source, target) in enumerate(
+            ((train_hbm, train_ref), (present_hbm, present_ref), (retrieved_hbm, retrieved_ref))
+        )
+    ]
+    for copy in copies:
+        copy.start()
+    for copy in copies:
+        copy.wait()
+    wide = train_ref.shape[1]
+    feats, rows = present_ref.shape
+    present = jnp.concatenate(
+        [present_ref[...].astype(f32), jnp.zeros((16 - feats, rows), f32)], axis=0
+    ).astype(bf16)
+    feature = lax.broadcasted_iota(jnp.int32, (16, wide), 0)
+    lane = lax.broadcasted_iota(jnp.int32, (16, wide), 1)
+    mine = (lane >= feature * E) & (lane < (feature + 1) * E)
+    mask = dot_tn(present, jnp.where(mine, 1.0, 0.0).astype(bf16))
+    marked = jnp.where(mask > 0.5, train_ref[...].astype(f32), ABSENT).astype(bf16)
+    marked_ref[...] = marked.reshape(marked_ref.shape)
+    requests_ref[...] = jnp.broadcast_to(retrieved_ref[...][None], requests_ref.shape)
+
+
+def arrived_kernel(in_ref, out_ref):
+    pass
+
+
+def asked_kernel(blocks, served_ref, table_ref, mirrored_ref, out_ref):
+    table = table_ref[:, 0, :]
+    owner = lax.div(table, blocks)
+    wanted = lax.rem(table, blocks) + 1
+    part = lax.broadcasted_iota(jnp.int32, out_ref.shape, 1)
+    own, mirrored = (
+        jnp.sum(jnp.where(owner == served_ref[i], wanted, 0), axis=1, keepdims=True) - 1
+        for i in range(2)
+    )
+    out_ref[...] = jnp.where(part == 0, own, mirrored)
+
+
+def pick_kernel(asked_ref, base_ref, own_ref, mirrored_ref, out_ref, sem):
+    def body(k, carry):
+        row = (k // 4) * Z + lax.rem(base_ref[0] + lax.rem(k, 4), Z)
+        for part, ref in enumerate((own_ref, mirrored_ref)):
+            pltpu.make_async_copy(
+                ref.at[jnp.maximum(asked_ref[row, part], 0)], out_ref.at[k, part], sem
+            ).start()
         return carry
 
     lax.fori_loop(0, out_ref.shape[0], body, 0)
@@ -145,6 +199,7 @@
 
 
 def prepare_kernel(
+    asked_ref,
     test_ref,
     cot_ref,
     w_query_ref,
@@ -201,6 +256,7 @@
 
 def main_kernel(
     tile,
+    source_ref,
     owner_ref,
     core_ref,
     rec_hbm,
@@ -243,7 +299,7 @@
 
     def gather(j, carry):
         pltpu.make_async_copy(
-            rec_hbm.at[owner_ref[j]],
+            rec_hbm.at[source_ref[j]],
             cells_s.at[pl.ds(pl.multiple_of(j * BLK, BLK), BLK), :],
             rec_sem,
         ).start()
@@ -501,7 +557,7 @@
 ANY_SPEC = pl.BlockSpec(memory_space=pl.ANY)
 HBM_SPEC = pl.BlockSpec(memory_space=pltpu.HBM)
 PARAMS = pltpu.CompilerParams(vmem_limit_bytes=12 * MIB)
-MAIN_PARAMS = pltpu.CompilerParams(vmem_limit_bytes=62 * MIB)
+BIG_PARAMS = pltpu.CompilerParams(vmem_limit_bytes=62 * MIB)
 
 
 def shape(dims, dtype=bf16):
@@ -520,7 +576,7 @@
     )(*scalars, *args)
 
 
-def prepare(test_cells, cotangent, weights):
+def prepare(asked, test_cells, cotangent, weights):
     w_query, q_gain, w_key, k_gain, w_value, w_out, gain_one, w_up, w_down, gain_two = weights
     rows, wide = test_cells.shape
     ht = H * rows
@@ -534,10 +590,10 @@
     args = (test_cells, cotangent, w_query, w_key, w_value, w_out, w_up, w_down.T) + tuple(
         gain.reshape(1, E) for gain in (q_gain, k_gain, gain_one, gain_two)
     )
-    return small_call(prepare_kernel, shapes, *args)
-
-
-def main_call(owner_of, core, rec, prepared, rows, tile):
+    return small_call(prepare_kernel, shapes, *args, scalars=(asked,))
+
+
+def main_call(source, owner_of, core, rec, prepared, rows, tile):
     count = owner_of.shape[0]
     keys = count * BLK
     owners, _, wide = rec.shape
@@ -553,7 +609,7 @@
             pltpu.HBM((GRAD_ROWS // 2, 128), bf16),
             pltpu.HBM((GRAD_ROWS // 2, 128), bf16),
         ),
-        in_specs=[SMEM_SPEC] * 2 + [HBM_SPEC] * (1 + len(prepared)),
+        in_specs=[SMEM_SPEC] * 3 + [HBM_SPEC] * (1 + len(prepared)),
         out_specs=tuple(vmem_specs(2)) + (HBM_SPEC,) * 5,
         scratch_shapes=[pltpu.VMEM(x.shape, x.dtype) for x in prepared]
         + [
@@ -572,12 +628,34 @@
             pltpu.SemaphoreType.DMA,
             pltpu.SemaphoreType.DMA((len(prepared),)),
         ],
-        compiler_params=MAIN_PARAMS,
-    )(owner_of, core, rec, *prepared)
+        compiler_params=BIG_PARAMS,
+    )(source, owner_of, core, rec, *prepared)
 
 
 def swap(x, axis):
     return lax.all_to_all(x, axis, split_axis=0, concat_axis=0, tiled=True)
+
+
+def mirror_pairs(owners, groups):
+    pairs = []
+    for row in range(owners):
+        for feat in range(groups):
+            z = row % Z
+            mirror = row - z + (7 + 4 * (feat % 2) - z) % Z
+            pairs.append((row * groups + feat, mirror * groups + feat))
+    return pairs
+
+
+def half_rings(owners, groups):
+    return [
+        [
+            (y * Z + (4 * half + place + 2 * (feat % 2)) % Z) * groups + feat
+            for y in range(owners // Z)
+            for place in range(4)
+        ]
+        for feat in range(groups)
+        for half in range(2)
+    ]
 
 
 def on_device(
@@ -602,30 +680,68 @@
     rows, wide = test_cells.shape
     count = retrieved.shape[1]
     owner_of = retrieved[0] // blocks_own
-    table = swap(jnp.broadcast_to(retrieved[None], (owners, 1, count)), "rows")
-    table = table.reshape(owners, count)
-    mine = table // blocks_own == lax.axis_index("rows")
-    asked = jnp.sum(jnp.where(mine, table % blocks_own + 1, 0), axis=1) - 1
-    mask = jnp.repeat(train_present.T != 0, E, axis=1)
-    marked = jnp.where(mask, train_cells, jnp.asarray(ABSENT, bf16)).reshape(blocks_own, BLK, wide)
+    me = lax.axis_index("rows")
+    feat = lax.axis_index("feat")
+    core, low, high = ((feat // bit % 2).reshape(1) for bit in (1, 2, 4))
+
+    marked, requests = pl.pallas_call(
+        mark_kernel,
+        out_shape=(shape((blocks_own, BLK, wide)), shape((owners, 1, count), jnp.int32)),
+        in_specs=[HBM_SPEC] * 3,
+        out_specs=tuple(vmem_specs(2)),
+        scratch_shapes=[
+            pltpu.VMEM(x.shape, x.dtype) for x in (train_cells, train_present, retrieved)
+        ]
+        + [pltpu.SemaphoreType.DMA((3,))],
+        compiler_params=BIG_PARAMS,
+    )(train_cells, train_present, retrieved)
+    mirrored = lax.ppermute(marked, ("rows", "feat"), mirror_pairs(owners, groups))
+    mirrored = pl.pallas_call(
+        arrived_kernel,
+        out_shape=shape(mirrored.shape),
+        in_specs=[ANY_SPEC],
+        out_specs=ANY_SPEC,
+        input_output_aliases={0: 0},
+        compiler_params=PARAMS,
+        cost_estimate=BUSY,
+    )(mirrored)
+    served = jnp.stack([me, me - me % Z + (7 + 4 * core[0] - me % Z) % Z])
+    asked_both = pl.pallas_call(
+        functools.partial(asked_kernel, blocks_own),
+        out_shape=shape((owners, 2), jnp.int32),
+        in_specs=[SMEM_SPEC] + vmem_specs(1) + [ANY_SPEC],
+        out_specs=vmem_specs(1)[0],
+        compiler_params=PARAMS,
+    )(served, swap(requests, "rows"), mirrored)
+    asked = asked_both[:, 0]
+    half = (me % Z - 2 * core[0]) % Z // 4
     to_send = pl.pallas_call(
         pick_kernel,
-        out_shape=shape((owners, BLK, wide)),
-        in_specs=[SMEM_SPEC] + vmem_specs(1),
+        out_shape=shape((owners // 2, 2, BLK, wide)),
+        in_specs=[SMEM_SPEC] * 2 + [ANY_SPEC] * 2,
         out_specs=ANY_SPEC,
         scratch_shapes=[pltpu.SemaphoreType.DMA],
         compiler_params=PARAMS,
-    )(asked, marked)
-    rec = swap(to_send, "rows")
+    )(asked_both, (half * 4 + 2 * core[0]).reshape(1), marked, mirrored)
+    rec = lax.all_to_all(
+        to_send.reshape(owners // 2, 2 * BLK, wide),
+        ("rows", "feat"),
+        split_axis=0,
+        concat_axis=0,
+        tiled=True,
+        axis_index_groups=half_rings(owners, groups),
+    ).reshape(owners, BLK, wide)
+    place = (owner_of % Z - 2 * core[0]) % Z
+    near = place // 4 == half
+    source = (owner_of // Z * 4 + jnp.where(near, place, 7 - place) % 4) * 2 + jnp.where(near, 0, 1)
     prepared = prepare(
+        asked,
         test_cells,
         cotangent,
         (w_query, q_gain, w_key, k_gain, w_value, w_out, gain_one, w_up, w_down, gain_two),
     )
-    feat = lax.axis_index("feat")
-    core, low, high = ((feat // bit % 2).reshape(1) for bit in (1, 2, 4))
     out_cells, grad_test, zero, one, two, keep, give = main_call(
-        owner_of, core, rec, prepared, rows, 1024
+        source, owner_of, core, rec, prepared, rows, 1024
     )
 
     back_zero = swap(zero, "rows")

time: 171 us -> 167 us (0.977)
  waiting for transfers between devices: 71.2 us -> 63.3 us
  Pallas kernels: 22 us -> 25.7 us
  local copies, waits for them, and re-layouts: 6.95 us -> 4.4 us
  starting transfers between devices: 33 us -> 35.4 us
    all_to_all x4 -> x3, waiting for transfers between devices: 58.9 us -> 26.4 us  [swap(): return lax.all_to_all(x, axis, split_axis=0, concat_axis=0, tiled=True)]
    all_to_all x0 -> x1, waiting for transfers between devices: none -> 21.2 us  [on_device(): lax.all_to_all(to_send.reshape(owners // 2, 2 * BLK, wide), ('rows', 'fea...]
    all_to_all x4 -> x3, starting transfers between devices: 28.1 us -> 18.5 us  [swap(): return lax.all_to_all(x, axis, split_axis=0, concat_axis=0, tiled=True)]
    ppermute x0 -> x1, starting transfers between devices: none -> 5.93 us  [on_device(): lax.ppermute(marked, ('rows', 'feat'), mirror_pairs(owners, groups))]
    all_to_all x0 -> x1, starting transfers between devices: none -> 5.71 us  [on_device(): lax.all_to_all(to_send.reshape(owners // 2, 2 * BLK, wide), ('rows', 'fea...]
    ppermute x0 -> x1, waiting for transfers between devices: none -> 3.58 us  [on_device(): lax.ppermute(marked, ('rows', 'feat'), mirror_pairs(owners, groups))]
    pallas_call x1 -> x4, Pallas kernels: 1.74 us -> 4.82 us  [the longest x1 2.07 us: on_device(): pl.pallas_call(mark_kernel, out_shape=(shape((blocks_own, BLK, wide)), sh...]
    unnamed x45 -> x46, local copies, waits for them, and re-layouts: 5.47 us -> 4.29 us
  transfers between devices with their start and end apart: 8 -> 9, of which waited for: 8 -> 9; matrix products, arithmetic and copies ran while one was open for 2% -> 0% of each run, Pallas kernels for 2% -> 3%
where the time goes in v5:
time: 167 us; the launch traced here: 165 us
  waiting for transfers between devices  63.3 us (38%)
  starting transfers between devices  35.4 us (21%)
  blocking collectives  35 us (21%)
  Pallas kernels  25.7 us (15%)
  local copies, waits for them, and re-layouts  4.4 us (3%)
    all_to_all x3, waiting for transfers between devices, swap(): return lax.all_to_all(x, axis, split_axis=0, concat_axis=0, tiled=True)  26.4 us
    all_to_all x1, blocking collectives, swap(): return lax.all_to_all(x, axis, split_axis=0, concat_axis=0, tiled=True)  22.8 us
    all_to_all x1, waiting for transfers between devices, on_device(): lax.all_to_all(to_send.reshape(owners // 2, 2 * BLK, wide), ('rows', 'fea...  21.2 us
    all_to_all x3, starting transfers between devices, swap(): return lax.all_to_all(x, axis, split_axis=0, concat_axis=0, tiled=True)  18.5 us
    pallas_call x1, Pallas kernels, main_call(): pl.pallas_call(functools.partial(main_kernel, tile), out_shape=(shape((ro...  13.8 us
    all_to_all x1, blocking collectives, on_device(): lax.all_to_all(copies, 'feat', split_axis=0, concat_axis=0, tiled=True, a...  12.2 us
    ppermute x4, waiting for transfers between devices, flip(): return lax.ppermute(x, 'feat', [(i, i ^ bit) for i in range(count)])  12.2 us
    pallas_call x7, Pallas kernels, small_call(): pl.pallas_call(kernel, out_shape=out_shape, in_specs=[SMEM_SPEC] * len(sc...  6.9 us
  transfers between devices with their start and end apart: 9, of which 9 were waited for; matrix products, arithmetic and copies ran while one was open for 0% of the time, Pallas kernels for 3%

profile of v5, /device:TPU:32, one launch (start us, length us, event | category | flops | bytes accessed | tf_op | source)
XLA Modules:
  0.0 165.4 jit_solution(9762953418330861789)
XLA Ops:
  0.6 2.1 %shard_map.214 = (bf16[8,64,384]{2,1,0:T(8,128)(2,1)}, s32[32,1,16]{2,1,0:T(1,128)}) custom-call(bf16[512,384]{1,0:T(8,128)(2,1)} %train_hbm.1, s32[2,512]{1,0:T(2,128)} %present_hbm.1, s32[1,16]{1,0:T(1,128)} %retrieved_hbm.1), custom_call_target="tpu_custom_call" | custom-call | tf_op jit(solution)/shard_map/pallas_call | solution.py:687
  2.7 5.9 %collective-permute-start = (bf16[8,64,384]{2,1,0:T(8,128)(2,1)}, bf16[8,64,384]{2,1,0:T(8,128)(2,1)S(1)}, u32[]{:S(2)}, u32[]{:S(2)}) collective-permute-start(bf16[8,64,384]{2,1,0:T(8,128)(2,1)} %get-tuple-element.36.own_ref), channel_id=1, source_target_pairs={{0,56},{1,25},{2,58},{3,27},{4,60},{5,29},{6,62},{7,31},{8,48},{9,... | collective-permute-start | bytes 1179656 | tf_op jit(solution)/shard_map/ppermute | solution.py:698
  8.7 6.5 %all-to-all-start = ((s32[32,1,16]{2,1,0:T(1,128)}), s32[32,1,16]{2,1,0:T(1,128)S(1)}, u32[]{:S(2)}, u32[]{:S(2)}) async-start(s32[32,1,16]{2,1,0:T(1,128)} %get-tuple-element.35), calls=%async_computation | async-start | bytes 32768 | tf_op jit(solution)/shard_map/all_to_all | solution.py:636
  15.3 0.1 pad_add_fusion.served_ref
  15.4 3.6 %collective-permute-done.in_ref = bf16[8,64,384]{2,1,0:T(8,128)(2,1)S(1)} collective-permute-done((bf16[8,64,384]{2,1,0:T(8,128)(2,1)}, bf16[8,64,384]{2,1,0:T(8,128)(2,1)S(1)}, u32[]{:S(2)}, u32[]{:S(2)}) %collective-permute-start) | collective-permute-done | bytes 393248 | tf_op jit(solution)/shard_map/ppermute | solution.py:698
  18.9 4.8 %all-to-all-done.table_ref = s32[32,1,16]{2,1,0:T(1,128)S(1)} async-done(((s32[32,1,16]{2,1,0:T(1,128)}), s32[32,1,16]{2,1,0:T(1,128)S(1)}, u32[]{:S(2)}, u32[]{:S(2)}) %all-to-all-start) | async-done | bytes 2080 | tf_op jit(solution)/shard_map/all_to_all | solution.py:636
  23.8 0.7 shard_map.216.asked_ref
  24.5 2.0 %shard_map.217 = bf16[16,2,64,384]{3,2,1,0:T(8,128)(2,1)} custom-call(s32[32,2]{1,0:T(8,128)S(1)} %shard_map.216.asked_ref, s32[1]{0:T(128)} %bitcast.4.base_ref, bf16[8,64,384]{2,1,0:T(8,128)(2,1)S(1)} %copy-done.6, bf16[8,64,384]{2,1,0:T(8,128)(2,1)S(1)} %shard_map.215.mirrored_ref), custom_call_target="tpu_custom_call" | custom-call | tf_op jit(solution)/shard_map/pallas_call | solution.py:718
  26.5 0.0 copy-start.8
  26.5 0.0 copy-start.9
  26.6 0.0 copy-start.11
  26.6 0.0 copy-start.12
  26.6 0.0 copy-start.15
  26.6 0.0 copy-start.17
  26.7 0.0 copy-start.20
  26.7 5.7 %all-to-all-start.1 = ((bf16[16,128,384]{2,1,0:T(8,128)(2,1)}), bf16[16,128,384]{2,1,0:T(8,128)(2,1)}, u32[]{:S(2)}, u32[]{:S(2)}) async-start(bf16[16,128,384]{2,1,0:T(8,128)(2,1)} %bitcast.5), calls=%async_computation.1 | async-start | bytes 3145728 | tf_op jit(solution)/shard_map/all_to_all | solution.py:726
  32.4 0.6 fusion.1
  33.0 0.1 slice_reduce_fusion.asked_ref
  33.2 1.1 shard_map.218
  34.3 1.0 copy-done
  35.3 0.9 copy-done.1
  36.2 0.9 copy-done.2
  37.1 0.8 copy-done.3
  37.9 0.6 copy-done.16
  38.5 21.2 %all-to-all-done.1 = bf16[16,128,384]{2,1,0:T(8,128)(2,1)} async-done(((bf16[16,128,384]{2,1,0:T(8,128)(2,1)}), bf16[16,128,384]{2,1,0:T(8,128)(2,1)}, u32[]{:S(2)}, u32[]{:S(2)}) %all-to-all-start.1) | async-done | bytes 1572896 | tf_op jit(solution)/shard_map/all_to_all | solution.py:726
  59.7 13.8 %shard_map.219 = (bf16[128,384]{1,0:T(8,128)(2,1)}, bf16[128,384]{1,0:T(8,128)(2,1)}, bf16[32,96,128]{2,1,0:T(8,128)(2,1)}, bf16[32,48,128]{2,1,0:T(8,128)(2,1)}...) custom-call(s32[16]{0:T(128)} %get-tuple-element.61.source_ref, ...), custom_call_target="tpu_custom_call" | custom-call | tf_op jit(solution)/shard_map/pallas_call | solution.py:601
  73.5 0.0 copy-start.4
  73.5 7.1 %all-to-all-start.2 = ((bf16[32,96,128]{2,1,0:T(8,128)(2,1)}), bf16[32,96,128]{2,1,0:T(8,128)(2,1)S(1)}, u32[]{:S(2)}, u32[]{:S(2)}) async-start(bf16[32,96,128]{2,1,0:T(8,128)(2,1)} %get-tuple-element.44), calls=%async_computation.2 | async-start | bytes 1572864 | tf_op jit(solution)/shard_map/all_to_all | solution.py:636
  80.7 0.5 collective-permute-start.1
  81.2 1.7 %collective-permute-done.1.got_ref = bf16[2048,128]{1,0:T(8,128)(2,1)S(1)} collective-permute-done((bf16[2048,128]{1,0:T(8,128)(2,1)S(1)}, bf16[2048,128]{1,0:T(8,128)(2,1)S(1)}, u32[]{:S(2)}, u32[]{:S(2)}) %collective-permute-start.1) | collective-permute-done | bytes 524320 | tf_op jit(solution)/shard_map/ppermute | solution.py:806
  82.9 0.1 shard_map.220
  83.0 1.6 collective-permute-start.2
  84.6 6.9 %collective-permute-done.2.got_ref = bf16[1024,128]{1,0:T(8,128)(2,1)S(1)} collective-permute-done((bf16[1024,128]{1,0:T(8,128)(2,1)S(1)}, bf16[1024,128]{1,0:T(8,128)(2,1)S(1)}, u32[]{:S(2)}, u32[]{:S(2)}) %collective-permute-start.2) | collective-permute-done | bytes 262176 | tf_op jit(solution)/shard_map/ppermute | solution.py:806
  91.5 0.1 shard_map.221
  91.6 3.1 %collective-permute-start.3 = (bf16[512,128]{1,0:T(8,128)(2,1)S(1)}, bf16[512,128]{1,0:T(8,128)(2,1)S(1)}, u32[]{:S(2)}, u32[]{:S(2)}) collective-permute-start(bf16[512,128]{1,0:T(8,128)(2,1)S(1)} %get-tuple-element.50), channel_id=1, source_target_pairs={{0,4},{1,5},{2,6},{3,7},{4,0},{5,1},{6,2},{7,3},{8,12},{9,13},{10,... | collective-permute-start | bytes 393224 | tf_op jit(solution)/shard_map/ppermute | solution.py:806
  94.7 3.4 %collective-permute-done.3.got_ref = bf16[512,128]{1,0:T(8,128)(2,1)S(1)} collective-permute-done((bf16[512,128]{1,0:T(8,128)(2,1)S(1)}, bf16[512,128]{1,0:T(8,128)(2,1)S(1)}, u32[]{:S(2)}, u32[]{:S(2)}) %collective-permute-start.3) | collective-permute-done | bytes 131104 | tf_op jit(solution)/shard_map/ppermute | solution.py:806
  98.2 6.2 %all-to-all-done.2.earlier_ref.zero_ref = bf16[32,96,128]{2,1,0:T(8,128)(2,1)S(1)} async-done(((bf16[32,96,128]{2,1,0:T(8,128)(2,1)}), bf16[32,96,128]{2,1,0:T(8,128)(2,1)S(1)}, u32[]{:S(2)}, u32[]{:S(2)}) %all-to-all-start.2) | async-done | bytes 786464 | tf_op jit(solution)/shard_map/all_to_all | solution.py:636
  104.4 0.1 shard_map.222
  104.5 22.8 %all_to_all.30.one_ref.back_ref = bf16[32,64,128]{2,1,0:T(8,128)(2,1)S(1)} all-to-all(bf16[32,64,128]{2,1,0:T(8,128)(2,1)S(1)} %shard_map.222), channel_id=1, replica_groups=mesh['rows'=32,'feat'=8] {'rows'}, dimensions={0} | all-to-all | bytes 1048576 | tf_op jit(solution)/shard_map/all_to_all | solution.py:636
  127.2 0.9 shard_map.224
  128.1 4.9 %all-to-all-start.4 = ((bf16[32,64,128]{2,1,0:T(8,128)(2,1)}), bf16[32,64,128]{2,1,0:T(8,128)(2,1)S(1)}, u32[]{:S(2)}, u32[]{:S(2)}) async-start(bf16[32,64,128]{2,1,0:T(8,128)(2,1)} %shard_map.224), calls=%async_computation.4 | async-start | bytes 1048576 | tf_op jit(solution)/shard_map/all_to_all | solution.py:636
  133.0 1.6 shard_map.223
  134.5 15.3 %all-to-all-done.4.back_ref = bf16[32,64,128]{2,1,0:T(8,128)(2,1)S(1)} async-done(((bf16[32,64,128]{2,1,0:T(8,128)(2,1)}), bf16[32,64,128]{2,1,0:T(8,128)(2,1)S(1)}, u32[]{:S(2)}, u32[]{:S(2)}) %all-to-all-start.4) | async-done | bytes 524320 | tf_op jit(solution)/shard_map/all_to_all | solution.py:636
  149.9 0.1 shard_map.226
  150.0 12.2 %all_to_all.31.mine_ref = bf16[4,512,128]{2,1,0:T(8,128)(2,1)S(1)} all-to-all(bf16[4,512,128]{2,1,0:T(8,128)(2,1)S(1)} %shard_map.226), channel_id=1, replica_groups={{0,2,4,6},{1,3,5,7},{8,10,12,14},{9,11,13,15},{16,18,20,22},{17,19,21,2..., dimensions={0} | all-to-all | bytes 1048576 | tf_op jit(solution)/shard_map/all_to_all | solution.py:782
  162.2 1.8 %shard_map.225 = bf16[8,64,384]{2,1,0:T(8,128)(2,1)} custom-call(s32[32]{0:T(128)S(1)} %slice_reduce_fusion.asked_ref, f32[8,96,128]{2,1,0:T(8,128)S(1)} %get-tuple-element.52.zero_ref, f32[8,48,128]{2,1,0:T(8,128)S(1)} %get-tuple-element.53.one_ref, bf16[32,64,128]{2,1,0:T(8,128)(2,1)S(1)} %all-to-all-done.4.back_ref), custom_call_target="tpu_custom_call" | custom-call | flops 1000000000 | bytes 4194304 | tf_op jit(solution)/shard_map/pallas_call | solution.py:568
  164.0 0.1 collective-permute-done.4.got_ref
  164.1 1.4 shard_map.227
  (35 shorter events, 0.1 us)
Async XLA Ops:
  2.7 16.2 %collective-permute-start = (bf16[8,64,384]{2,1,0:T(8,128)(2,1)}, bf16[8,64,384]{2,1,0:T(8,128)(2,1)S(1)}, u32[]{:S(2)}, u32[]{:S(2)}) collective-permute-start(bf16[8,64,384]{2,1,0:T(8,128)(2,1)} %get-tuple-element.36.own_ref), channel_id=1, source_target_pairs={{0,56},{1,25},{2,58},{3,27},{4,60},{5,29},{6,62},{7,31},{8,48},{9,... | collective-permute-start | bytes 1179656 | tf_op jit(solution)/shard_map/ppermute | solution.py:698
  8.7 15.1 %all-to-all-start = ((s32[32,1,16]{2,1,0:T(1,128)}), s32[32,1,16]{2,1,0:T(1,128)S(1)}, u32[]{:S(2)}, u32[]{:S(2)}) async-start(s32[32,1,16]{2,1,0:T(1,128)} %get-tuple-element.35), calls=%async_computation | async-start | bytes 32768 | tf_op jit(solution)/shard_map/all_to_all | solution.py:636
  15.4 9.1 %copy-start.6 = (bf16[8,64,384]{2,1,0:T(8,128)(2,1)S(1)}, bf16[8,64,384]{2,1,0:T(8,128)(2,1)}, u32[]{:S(2)}) copy-start(bf16[8,64,384]{2,1,0:T(8,128)(2,1)} %get-tuple-element.36.own_ref) | copy-start | bytes 1179652
  26.5 5.9 %copy-start.21 = (s32[1,16]{1,0:T(1,128)S(1)}, s32[1,16]{1,0:T(1,128)}, u32[]{:S(2)}) copy-start(s32[1,16]{1,0:T(1,128)} %retrieved_hbm.1) | copy-start | bytes 196
  26.5 6.5 %copy-start.8 = (bf16[192,768]{1,0:T(8,128)(2,1)S(1)}, bf16[192,768]{1,0:T(8,128)(2,1)}, u32[]{:S(2)}) copy-start(bf16[192,768]{1,0:T(8,128)(2,1)} %w_up_ref.1) | copy-start | bytes 884740
  26.5 6.5 %copy-start.9 = (bf16[768,192]{0,1:T(8,128)(2,1)S(1)}, bf16[768,192]{0,1:T(8,128)(2,1)}, u32[]{:S(2)}) copy-start(bf16[768,192]{0,1:T(8,128)(2,1)} %param.27) | copy-start | bytes 884740
  26.6 6.5 %copy-start.10 = (bf16[128,384]{1,0:T(8,128)(2,1)S(1)}, bf16[128,384]{1,0:T(8,128)(2,1)}, u32[]{:S(2)}) copy-start(bf16[128,384]{1,0:T(8,128)(2,1)} %test_ref.1) | copy-start | bytes 294916
  26.6 6.5 %copy-start.11 = (bf16[128,384]{1,0:T(8,128)(2,1)S(1)}, bf16[128,384]{1,0:T(8,128)(2,1)}, u32[]{:S(2)}) copy-start(bf16[128,384]{1,0:T(8,128)(2,1)} %cot_ref.1) | copy-start | bytes 294916
  26.6 6.5 %copy-start.12 = (bf16[192,192]{1,0:T(8,128)(2,1)S(1)}, bf16[192,192]{1,0:T(8,128)(2,1)}, u32[]{:S(2)}) copy-start(bf16[192,192]{1,0:T(8,128)(2,1)} %w_query_ref.1) | copy-start | bytes 221188
  26.6 6.5 %copy-start.13 = (bf16[192,192]{1,0:T(8,128)(2,1)S(1)}, bf16[192,192]{1,0:T(8,128)(2,1)}, u32[]{:S(2)}) copy-start(bf16[192,192]{1,0:T(8,128)(2,1)} %w_key_ref.1) | copy-start | bytes 221188
  26.6 6.5 %copy-start.14 = (bf16[192,192]{1,0:T(8,128)(2,1)S(1)}, bf16[192,192]{1,0:T(8,128)(2,1)}, u32[]{:S(2)}) copy-start(bf16[192,192]{1,0:T(8,128)(2,1)} %w_value_ref.1) | copy-start | bytes 221188
  26.6 6.5 %copy-start.15 = (bf16[192,192]{1,0:T(8,128)(2,1)S(1)}, bf16[192,192]{1,0:T(8,128)(2,1)}, u32[]{:S(2)}) copy-start(bf16[192,192]{1,0:T(8,128)(2,1)} %w_out_ref.1) | copy-start | bytes 221188
  26.6 6.5 %copy-start.17 = (f32[192]{0:T(256)S(1)}, f32[192]{0:T(256)}, u32[]{:S(2)}) copy-start(f32[192]{0:T(256)} %param.20) | copy-start | bytes 2308
  26.6 6.5 %copy-start.18 = (f32[192]{0:T(256)S(1)}, f32[192]{0:T(256)}, u32[]{:S(2)}) copy-start(f32[192]{0:T(256)} %param.22) | copy-start | bytes 2308
  26.7 6.5 %copy-start.19 = (f32[192]{0:T(256)S(1)}, f32[192]{0:T(256)}, u32[]{:S(2)}) copy-start(f32[192]{0:T(256)} %param.25) | copy-start | bytes 2308
  26.7 6.5 %copy-start.20 = (f32[192]{0:T(256)S(1)}, f32[192]{0:T(256)}, u32[]{:S(2)}) copy-start(f32[192]{0:T(256)} %param.28) | copy-start | bytes 2308
  26.7 33.0 %all-to-all-start.1 = ((bf16[16,128,384]{2,1,0:T(8,128)(2,1)}), bf16[16,128,384]{2,1,0:T(8,128)(2,1)}, u32[]{:S(2)}, u32[]{:S(2)}) async-start(bf16[16,128,384]{2,1,0:T(8,128)(2,1)} %bitcast.5), calls=%async_computation.1 | async-start | bytes 3145728 | tf_op jit(solution)/shard_map/all_to_all | solution.py:726
  34.3 1.0 copy-start
  35.3 0.9 copy-start.1
  36.2 0.9 copy-start.2
  37.1 0.8 copy-start.3
  37.9 0.6 copy-start.16
  73.5 7.2 %copy-start.22 = (bf16[2048,128]{1,0:T(8,128)(2,1)S(1)}, bf16[2048,128]{1,0:T(8,128)(2,1)}, u32[]{:S(2)}) copy-start(bf16[2048,128]{1,0:T(8,128)(2,1)} %get-tuple-element.46) | copy-start | bytes 1572868
  73.5 9.4 %copy-start.4 = (bf16[2048,128]{1,0:T(8,128)(2,1)S(1)}, bf16[2048,128]{1,0:T(8,128)(2,1)}, u32[]{:S(2)}) copy-start(bf16[2048,128]{1,0:T(8,128)(2,1)} %get-tuple-element.45.keep_ref) | copy-start | bytes 1572868
  73.5 30.9 %copy-start.7 = (bf16[32,48,128]{2,1,0:T(8,128)(2,1)S(1)}, bf16[32,48,128]{2,1,0:T(8,128)(2,1)}, u32[]{:S(2)}) copy-start(bf16[32,48,128]{2,1,0:T(8,128)(2,1)} %get-tuple-element.51.one_ref) | copy-start | bytes 1179652
  73.5 30.9 %all-to-all-start.2 = ((bf16[32,96,128]{2,1,0:T(8,128)(2,1)}), bf16[32,96,128]{2,1,0:T(8,128)(2,1)S(1)}, u32[]{:S(2)}, u32[]{:S(2)}) async-start(bf16[32,96,128]{2,1,0:T(8,128)(2,1)} %get-tuple-element.44), calls=%async_computation.2 | async-start | bytes 1572864 | tf_op jit(solution)/shard_map/all_to_all | solution.py:636
  80.7 2.2 %collective-permute-start.1 = (bf16[2048,128]{1,0:T(8,128)(2,1)S(1)}, bf16[2048,128]{1,0:T(8,128)(2,1)S(1)}, u32[]{:S(2)}, u32[]{:S(2)}) collective-permute-start(bf16[2048,128]{1,0:T(8,128)(2,1)S(1)} %copy-done.22), channel_id=1, source_target_pairs={{0,1},{1,0},{2,3},{3,2},{4,5},{5,4},{6,7},{7,6},{8,9},{9,8},{10,11... | collective-permute-start | bytes 1572872 | tf_op jit(solution)/shard_map/ppermute | solution.py:806
  83.0 8.5 %collective-permute-start.2 = (bf16[1024,128]{1,0:T(8,128)(2,1)S(1)}, bf16[1024,128]{1,0:T(8,128)(2,1)S(1)}, u32[]{:S(2)}, u32[]{:S(2)}) collective-permute-start(bf16[1024,128]{1,0:T(8,128)(2,1)S(1)} %get-tuple-element.48), channel_id=1, source_target_pairs={{0,2},{1,3},{2,0},{3,1},{4,6},{5,7},{6,4},{7,5},{8,10},{9,11},{10,... | collective-permute-start | bytes 786440 | tf_op jit(solution)/shard_map/ppermute | solution.py:806
  91.6 35.6 %copy-start.5 = (bf16[32,48,128]{2,1,0:T(8,128)(2,1)S(1)}, bf16[32,48,128]{2,1,0:T(8,128)(2,1)}, u32[]{:S(2)}) copy-start(bf16[32,48,128]{2,1,0:T(8,128)(2,1)} %get-tuple-element.54.two_ref) | copy-start | bytes 1179652
  91.6 6.6 %collective-permute-start.3 = (bf16[512,128]{1,0:T(8,128)(2,1)S(1)}, bf16[512,128]{1,0:T(8,128)(2,1)S(1)}, u32[]{:S(2)}, u32[]{:S(2)}) collective-permute-start(bf16[512,128]{1,0:T(8,128)(2,1)S(1)} %get-tuple-element.50), channel_id=1, source_target_pairs={{0,4},{1,5},{2,6},{3,7},{4,0},{5,1},{6,2},{7,3},{8,12},{9,13},{10,... | collective-permute-start | bytes 393224 | tf_op jit(solution)/shard_map/ppermute | solution.py:806
  128.1 21.8 %all-to-all-start.4 = ((bf16[32,64,128]{2,1,0:T(8,128)(2,1)}), bf16[32,64,128]{2,1,0:T(8,128)(2,1)S(1)}, u32[]{:S(2)}, u32[]{:S(2)}) async-start(bf16[32,64,128]{2,1,0:T(8,128)(2,1)} %shard_map.224), calls=%async_computation.4 | async-start | bytes 1048576 | tf_op jit(solution)/shard_map/all_to_all | solution.py:636
  162.2 1.9 %collective-permute-start.4 = (bf16[4,512,128]{2,1,0:T(8,128)(2,1)S(1)}, bf16[4,512,128]{2,1,0:T(8,128)(2,1)S(1)}, u32[]{:S(2)}, u32[]{:S(2)}) collective-permute-start(bf16[4,512,128]{2,1,0:T(8,128)(2,1)S(1)} %all_to_all.31.mine_ref), channel_id=1, source_target_pairs={{0,1},{1,0},{2,3},{3,2},{4,5},{5,4},{6,7},{7,6},{8,9},{9,8},{10,11... | collective-permute-start | bytes 1572872 | tf_op jit(solution)/shard_map/ppermute | solution.py:806

commit v6 on v5

--- a/solution.py
+++ b/solution.py
@@ -116,19 +116,21 @@
     lax.fori_loop(0, back_ref.shape[0], body, 0)
 
 
-def sum_kernel(asked_ref, zero_ref, one_ref, zero_acc, one_acc):
-    for ref, acc in ((zero_ref, zero_acc), (one_ref, one_acc)):
+def sum_kernel(asked_ref, zero_ref, one_ref, zero_sum, one_sum, zero_acc, one_acc):
+    for ref, acc, out in ((zero_ref, zero_acc, zero_sum), (one_ref, one_acc, one_sum)):
         acc[...] = jnp.zeros(acc.shape, f32)
         add_terms(asked_ref, ref, acc)
+        out[...] = acc[...].astype(bf16)
 
 
 def last_kernel(asked_ref, zero_ref, one_ref, back_ref, out_ref, acc_ref):
     acc_ref[...] = jnp.zeros_like(acc_ref)
     add_terms(asked_ref, back_ref, acc_ref)
-    zero, one, two = zero_ref[...], one_ref[...], acc_ref[...]
-    out_ref[:, :, 0:128] = zero[:, :BLK].astype(bf16)
-    out_ref[:, :, 128:256] = jnp.concatenate([zero[:, BLK:], one[:, :32]], axis=1).astype(bf16)
-    out_ref[:, :, 256:384] = jnp.concatenate([one[:, 32:], two], axis=1).astype(bf16)
+    out_ref[:, :, 0:128] = zero_ref[:, :BLK]
+    out_ref[:, :32, 128:256] = zero_ref[:, BLK:]
+    out_ref[:, 32:, 128:256] = one_ref[:, :32]
+    out_ref[:, :32, 256:384] = one_ref[:, 32:]
+    out_ref[:, 32:, 256:384] = acc_ref[...].astype(bf16)
 
 
 def mean_e(x):
@@ -447,8 +449,8 @@
             zero_ref[owner, :BLK] = block[:, :128]
             zero_ref[owner, BLK:] = block[:32, 128:256]
             one_ref[owner, :32] = block[32:, 128:256]
-            one_ref[owner, 32:] = block[:16, 256:]
-            two_ref[owner] = block[16:, 256:]
+            one_ref[owner, 32:] = block[:32, 256:]
+            two_ref[owner] = block[32:, 256:]
 
     sends = [
         pltpu.make_async_copy(source, target, sems.at[i])
@@ -518,7 +520,8 @@
 
 def ride_back_kernel(back_ref, two_ref, out_ref):
     cut = two_ref.shape[1]
-    total = jnp.sum(back_ref[:, cut:, :].astype(f32), axis=0).astype(bf16)
+    pieces = out_ref.shape[1] - cut
+    total = jnp.sum(back_ref[:, back_ref.shape[1] - pieces :, :].astype(f32), axis=0).astype(bf16)
     out_ref[:, :cut, :] = two_ref[...]
     out_ref[:, cut:, :] = jnp.broadcast_to(total[None], out_ref[:, cut:, :].shape)
 
@@ -604,8 +607,8 @@
             shape((rows, wide)),
             shape((rows, wide)),
             pltpu.HBM((owners, 96, 128), bf16),
-            pltpu.HBM((owners, 48, 128), bf16),
-            pltpu.HBM((owners, 48, 128), bf16),
+            pltpu.HBM((owners, 64, 128), bf16),
+            pltpu.HBM((owners, 32, 128), bf16),
             pltpu.HBM((GRAD_ROWS // 2, 128), bf16),
             pltpu.HBM((GRAD_ROWS // 2, 128), bf16),
         ),
@@ -623,8 +626,8 @@
             pltpu.VMEM((keys, 4 * W), bf16),
             pltpu.VMEM((GRAD_ROWS, 128), bf16),
             pltpu.VMEM((owners, 96, 128), bf16),
-            pltpu.VMEM((owners, 48, 128), bf16),
-            pltpu.VMEM((owners, 48, 128), bf16),
+            pltpu.VMEM((owners, 64, 128), bf16),
+            pltpu.VMEM((owners, 32, 128), bf16),
             pltpu.SemaphoreType.DMA,
             pltpu.SemaphoreType.DMA((len(prepared),)),
         ],
@@ -753,7 +756,7 @@
     keep, give = small_call(halve_kernel, (shape((half, 128)),) * 2, keep, got, scalars=(high,))
     got = flip(give, 4)
     piece = half // owners
-    riding = shape((owners, one.shape[1] + piece, 128))
+    riding, riding_back = (shape((owners, x.shape[1] + piece, 128)) for x in (one, two))
     ride = pl.pallas_call(
         ride_kernel,
         out_shape=riding,
@@ -762,14 +765,15 @@
         compiler_params=PARAMS,
     )(keep, got, one, back_zero)
     back_one = swap(ride, "rows")
-    back_two = swap(small_call(ride_back_kernel, riding, back_one, two), "rows")
+    back_two = swap(small_call(ride_back_kernel, riding_back, back_one, two), "rows")
     chips = groups // 2
     sums = small_call(
         sum_kernel,
-        tuple(shape((blocks_own, x.shape[1], 128), f32) for x in (zero, one)),
+        tuple(shape((blocks_own, x.shape[1], 128)) for x in (zero, one)),
         back_zero,
         back_one,
         scalars=(asked,),
+        scratch=[pltpu.VMEM((blocks_own, x.shape[1], 128), f32) for x in (zero, one)],
         cost=BUSY,
     )
     copies = pl.pallas_call(

time: 167 us -> 167 us (level)
  blocking collectives: 35 us -> 37.6 us
  waiting for transfers between devices: 63.3 us -> 60.9 us
    all_to_all x1, blocking collectives: 22.8 us -> 25.4 us  [swap(): return lax.all_to_all(x, axis, split_axis=0, concat_axis=0, tiled=True)]
    all_to_all x3, waiting for transfers between devices: 26.4 us -> 24 us  [swap(): return lax.all_to_all(x, axis, split_axis=0, concat_axis=0, tiled=True)]
where the time goes in v6:
time: 167 us; the launch traced here: 166 us
  waiting for transfers between devices  60.9 us (36%)
  blocking collectives  37.6 us (23%)
  starting transfers between devices  35.5 us (21%)
  Pallas kernels  25.6 us (15%)
  local copies, waits for them, and re-layouts  4.4 us (3%)
    all_to_all x1, blocking collectives, swap(): return lax.all_to_all(x, axis, split_axis=0, concat_axis=0, tiled=True)  25.4 us
    all_to_all x3, waiting for transfers between devices, swap(): return lax.all_to_all(x, axis, split_axis=0, concat_axis=0, tiled=True)  24 us
    all_to_all x1, waiting for transfers between devices, on_device(): lax.all_to_all(to_send.reshape(owners // 2, 2 * BLK, wide), ('rows', 'fea...  21.2 us
    all_to_all x3, starting transfers between devices, swap(): return lax.all_to_all(x, axis, split_axis=0, concat_axis=0, tiled=True)  18.7 us
    pallas_call x1, Pallas kernels, main_call(): pl.pallas_call(functools.partial(main_kernel, tile), out_shape=(shape((ro...  13.8 us
    all_to_all x1, blocking collectives, on_device(): lax.all_to_all(copies, 'feat', split_axis=0, concat_axis=0, tiled=True, a...  12.2 us
    ppermute x4, waiting for transfers between devices, flip(): return lax.ppermute(x, 'feat', [(i, i ^ bit) for i in range(count)])  12.2 us
    pallas_call x7, Pallas kernels, small_call(): pl.pallas_call(kernel, out_shape=out_shape, in_specs=[SMEM_SPEC] * len(sc...  6.85 us
  transfers between devices with their start and end apart: 9, of which 9 were waited for; matrix products, arithmetic and copies ran while one was open for 0% of the time, Pallas kernels for 3%

profile of v6, /device:TPU:32, one launch (start us, length us, event | category | flops | bytes accessed | tf_op | source)
XLA Modules:
  0.0 165.8 jit_solution(17575164766060072493)
XLA Ops:
  0.6 2.1 %shard_map.214 = (bf16[8,64,384]{2,1,0:T(8,128)(2,1)}, s32[32,1,16]{2,1,0:T(1,128)}) custom-call(bf16[512,384]{1,0:T(8,128)(2,1)} %train_hbm.1, s32[2,512]{1,0:T(2,128)} %present_hbm.1, s32[1,16]{1,0:T(1,128)} %retrieved_hbm.1), custom_call_target="tpu_custom_call" | custom-call | tf_op jit(solution)/shard_map/pallas_call | solution.py:690
  2.7 5.9 %collective-permute-start = (bf16[8,64,384]{2,1,0:T(8,128)(2,1)}, bf16[8,64,384]{2,1,0:T(8,128)(2,1)S(1)}, u32[]{:S(2)}, u32[]{:S(2)}) collective-permute-start(bf16[8,64,384]{2,1,0:T(8,128)(2,1)} %get-tuple-element.36.own_ref), channel_id=1, source_target_pairs={{0,56},{1,25},{2,58},{3,27},{4,60},{5,29},{6,62},{7,31},{8,48},{9,... | collective-permute-start | bytes 1179656 | tf_op jit(solution)/shard_map/ppermute | solution.py:701
  8.7 6.5 %all-to-all-start = ((s32[32,1,16]{2,1,0:T(1,128)}), s32[32,1,16]{2,1,0:T(1,128)S(1)}, u32[]{:S(2)}, u32[]{:S(2)}) async-start(s32[32,1,16]{2,1,0:T(1,128)} %get-tuple-element.35), calls=%async_computation | async-start | bytes 32768 | tf_op jit(solution)/shard_map/all_to_all | solution.py:639
  15.3 0.1 pad_add_fusion.served_ref
  15.4 3.6 %collective-permute-done.in_ref = bf16[8,64,384]{2,1,0:T(8,128)(2,1)S(1)} collective-permute-done((bf16[8,64,384]{2,1,0:T(8,128)(2,1)}, bf16[8,64,384]{2,1,0:T(8,128)(2,1)S(1)}, u32[]{:S(2)}, u32[]{:S(2)}) %collective-permute-start) | collective-permute-done | bytes 393248 | tf_op jit(solution)/shard_map/ppermute | solution.py:701
  18.9 4.8 %all-to-all-done.table_ref = s32[32,1,16]{2,1,0:T(1,128)S(1)} async-done(((s32[32,1,16]{2,1,0:T(1,128)}), s32[32,1,16]{2,1,0:T(1,128)S(1)}, u32[]{:S(2)}, u32[]{:S(2)}) %all-to-all-start) | async-done | bytes 2080 | tf_op jit(solution)/shard_map/all_to_all | solution.py:639
  23.8 0.7 shard_map.216.asked_ref
  24.5 2.0 %shard_map.217 = bf16[16,2,64,384]{3,2,1,0:T(8,128)(2,1)} custom-call(s32[32,2]{1,0:T(8,128)S(1)} %shard_map.216.asked_ref, s32[1]{0:T(128)} %bitcast.4.base_ref, bf16[8,64,384]{2,1,0:T(8,128)(2,1)S(1)} %copy-done.6, bf16[8,64,384]{2,1,0:T(8,128)(2,1)S(1)} %shard_map.215.mirrored_ref), custom_call_target="tpu_custom_call" | custom-call | tf_op jit(solution)/shard_map/pallas_call | solution.py:721
  26.5 0.0 copy-start.21
  26.5 0.0 copy-start.7
  26.5 0.0 copy-start.8
  26.6 0.0 copy-start.11
  26.6 0.0 copy-start.12
  26.6 0.0 copy-start.15
  26.6 0.0 copy-start.17
  26.7 0.0 copy-start.20
  26.7 5.7 %all-to-all-start.1 = ((bf16[16,128,384]{2,1,0:T(8,128)(2,1)}), bf16[16,128,384]{2,1,0:T(8,128)(2,1)}, u32[]{:S(2)}, u32[]{:S(2)}) async-start(bf16[16,128,384]{2,1,0:T(8,128)(2,1)} %bitcast.5), calls=%async_computation.1 | async-start | bytes 3145728 | tf_op jit(solution)/shard_map/all_to_all | solution.py:729
  32.4 0.6 fusion.1
  33.0 0.1 slice_reduce_fusion.asked_ref
  33.2 1.1 shard_map.218
  34.3 1.0 copy-done
  35.3 0.9 copy-done.1
  36.2 0.9 copy-done.2
  37.1 0.8 copy-done.4
  37.9 0.6 copy-done.16
  38.5 21.2 %all-to-all-done.1 = bf16[16,128,384]{2,1,0:T(8,128)(2,1)} async-done(((bf16[16,128,384]{2,1,0:T(8,128)(2,1)}), bf16[16,128,384]{2,1,0:T(8,128)(2,1)}, u32[]{:S(2)}, u32[]{:S(2)}) %all-to-all-start.1) | async-done | bytes 1572896 | tf_op jit(solution)/shard_map/all_to_all | solution.py:729
  59.7 13.8 %shard_map.219 = (bf16[128,384]{1,0:T(8,128)(2,1)}, bf16[128,384]{1,0:T(8,128)(2,1)}, bf16[32,96,128]{2,1,0:T(8,128)(2,1)}, bf16[32,64,128]{2,1,0:T(8,128)(2,1)}...) custom-call(s32[16]{0:T(128)} %get-tuple-element.61.source_ref, ...), custom_call_target="tpu_custom_call" | custom-call | tf_op jit(solution)/shard_map/pallas_call | solution.py:604
  73.5 7.1 %all-to-all-start.2 = ((bf16[32,96,128]{2,1,0:T(8,128)(2,1)}), bf16[32,96,128]{2,1,0:T(8,128)(2,1)S(1)}, u32[]{:S(2)}, u32[]{:S(2)}) async-start(bf16[32,96,128]{2,1,0:T(8,128)(2,1)} %get-tuple-element.44), calls=%async_computation.2 | async-start | bytes 1572864 | tf_op jit(solution)/shard_map/all_to_all | solution.py:639
  80.7 0.5 collective-permute-start.1
  81.2 1.7 %collective-permute-done.1.got_ref = bf16[2048,128]{1,0:T(8,128)(2,1)S(1)} collective-permute-done((bf16[2048,128]{1,0:T(8,128)(2,1)S(1)}, bf16[2048,128]{1,0:T(8,128)(2,1)S(1)}, u32[]{:S(2)}, u32[]{:S(2)}) %collective-permute-start.1) | collective-permute-done | bytes 524320 | tf_op jit(solution)/shard_map/ppermute | solution.py:810
  82.9 0.1 shard_map.220
  83.0 1.6 collective-permute-start.2
  84.6 6.9 %collective-permute-done.2.got_ref = bf16[1024,128]{1,0:T(8,128)(2,1)S(1)} collective-permute-done((bf16[1024,128]{1,0:T(8,128)(2,1)S(1)}, bf16[1024,128]{1,0:T(8,128)(2,1)S(1)}, u32[]{:S(2)}, u32[]{:S(2)}) %collective-permute-start.2) | collective-permute-done | bytes 262176 | tf_op jit(solution)/shard_map/ppermute | solution.py:810
  91.5 0.1 shard_map.221
  91.6 3.1 %collective-permute-start.3 = (bf16[512,128]{1,0:T(8,128)(2,1)S(1)}, bf16[512,128]{1,0:T(8,128)(2,1)S(1)}, u32[]{:S(2)}, u32[]{:S(2)}) collective-permute-start(bf16[512,128]{1,0:T(8,128)(2,1)S(1)} %get-tuple-element.50), channel_id=1, source_target_pairs={{0,4},{1,5},{2,6},{3,7},{4,0},{5,1},{6,2},{7,3},{8,12},{9,13},{10,... | collective-permute-start | bytes 393224 | tf_op jit(solution)/shard_map/ppermute | solution.py:810
  94.7 3.4 %collective-permute-done.3.got_ref = bf16[512,128]{1,0:T(8,128)(2,1)S(1)} collective-permute-done((bf16[512,128]{1,0:T(8,128)(2,1)S(1)}, bf16[512,128]{1,0:T(8,128)(2,1)S(1)}, u32[]{:S(2)}, u32[]{:S(2)}) %collective-permute-start.3) | collective-permute-done | bytes 131104 | tf_op jit(solution)/shard_map/ppermute | solution.py:810
  98.1 6.3 %all-to-all-done.2.earlier_ref.zero_ref = bf16[32,96,128]{2,1,0:T(8,128)(2,1)S(1)} async-done(((bf16[32,96,128]{2,1,0:T(8,128)(2,1)}), bf16[32,96,128]{2,1,0:T(8,128)(2,1)S(1)}, u32[]{:S(2)}, u32[]{:S(2)}) %all-to-all-start.2) | async-done | bytes 786464 | tf_op jit(solution)/shard_map/all_to_all | solution.py:639
  104.4 0.1 shard_map.222
  104.5 25.4 %all_to_all.30.one_ref.back_ref = bf16[32,80,128]{2,1,0:T(8,128)(2,1)S(1)} all-to-all(bf16[32,80,128]{2,1,0:T(8,128)(2,1)S(1)} %shard_map.222), channel_id=1, replica_groups=mesh['rows'=32,'feat'=8] {'rows'}, dimensions={0} | all-to-all | bytes 1310720 | tf_op jit(solution)/shard_map/all_to_all | solution.py:639
  129.9 0.8 shard_map.224
  130.7 5.0 %all-to-all-start.4 = ((bf16[32,48,128]{2,1,0:T(8,128)(2,1)}), bf16[32,48,128]{2,1,0:T(8,128)(2,1)S(1)}, u32[]{:S(2)}, u32[]{:S(2)}) async-start(bf16[32,48,128]{2,1,0:T(8,128)(2,1)} %shard_map.224), calls=%async_computation.4 | async-start | bytes 786432 | tf_op jit(solution)/shard_map/all_to_all | solution.py:639
  135.7 1.6 shard_map.223
  137.3 12.9 %all-to-all-done.4.back_ref = bf16[32,48,128]{2,1,0:T(8,128)(2,1)S(1)} async-done(((bf16[32,48,128]{2,1,0:T(8,128)(2,1)}), bf16[32,48,128]{2,1,0:T(8,128)(2,1)S(1)}, u32[]{:S(2)}, u32[]{:S(2)}) %all-to-all-start.4) | async-done | bytes 393248 | tf_op jit(solution)/shard_map/all_to_all | solution.py:639
  150.2 0.1 shard_map.226
  150.3 12.2 %all_to_all.31.mine_ref = bf16[4,512,128]{2,1,0:T(8,128)(2,1)S(1)} all-to-all(bf16[4,512,128]{2,1,0:T(8,128)(2,1)S(1)} %shard_map.226), channel_id=1, replica_groups={{0,2,4,6},{1,3,5,7},{8,10,12,14},{9,11,13,15},{16,18,20,22},{17,19,21,2..., dimensions={0} | all-to-all | bytes 1048576 | tf_op jit(solution)/shard_map/all_to_all | solution.py:786
  162.5 1.8 %shard_map.225 = bf16[8,64,384]{2,1,0:T(8,128)(2,1)} custom-call(s32[32]{0:T(128)S(1)} %slice_reduce_fusion.asked_ref, bf16[8,96,128]{2,1,0:T(8,128)(2,1)S(1)} %get-tuple-element.52.zero_ref, bf16[8,64,128]{2,1,0:T(8,128)(2,1)S(1)} %get-tuple-element.53.one_ref, bf16[32,48,128]{2,1,0:T(8,128)(2,1)S(1)} %all-to-all-done.4.back_ref), custom_call_target="tpu_custom_call" | custom-call | flops 1000000000 | bytes 4194304 | tf_op jit(solution)/shard_map/pallas_call | solution.py:571
  164.3 0.1 collective-permute-done.4.got_ref
  164.4 1.4 shard_map.227
  (35 shorter events, 0.1 us)
Async XLA Ops:
  2.7 16.2 %collective-permute-start = (bf16[8,64,384]{2,1,0:T(8,128)(2,1)}, bf16[8,64,384]{2,1,0:T(8,128)(2,1)S(1)}, u32[]{:S(2)}, u32[]{:S(2)}) collective-permute-start(bf16[8,64,384]{2,1,0:T(8,128)(2,1)} %get-tuple-element.36.own_ref), channel_id=1, source_target_pairs={{0,56},{1,25},{2,58},{3,27},{4,60},{5,29},{6,62},{7,31},{8,48},{9,... | collective-permute-start | bytes 1179656 | tf_op jit(solution)/shard_map/ppermute | solution.py:701
  8.7 15.1 %all-to-all-start = ((s32[32,1,16]{2,1,0:T(1,128)}), s32[32,1,16]{2,1,0:T(1,128)S(1)}, u32[]{:S(2)}, u32[]{:S(2)}) async-start(s32[32,1,16]{2,1,0:T(1,128)} %get-tuple-element.35), calls=%async_computation | async-start | bytes 32768 | tf_op jit(solution)/shard_map/all_to_all | solution.py:639
  15.4 9.1 %copy-start.6 = (bf16[8,64,384]{2,1,0:T(8,128)(2,1)S(1)}, bf16[8,64,384]{2,1,0:T(8,128)(2,1)}, u32[]{:S(2)}) copy-start(bf16[8,64,384]{2,1,0:T(8,128)(2,1)} %get-tuple-element.36.own_ref) | copy-start | bytes 1179652
  26.5 5.9 %copy-start.21 = (s32[1,16]{1,0:T(1,128)S(1)}, s32[1,16]{1,0:T(1,128)}, u32[]{:S(2)}) copy-start(s32[1,16]{1,0:T(1,128)} %retrieved_hbm.1) | copy-start | bytes 196
  26.5 6.5 %copy-start.7 = (bf16[192,768]{1,0:T(8,128)(2,1)S(1)}, bf16[192,768]{1,0:T(8,128)(2,1)}, u32[]{:S(2)}) copy-start(bf16[192,768]{1,0:T(8,128)(2,1)} %w_up_ref.1) | copy-start | bytes 884740
  26.5 6.5 %copy-start.8 = (bf16[768,192]{0,1:T(8,128)(2,1)S(1)}, bf16[768,192]{0,1:T(8,128)(2,1)}, u32[]{:S(2)}) copy-start(bf16[768,192]{0,1:T(8,128)(2,1)} %param.27) | copy-start | bytes 884740
  26.6 6.5 %copy-start.10 = (bf16[128,384]{1,0:T(8,128)(2,1)S(1)}, bf16[128,384]{1,0:T(8,128)(2,1)}, u32[]{:S(2)}) copy-start(bf16[128,384]{1,0:T(8,128)(2,1)} %test_ref.1) | copy-start | bytes 294916
  26.6 6.5 %copy-start.11 = (bf16[128,384]{1,0:T(8,128)(2,1)S(1)}, bf16[128,384]{1,0:T(8,128)(2,1)}, u32[]{:S(2)}) copy-start(bf16[128,384]{1,0:T(8,128)(2,1)} %cot_ref.1) | copy-start | bytes 294916
  26.6 6.5 %copy-start.12 = (bf16[192,192]{1,0:T(8,128)(2,1)S(1)}, bf16[192,192]{1,0:T(8,128)(2,1)}, u32[]{:S(2)}) copy-start(bf16[192,192]{1,0:T(8,128)(2,1)} %w_query_ref.1) | copy-start | bytes 221188
  26.6 6.5 %copy-start.13 = (bf16[192,192]{1,0:T(8,128)(2,1)S(1)}, bf16[192,192]{1,0:T(8,128)(2,1)}, u32[]{:S(2)}) copy-start(bf16[192,192]{1,0:T(8,128)(2,1)} %w_key_ref.1) | copy-start | bytes 221188
  26.6 6.5 %copy-start.14 = (bf16[192,192]{1,0:T(8,128)(2,1)S(1)}, bf16[192,192]{1,0:T(8,128)(2,1)}, u32[]{:S(2)}) copy-start(bf16[192,192]{1,0:T(8,128)(2,1)} %w_value_ref.1) | copy-start | bytes 221188
  26.6 6.5 %copy-start.15 = (bf16[192,192]{1,0:T(8,128)(2,1)S(1)}, bf16[192,192]{1,0:T(8,128)(2,1)}, u32[]{:S(2)}) copy-start(bf16[192,192]{1,0:T(8,128)(2,1)} %w_out_ref.1) | copy-start | bytes 221188
  26.6 6.5 %copy-start.17 = (f32[192]{0:T(256)S(1)}, f32[192]{0:T(256)}, u32[]{:S(2)}) copy-start(f32[192]{0:T(256)} %param.20) | copy-start | bytes 2308
  26.6 6.5 %copy-start.18 = (f32[192]{0:T(256)S(1)}, f32[192]{0:T(256)}, u32[]{:S(2)}) copy-start(f32[192]{0:T(256)} %param.22) | copy-start | bytes 2308
  26.7 6.5 %copy-start.19 = (f32[192]{0:T(256)S(1)}, f32[192]{0:T(256)}, u32[]{:S(2)}) copy-start(f32[192]{0:T(256)} %param.25) | copy-start | bytes 2308
  26.7 6.5 %copy-start.20 = (f32[192]{0:T(256)S(1)}, f32[192]{0:T(256)}, u32[]{:S(2)}) copy-start(f32[192]{0:T(256)} %param.28) | copy-start | bytes 2308
  26.7 33.0 %all-to-all-start.1 = ((bf16[16,128,384]{2,1,0:T(8,128)(2,1)}), bf16[16,128,384]{2,1,0:T(8,128)(2,1)}, u32[]{:S(2)}, u32[]{:S(2)}) async-start(bf16[16,128,384]{2,1,0:T(8,128)(2,1)} %bitcast.5), calls=%async_computation.1 | async-start | bytes 3145728 | tf_op jit(solution)/shard_map/all_to_all | solution.py:729
  34.3 1.0 copy-start
  35.3 0.9 copy-start.1
  36.2 0.9 copy-start.2
  37.1 0.8 copy-start.4
  37.9 0.6 copy-start.16
  73.5 7.2 %copy-start.22 = (bf16[2048,128]{1,0:T(8,128)(2,1)S(1)}, bf16[2048,128]{1,0:T(8,128)(2,1)}, u32[]{:S(2)}) copy-start(bf16[2048,128]{1,0:T(8,128)(2,1)} %get-tuple-element.46) | copy-start | bytes 1572868
  73.5 9.4 %copy-start.5 = (bf16[2048,128]{1,0:T(8,128)(2,1)S(1)}, bf16[2048,128]{1,0:T(8,128)(2,1)}, u32[]{:S(2)}) copy-start(bf16[2048,128]{1,0:T(8,128)(2,1)} %get-tuple-element.45.keep_ref) | copy-start | bytes 1572868
  73.5 30.9 %copy-start.3 = (bf16[32,64,128]{2,1,0:T(8,128)(2,1)S(1)}, bf16[32,64,128]{2,1,0:T(8,128)(2,1)}, u32[]{:S(2)}) copy-start(bf16[32,64,128]{2,1,0:T(8,128)(2,1)} %get-tuple-element.51.one_ref) | copy-start | bytes 1572868
  73.5 30.9 %all-to-all-start.2 = ((bf16[32,96,128]{2,1,0:T(8,128)(2,1)}), bf16[32,96,128]{2,1,0:T(8,128)(2,1)S(1)}, u32[]{:S(2)}, u32[]{:S(2)}) async-start(bf16[32,96,128]{2,1,0:T(8,128)(2,1)} %get-tuple-element.44), calls=%async_computation.2 | async-start | bytes 1572864 | tf_op jit(solution)/shard_map/all_to_all | solution.py:639
  80.7 2.2 %collective-permute-start.1 = (bf16[2048,128]{1,0:T(8,128)(2,1)S(1)}, bf16[2048,128]{1,0:T(8,128)(2,1)S(1)}, u32[]{:S(2)}, u32[]{:S(2)}) collective-permute-start(bf16[2048,128]{1,0:T(8,128)(2,1)S(1)} %copy-done.22), channel_id=1, source_target_pairs={{0,1},{1,0},{2,3},{3,2},{4,5},{5,4},{6,7},{7,6},{8,9},{9,8},{10,11... | collective-permute-start | bytes 1572872 | tf_op jit(solution)/shard_map/ppermute | solution.py:810
  83.0 8.5 %collective-permute-start.2 = (bf16[1024,128]{1,0:T(8,128)(2,1)S(1)}, bf16[1024,128]{1,0:T(8,128)(2,1)S(1)}, u32[]{:S(2)}, u32[]{:S(2)}) collective-permute-start(bf16[1024,128]{1,0:T(8,128)(2,1)S(1)} %get-tuple-element.48), channel_id=1, source_target_pairs={{0,2},{1,3},{2,0},{3,1},{4,6},{5,7},{6,4},{7,5},{8,10},{9,11},{10,... | collective-permute-start | bytes 786440 | tf_op jit(solution)/shard_map/ppermute | solution.py:810
  91.6 6.6 %collective-permute-start.3 = (bf16[512,128]{1,0:T(8,128)(2,1)S(1)}, bf16[512,128]{1,0:T(8,128)(2,1)S(1)}, u32[]{:S(2)}, u32[]{:S(2)}) collective-permute-start(bf16[512,128]{1,0:T(8,128)(2,1)S(1)} %get-tuple-element.50), channel_id=1, source_target_pairs={{0,4},{1,5},{2,6},{3,7},{4,0},{5,1},{6,2},{7,3},{8,12},{9,13},{10,... | collective-permute-start | bytes 393224 | tf_op jit(solution)/shard_map/ppermute | solution.py:810
  104.4 25.5 %copy-start.9 = (bf16[32,32,128]{2,1,0:T(8,128)(2,1)S(1)}, bf16[32,32,128]{2,1,0:T(8,128)(2,1)}, u32[]{:S(2)}) copy-start(bf16[32,32,128]{2,1,0:T(8,128)(2,1)} %get-tuple-element.54.two_ref) | copy-start | bytes 786436
  130.7 19.5 %all-to-all-start.4 = ((bf16[32,48,128]{2,1,0:T(8,128)(2,1)}), bf16[32,48,128]{2,1,0:T(8,128)(2,1)S(1)}, u32[]{:S(2)}, u32[]{:S(2)}) async-start(bf16[32,48,128]{2,1,0:T(8,128)(2,1)} %shard_map.224), calls=%async_computation.4 | async-start | bytes 786432 | tf_op jit(solution)/shard_map/all_to_all | solution.py:639
  162.5 1.9 %collective-permute-start.4 = (bf16[4,512,128]{2,1,0:T(8,128)(2,1)S(1)}, bf16[4,512,128]{2,1,0:T(8,128)(2,1)S(1)}, u32[]{:S(2)}, u32[]{:S(2)}) collective-permute-start(bf16[4,512,128]{2,1,0:T(8,128)(2,1)S(1)} %all_to_all.31.mine_ref), channel_id=1, source_target_pairs={{0,1},{1,0},{2,3},{3,2},{4,5},{5,4},{6,7},{7,6},{8,9},{9,8},{10,11... | collective-permute-start | bytes 1572872 | tf_op jit(solution)/shard_map/ppermute | solution.py:810
